TPU v7x, 32 devices: a whole 2x2x4 slice. The times are simulated.
32 devices in a mesh: dp: 8 (over z, y), mp: 2 (over core), side: 2 (over x).
Axes of the slice: x: 2, y: 2, z: 4, core: 2. Of those that a mesh axis runs over, the one named last changes fastest.
Arguments:
- tokens: bfloat16 [2048, 3072], P('dp', 'mp'), may hold values from -6 to 6
- up_weight: bfloat16 [2, 3072, 6144], P('side', 'dp', 'mp'), may hold values from -0.109375 to 0.109375
- down_weight: bfloat16 [2, 6144, 3072], P('side', 'mp', 'dp'), may hold values from -0.078125 to 0.078125
- mod_table: float32 [2, 50, 3, 3072], P('side'), may hold values from -3 to 3
- timesteps: int32 [8], P('dp'), may hold values from 0 to 49
- valid_counts: int32 [8], replicated, may hold values from 64 to 256, as said below
Outputs:
- block_out: bfloat16 [2, 2048, 3072], P('side', 'dp', 'mp')
- up_grads: float32 [3072, 6144], P(('dp', 'side'), 'mp')
- down_grads: float32 [6144, 3072], P('mp', ('dp', 'side'))
Inputs may be any that keep to these rules, and one draw needn't show every extreme that they name: `valid_counts`: every image has at least 64 valid tokens, and in every draw some image has all 256 valid.
All inputs are finite; a program needn't handle non-finite values.
Results may differ from a plain program's by a relative error of at most 0.018.
Values may be sent and summed in bfloat16 or wider, within the bound.
No kernel may reach another device: no remote copies, remote signals or barrier semaphores. Data moves between devices by JAX's collectives and lax.ppermute only.
A program may use at most 128 MiB of HBM per device.

v0:
```python
import jax
import jax.numpy as jnp
from jax import lax
from jax.sharding import PartitionSpec as P


def passed_along(x, axis, by):
    peers = lax.axis_size(axis)
    pairs = [(i, i + by) for i in range(peers) if 0 <= i + by < peers]
    return lax.ppermute(x, axis, pairs)


def gelu_tanh(values):
    return jax.nn.gelu(values, approximate=True)


def shards(tokens, up_weight, down_weight, mod_table, timesteps, valid_counts):
    gathered = lax.all_gather(tokens, "mp", axis=1, tiled=True)
    width = gathered.shape[1]
    shard_width = tokens.shape[1]
    mp_offset = lax.axis_index("mp") * shard_width
    is_student = lax.axis_index("side") == 1
    wide = gathered.astype(jnp.float32)
    average = jnp.mean(wide, axis=-1, keepdims=True)
    centred = wide - average
    variance = jnp.mean(centred * centred, axis=-1, keepdims=True)
    scaled = centred * lax.rsqrt(variance + 1e-06)
    plan = mod_table.shape[1]
    one_hot = (jnp.arange(plan, dtype=jnp.int32)[None, :] == timesteps[0]).astype(jnp.float32)
    modulation = jnp.dot(
        one_hot,
        mod_table[0].reshape(plan, 3 * width),
        precision=lax.Precision.HIGHEST,
        preferred_element_type=jnp.float32,
    ).reshape(3, width)
    normed = (scaled * (1.0 + modulation[1]) + modulation[0]).astype(jnp.bfloat16)
    gate_row = modulation[2]
    hidden_pre = jnp.dot(
        normed,
        lax.all_gather(up_weight[0], "dp", axis=0, tiled=True),
        preferred_element_type=jnp.float32,
    )
    hidden_act = gelu_tanh(hidden_pre).astype(jnp.bfloat16)
    down_full = lax.all_gather(down_weight[0], "dp", axis=1, tiled=True)
    partial_value = jnp.dot(hidden_act, down_full, preferred_element_type=jnp.float32)
    positions = jnp.arange(normed.shape[0], dtype=jnp.int32)
    own_count = lax.dynamic_index_in_dim(valid_counts, lax.axis_index("dp"), 0, keepdims=False)
    valid_col = (positions < own_count).astype(jnp.float32)[:, None]
    valid_total = jnp.sum(valid_counts).astype(jnp.float32)
    mixed_local = lax.psum_scatter(
        partial_value.astype(jnp.bfloat16), "mp", scatter_dimension=1, tiled=True
    ).astype(jnp.float32)
    gate_local = lax.dynamic_slice_in_dim(gate_row, mp_offset, shard_width, 0)
    out_local = (tokens.astype(jnp.float32) + gate_local * mixed_local).astype(jnp.bfloat16)
    other_local = passed_along(out_local, "side", 1)
    differ = out_local.astype(jnp.float32) - other_local.astype(jnp.float32)
    grad_local = (gate_local * differ * valid_col / jnp.sqrt(valid_total)).astype(jnp.bfloat16)
    grad_out = lax.all_gather(grad_local, "mp", axis=1, tiled=True)

    def backprop():
        grad_act = lax.dot_general(
            grad_out, down_full, (((1,), (1,)), ((), ())), preferred_element_type=jnp.float32
        )
        unused, pullback = jax.vjp(gelu_tanh, hidden_pre)
        return pullback(grad_act)[0].astype(jnp.bfloat16)

    def no_backprop():
        return jnp.zeros(hidden_pre.shape, jnp.bfloat16)

    grad_pre = lax.cond(is_student, backprop, no_backprop)
    ff_width = hidden_act.shape[1]

    def product():
        return lax.dot_general(
            normed, grad_pre, (((0,), (0,)), ((), ())), preferred_element_type=jnp.float32
        )

    def nothing():
        return jnp.zeros(
            (width // lax.axis_size(("dp", "side")) * lax.axis_size(("dp", "side")), ff_width),
            jnp.float32,
        )

    up_share = lax.psum_scatter(
        lax.cond(is_student, product, nothing).astype(jnp.bfloat16),
        ("dp", "side"),
        scatter_dimension=0,
        tiled=True,
    ).astype(jnp.float32)

    def down_product():
        return lax.dot_general(
            hidden_act, grad_out, (((0,), (0,)), ((), ())), preferred_element_type=jnp.float32
        )

    def down_nothing():
        return jnp.zeros((ff_width, width), jnp.float32)

    down_term = lax.cond(is_student, down_product, down_nothing)
    down_share = lax.psum_scatter(
        down_term.astype(jnp.bfloat16), ("dp", "side"), scatter_dimension=1, tiled=True
    ).astype(jnp.float32)
    return (out_local[None], up_share, down_share)


def solution(mesh):
    placed = (
        P("dp", "mp"),
        P("side", "dp", "mp"),
        P("side", "mp", "dp"),
        P("side", None, None, None),
        P("dp"),
        P(),
    )
    return jax.shard_map(
        shards,
        mesh=mesh,
        in_specs=placed,
        out_specs=(P("side", "dp", "mp"), P(("dp", "side"), "mp"), P("mp", ("dp", "side"))),
        check_vma=False,
    )
```

profile of v0, /device:TPU:10, one launch (start us, length us, event | category | flops | bytes accessed | tf_op | source)
XLA Modules:
  0.0 1411.7 jit_solution(10471035607426063032)
XLA Ops:
  9.4 6.5 reduce
  19.1 1.7 all-gather.7.cloned.1.call-done
  20.8 1.8 convert_reduce_fusion
  22.6 2.0 fusion.11
  25.4 360.3 %all-gather.11.cloned.1.call-done = bf16[1,3072,3072]{2,1,0:T(8,128)(2,1)} async-done(((bf16[1,384,3072]{2,1,0:T(8,128)(2,1)}), bf16[1,3072,3072]{2,1,0:T(8,128)(2,1)}) %all-gather.11.cloned.1.call-update) | async-done | bytes 18874384 | tf_op jit(solution)/shard_map/all_gather | solution.py:40
  385.7 13.9 fusion.22
  399.6 350.1 %all-gather.13.cloned.1.call-done = bf16[1,3072,3072]{2,1,0:T(8,128)(2,1)} async-done(((bf16[1,3072,384]{2,1,0:T(8,128)(2,1)}), bf16[1,3072,3072]{2,1,0:T(8,128)(2,1)}) %all-gather.13.cloned.1.call-update) | async-done | bytes 18874384 | tf_op jit(solution)/shard_map/all_gather | solution.py:44
  749.7 10.4 convolution_convert_fusion
  760.2 9.4 reduce-scatter.4.cloned.1.call-done
  769.6 1.4 add_convert_fusion
  774.9 17.7 %collective-permute-done = bf16[256,1536]{1,0:T(8,128)(2,1)S(1)} collective-permute-done((bf16[256,1536]{1,0:T(8,128)(2,1)S(1)}, bf16[256,1536]{1,0:T(8,128)(2,1)S(1)}, u32[]{:S(2)}, u32[]{:S(2)}) %collective-permute-start) | collective-permute-done | bytes 786464 | tf_op jit(solution)/shard_map/ppermute | solution.py:10
  793.9 11.1 all-gather.9.cloned.1.call-done
  805.0 11.3 conditional.3
  805.0 11.3 fusion.6
  816.3 9.2 conditional.4
  816.4 9.1 fusion.30
  825.6 1.3 copy-done.3
  827.4 9.4 conditional.5
  827.4 9.4 fusion.31
  836.8 24.7 %copy.9 = bf16[3072,3072]{0,1:T(8,128)(2,1)} copy(bf16[3072,3072]{1,0:T(8,128)(2,1)} %get-tuple-element.40) | data formatting | bytes 37748736 | tf_op jit(solution)/shard_map/cond | solution.py:99
  861.6 249.3 %reduce-scatter.6.cloned.1.call-done = bf16[192,3072]{1,0:T(8,128)(2,1)} async-done(((bf16[3072,3072]{1,0:T(8,128)(2,1)}), bf16[192,3072]{1,0:T(8,128)(2,1)}) %reduce-scatter.6.cloned.1.call-update) | async-done | bytes 1179664 | tf_op jit(solution)/shard_map/reduce_scatter | solution.py:84
  1110.9 2.9 convert_element_type.75
  1113.8 288.2 %reduce-scatter.8.cloned.1.call-done = bf16[3072,192]{0,1:T(8,128)(2,1)} async-done(((bf16[3072,3072]{0,1:T(8,128)(2,1)}), bf16[3072,192]{0,1:T(8,128)(2,1)}) %reduce-scatter.8.cloned.1.call-update) | async-done | bytes 1179664 | tf_op jit(solution)/shard_map/reduce_scatter | solution.py:100
  1402.0 2.9 convert_element_type.77
  (38 shorter events, 10.6 us)
Async XLA Ops:
  7.2 13.6 all-gather.7.cloned.1.call-start
  7.9 377.8 %all-gather.11.cloned.1.call-start = ((), (), s32[]{:S(2)}) async-start(), calls=%async_computation.8 | async-start | bytes 21233664 | tf_op jit(solution)/shard_map/all_gather | solution.py:40
  8.6 741.1 %all-gather.13.cloned.1.call-start = ((), (), s32[]{:S(2)}) async-start(), calls=%async_computation.9 | async-start | bytes 21233664 | tf_op jit(solution)/shard_map/all_gather | solution.py:44
  9.4 760.2 %reduce-scatter.4.cloned.1.call-start = ((), (), s32[]{:S(2)}) async-start(), calls=%async_computation.4 | async-start | bytes 2359296 | tf_op jit(solution)/shard_map/reduce_scatter | solution.py:50
  20.8 3.8 copy-start
  749.7 19.9 %copy-start.1 = (bf16[256,1536]{1,0:T(8,128)(2,1)S(1)}, bf16[256,1536]{1,0:T(8,128)(2,1)}, u32[]{:S(2)}) copy-start(bf16[256,1536]{1,0:T(8,128)(2,1)} %param.12) | copy-start | bytes 2359300
  760.1 12.2 copy-start.5
  760.1 44.9 %all-gather.9.cloned.1.call-start = ((), (), s32[]{:S(2)}) async-start(), calls=%async_computation.5 | async-start | bytes 2359296 | tf_op jit(solution)/shard_map/all_gather | solution.py:58
  771.0 34.0 %copy-start.2 = (bf16[256,1536]{1,0:T(8,128)(2,1)}, bf16[256,1536]{1,0:T(8,128)(2,1)S(1)}, u32[]{:S(2)}) copy-start(bf16[256,1536]{1,0:T(8,128)(2,1)S(1)} %add_convert_fusion) | copy-start | bytes 2359300
  771.0 21.6 %collective-permute-start = (bf16[256,1536]{1,0:T(8,128)(2,1)S(1)}, bf16[256,1536]{1,0:T(8,128)(2,1)S(1)}, u32[]{:S(2)}, u32[]{:S(2)}) collective-permute-start(bf16[256,1536]{1,0:T(8,128)(2,1)S(1)} %add_convert_fusion), channel_id=1, source_target_pairs={{0,1},{2,3},{4,5},{6,7},{8,9},{10,11},{12,13},{14,15},{16,17},{18,... | collective-permute-start | bytes 2359304 | tf_op jit(solution)/shard_map/ppermute | solution.py:10
  793.8 317.0 %reduce-scatter.6.cloned.1.call-start = ((), (), s32[]{:S(2)}) async-start(), calls=%async_computation.6 | async-start | bytes 20054016 | tf_op jit(solution)/shard_map/reduce_scatter | solution.py:84
  825.5 1.4 copy-start.3
  825.5 1.9 copy-start.4
  825.5 576.4 %reduce-scatter.8.cloned.1.call-start = ((), (), s32[]{:S(2)}) async-start(), calls=%async_computation.7 | async-start | bytes 20054016 | tf_op jit(solution)/shard_map/reduce_scatter | solution.py:100
Sparse Core Ops, SparseCore 0:
  9.5 11.1 all-gather.6
  22.3 363.3 all-gather.10
  387.2 362.4 all-gather.12
  760.2 9.3 reduce-scatter.3
  794.0 10.9 all-gather.8
  825.6 285.1 reduce-scatter.5
  1117.6 284.2 reduce-scatter.7
where the time goes:
time: 1420 us; the launch traced here: 1410 us
  waiting for transfers between devices  1290 us (91%)
  matrix products  55 us (4%)
  local copies, waits for them, and re-layouts  28.9 us (2%)
  other arithmetic  20.8 us (1%)
  between operations  15.6 us (1%)
    all_gather x1, waiting for transfers between devices, shards(): lax.all_gather(up_weight[0], 'dp', axis=0, tiled=True)  360 us
    all_gather x1, waiting for transfers between devices, shards(): down_full = lax.all_gather(down_weight[0], 'dp', axis=1, tiled=True)  350 us
    reduce_scatter x1, waiting for transfers between devices, shards(): lax.psum_scatter(down_term.astype(jnp.bfloat16), ('dp', 'side'), scatter_...  288 us
    reduce_scatter x1, waiting for transfers between devices, shards(): lax.psum_scatter(lax.cond(is_student, product, nothing).astype(jnp.bfloat...  249 us
  transfers between devices with their start and end apart: 8, of which 8 were waited for; matrix products, arithmetic and copies ran while one was open for 5% of the time, Pallas kernels for 0%

commit v1 on v0

v1 whole, which is shorter than its diff:
```python
import jax
import jax.numpy as jnp
from jax import lax
from jax.experimental import pallas as pl
from jax.experimental.pallas import tpu as pltpu
from jax.sharding import PartitionSpec as P

LANES = 128


def gelu_tanh(values):
    return jax.nn.gelu(values, approximate=True)


def product(left, right):
    return jnp.dot(left, right, preferred_element_type=jnp.float32)


def over_tokens(left, right):
    return lax.dot_general(left, right, (((0,), (0,)), ((), ())), preferred_element_type=jnp.float32)


def across(left, right):
    return lax.dot_general(left, right, (((1,), (1,)), ((), ())), preferred_element_type=jnp.float32)


def ring_order(count):
    return list(range(0, count, 2)) + list(range(1, count, 2))[::-1]


def ring_shift(x, by):
    order = ring_order(lax.axis_size("dp"))
    count = len(order)
    return lax.ppermute(x, "dp", [(order[p], order[(p + by) % count]) for p in range(count)])


def from_core(x, by):
    count = lax.axis_size("mp")
    return lax.ppermute(x, "mp", [((c + by) % count, c) for c in range(count)])


def ring_gather(x, sign):
    count = lax.axis_size("dp")
    found = [x] * count
    there = back = x
    for hop in range(1, count // 2 + 1):
        there = ring_shift(there, sign)
        found[(-sign * hop) % count] = there
        if hop <= (count - 1) // 2:
            back = ring_shift(back, -sign)
            found[(sign * hop) % count] = back
    return found


def ring_scatter(terms, sign):
    count = lax.axis_size("dp")
    total = terms[0]
    for way, hops in ((sign, count // 2), (-sign, (count - 1) // 2)):
        if hops:
            running = terms[(way * hops) % count]
            for hop in range(hops - 1, -1, -1):
                arrived = ring_shift(running.astype(jnp.bfloat16), way).astype(jnp.float32)
                if hop:
                    running = arrived + terms[(way * hop) % count]
                else:
                    total = total + arrived
    return total


def in_vmem(count):
    return [pl.BlockSpec(memory_space=pltpu.VMEM)] * count


def placed_along(axis, offsets, pieces, length):
    extent = pieces[0].shape[axis]
    shape = list(pieces[0].shape)
    shape[axis] = length
    if axis == 1 and extent % LANES:
        result = jnp.zeros(shape, pieces[0].dtype)
        for k, piece in enumerate(pieces):
            result = lax.dynamic_update_slice_in_dim(result, piece, offsets[k], axis)
        return result

    def kernel(offset_ref, *refs):
        for k, ref in enumerate(refs[:-1]):
            where = pl.ds(pl.multiple_of(offset_ref[k], extent), extent)
            if axis == 0:
                refs[-1][where, :] = ref[...]
            else:
                refs[-1][:, where] = ref[...]

    return pl.pallas_call(
        kernel,
        out_shape=jax.ShapeDtypeStruct(shape, pieces[0].dtype),
        in_specs=[pl.BlockSpec(memory_space=pltpu.SMEM)] + in_vmem(len(pieces)),
        out_specs=pl.BlockSpec(memory_space=pltpu.VMEM),
        compiler_params=pltpu.CompilerParams(vmem_limit_bytes=16 << 20),
        cost_estimate=pl.CostEstimate(flops=0, bytes_accessed=4 * length * pieces[0].size // extent, transcendentals=0),
        name="place",
    )(jnp.stack(offsets).astype(jnp.int32), *pieces)


def received(side, offsets, arrivals, width):
    rows, share = arrivals[0][0].shape
    rows //= 2
    if share % LANES:
        results = []
        for top in (0, rows):
            result = jnp.zeros((rows, width), jnp.float32)
            for k, pieces in enumerate(arrivals):
                piece = lax.select_n(side, *[piece[top : top + rows] for piece in pieces]).astype(jnp.float32)
                result = lax.dynamic_update_slice_in_dim(result, piece, offsets[k], 1)
            results.append(result)
        return results
    sides = len(arrivals[0])
    flat = [piece for pieces in arrivals for piece in pieces]

    def kernel(offset_ref, *refs):
        for k in range(len(arrivals)):
            where = pl.ds(pl.multiple_of(offset_ref[k], share), share)
            for to in range(sides):

                @pl.when(offset_ref[len(arrivals)] == to)
                def _():
                    piece = refs[k * sides + to]
                    for half in range(2):
                        refs[-2 + half][:, where] = piece[half * rows : half * rows + rows, :].astype(jnp.float32)

    return pl.pallas_call(
        kernel,
        out_shape=[jax.ShapeDtypeStruct((rows, width), jnp.float32)] * 2,
        in_specs=[pl.BlockSpec(memory_space=pltpu.SMEM)] + in_vmem(len(flat)),
        out_specs=in_vmem(2),
        compiler_params=pltpu.CompilerParams(vmem_limit_bytes=24 << 20),
        name="received",
    )(jnp.stack(offsets + [side]).astype(jnp.int32), *flat)


def partner(index, step, count):
    return index ^ step if count & (count - 1) == 0 else (step - index) % count


def shards(tokens, up_weight, down_weight, mod_table, timesteps, valid_counts):
    count, cores, sides = lax.axis_size("dp"), lax.axis_size("mp"), lax.axis_size("side")
    me, core, side = lax.axis_index("dp"), lax.axis_index("mp"), lax.axis_index("side")
    rows, width = tokens.shape
    pieces = 2 if width % (2 * LANES) == 0 and cores == 2 else 1
    part = width // pieces
    block, hidden = up_weight.shape[1:]
    share = hidden // count
    features = block * count
    first = core * width if cores == 2 else 0
    peers = [partner(me, step, count) for step in range(count)]
    feature_offsets = [(peer * block - first) % features for peer in peers]

    def sent(step, piece, to=None):
        pairs = [(i, partner(i, step, count)) for i in range(count)]
        if to is not None:
            pairs = [(i * sides + sides - 1, j * sides + to) for i, j in pairs]
        if all(i == j for i, j in pairs):
            return piece
        return lax.ppermute(piece, "dp" if to is None else ("dp", "side"), pairs)

    ups = [sent(k, lax.dynamic_slice_in_dim(up_weight[0], peers[k] * share, share, 1)) for k in range(count)]
    downs = [sent(k, lax.dynamic_slice_in_dim(down_weight[0], peers[k] * share, share, 0)) for k in range(count)]
    up = placed_along(0, feature_offsets, ups, features)
    down = placed_along(1, feature_offsets, downs, features)

    wide = tokens.astype(jnp.float32)
    own_mean = jnp.mean(wide, axis=-1, keepdims=True)
    own_spread = jnp.sum((wide - own_mean) ** 2, axis=-1, keepdims=True)
    moments = jnp.concatenate([own_mean, own_spread], axis=1)
    if cores == 2:
        all_moments = jnp.stack([moments, from_core(moments, 1)])
    else:
        all_moments = lax.all_gather(moments, "mp")
    average = jnp.mean(all_moments[:, :, :1], axis=0)
    spread = jnp.sum(all_moments[:, :, 1:] + width * (all_moments[:, :, :1] - average) ** 2, axis=0)
    scaled = (wide - average) * lax.rsqrt(spread / features + 1e-06)
    modulation = lax.dynamic_slice(
        mod_table[0], (timesteps[0], 0, core * width), (1, mod_table.shape[2], width)
    )[0]
    normed = (scaled * (1.0 + modulation[1]) + modulation[0]).astype(jnp.bfloat16)
    gate = modulation[2]

    def spread_out(piece, index):
        found = ring_gather(piece, 1 if index % 2 == 0 else -1)
        return [found, [from_core(x, 1) for x in found]] if cores == 2 else of_all_cores(found)

    def of_all_cores(found):
        everything = lax.all_gather(jnp.concatenate(found, axis=0), "mp")
        return [[everything[t]] for t in range(cores)]

    def at(t, c):
        start = t * width + c * part
        return slice(start, start + part)

    parts = [(t, c) for t in range(cores) for c in range(pieces)]

    def summed(found, weight, times):
        return jnp.concatenate(
            [sum(times(found[c][t][r], weight(t, c)) for t, c in parts) for r in range(len(found[0][0]))], axis=0
        )

    all_normed = [spread_out(normed[:, c * part : (c + 1) * part], c) for c in range(pieces)]
    hidden_pre = summed(all_normed, lambda t, c: up[at(t, c)], product)
    hidden_act = gelu_tanh(hidden_pre).astype(jnp.bfloat16)

    valid_col = (jnp.arange(rows, dtype=jnp.int32) < valid_counts[me]).astype(jnp.float32)[:, None]
    valid_total = jnp.sum(valid_counts).astype(jnp.float32)

    outs, all_grads = [], []
    for c in range(pieces):
        if cores == 2:
            away = product(hidden_act, down[:, at(1, c)]).astype(jnp.bfloat16)
            term = product(hidden_act, down[:, at(0, c)]) + from_core(away, 1).astype(jnp.float32)
        else:
            term = lax.psum_scatter(
                product(hidden_act, down).astype(jnp.bfloat16), "mp", scatter_dimension=1, tiled=True
            ).astype(jnp.float32)
        mixed = ring_scatter([term[r * rows : (r + 1) * rows] for r in range(count)], 1 if c % 2 == 0 else -1)
        own = slice(c * part, (c + 1) * part)
        out = (wide[:, own] + gate[own] * mixed).astype(jnp.bfloat16)
        other = lax.ppermute(out, "side", [(i, i + 1) for i in range(sides - 1)])
        differ = out.astype(jnp.float32) - other.astype(jnp.float32)
        grad = (gate[own] * differ * valid_col / jnp.sqrt(valid_total)).astype(jnp.bfloat16)
        outs.append(out)
        all_grads.append(spread_out(grad, c))

    grad_act = summed(all_grads, lambda t, c: down[:, at(t, c)], across)
    unused, pullback = jax.vjp(gelu_tanh, hidden_pre)
    grad_pre = pullback(grad_act)[0].astype(jnp.bfloat16)

    def over_all_tokens(found, right):
        return jnp.concatenate(
            [over_tokens(jnp.concatenate(found[c][t], axis=0), right).astype(jnp.bfloat16) for t, c in parts], axis=0
        )

    down_found = over_all_tokens(all_grads, hidden_act)
    if cores > 2:
        own_normed, grad_pre = lax.optimization_barrier((normed, grad_pre))
        all_normed = [spread_out(own_normed[:, c * part : (c + 1) * part], c) for c in range(pieces)]
    up_found = over_all_tokens(all_normed, grad_pre)
    taken = block // sides
    arrivals = []
    for k in range(count):
        arrivals.append([])
        for to in range(sides):
            start = feature_offsets[k] + to * taken
            piece = jnp.concatenate(
                [lax.dynamic_slice_in_dim(found, start, taken, 0) for found in (up_found, down_found)], axis=0
            )
            arrivals[k].append(sent(k, piece, to))
    up_share, down_share = received(side, [peer * share for peer in peers], arrivals, hidden)
    return (jnp.concatenate(outs, axis=1)[None], up_share, down_share.T)


def solution(mesh):
    placed = (
        P("dp", "mp"),
        P("side", "dp", "mp"),
        P("side", "mp", "dp"),
        P("side", None, None, None),
        P("dp"),
        P(),
    )
    return jax.shard_map(
        shards,
        mesh=mesh,
        in_specs=placed,
        out_specs=(P("side", "dp", "mp"), P(("dp", "side"), "mp"), P("mp", ("dp", "side"))),
        check_vma=False,
    )
```

time: 1420 us -> 575 us (0.40)
  waiting for transfers between devices: 1290 us -> 336 us
  starting transfers between devices: 1.57 us -> 120 us
    all_gather x4 -> x0, waiting for transfers between devices: 723 us -> none  [the longest x1 360 us: shards(): lax.all_gather(up_weight[0], 'dp', axis=0, tiled=True)]
    reduce_scatter x3 -> x0, waiting for transfers between devices: 547 us -> none  [the longest x1 288 us: shards(): lax.psum_scatter(down_term.astype(jnp.bfloat16), ('dp', 'side'), scatter_...]
    ppermute x1 -> x108, waiting for transfers between devices: 17.7 us -> 336 us  [the longest x42 159 us: ring_shift(): lax.ppermute(x, 'dp', [(order[p], order[(p + by) % count]) for p in range...]
    ppermute x1 -> x108, starting transfers between devices: 1.29 us -> 120 us  [the longest x29 72 us: sent(): return lax.ppermute(piece, 'dp' if to is None else ('dp', 'side'), pairs)]
    cond x1 -> x0, local copies, waits for them, and re-layouts: 24.7 us -> none  [shards(): down_term = lax.cond(is_student, down_product, down_nothing)]
    unnamed x14 -> x189, local copies, waits for them, and re-layouts: 3.5 us -> 19.7 us
    dot_general x6 -> x76, matrix products: 55 us -> 54.4 us  [the longest x36 27.3 us: product(): return jnp.dot(left, right, preferred_element_type=jnp.float32)]
  transfers between devices with their start and end apart: 8 -> 108, of which waited for: 8 -> 57; matrix products, arithmetic and copies ran while one was open for 5% -> 12% of each run, Pallas kernels for 0% -> 0%
where the time goes in v1:
time: 575 us; the launch traced here: 566 us
  waiting for transfers between devices  336 us (58%)
  starting transfers between devices  120 us (21%)
  matrix products  54.4 us (9%)
  local copies, waits for them, and re-layouts  31.1 us (5%)
  other arithmetic  14.7 us (3%)
    ppermute x42, waiting for transfers between devices, ring_shift(): lax.ppermute(x, 'dp', [(order[p], order[(p + by) % count]) for p in range...  159 us
    ppermute x29, waiting for transfers between devices, sent(): return lax.ppermute(piece, 'dp' if to is None else ('dp', 'side'), pairs)  155 us
    ppermute x29, starting transfers between devices, sent(): return lax.ppermute(piece, 'dp' if to is None else ('dp', 'side'), pairs)  72 us
    ppermute x42, starting transfers between devices, ring_shift(): lax.ppermute(x, 'dp', [(order[p], order[(p + by) % count]) for p in range...  39.7 us
    dot_general x36, matrix products, product(): return jnp.dot(left, right, preferred_element_type=jnp.float32)  27.3 us
    unnamed x189, local copies, waits for them, and re-layouts  19.7 us
    ppermute x2, waiting for transfers between devices, shards(): other = lax.ppermute(out, 'side', [(i, i + 1) for i in range(sides - 1)])  17.8 us
    dot_general x8, matrix products, over_tokens(): lax.dot_general(left, right, (((0,), (0,)), ((), ())), preferred_element_...  14.6 us
  transfers between devices with their start and end apart: 108, of which 57 were waited for; matrix products, arithmetic and copies ran while one was open for 12% of the time, Pallas kernels for 0%

profile of v1, /device:TPU:10, one launch (start us, length us, event | category | flops | bytes accessed | tf_op | source)
XLA Modules:
  0.0 565.7 jit_solution(2458245660944807312)
XLA Ops:
  19.6 20.2 %collective-permute-done.7.refs_7_ = bf16[384,384]{1,0:T(8,128)(2,1)S(1)} collective-permute-done((bf16[384,384]{1,0:T(8,128)(2,1)S(1)}, bf16[384,384]{1,0:T(8,128)(2,1)S(1)}, u32[]{:S(2)}, u32[]{:S(2)}) %collective-permute-start.7) | collective-permute-done | bytes 294944 | tf_op jit(solution)/shard_map/ppermute | solution.py:162
  44.9 11.9 %collective-permute-done.4.refs_4_ = bf16[384,384]{1,0:T(8,128)(2,1)S(1)} collective-permute-done((bf16[384,384]{1,0:T(8,128)(2,1)S(1)}, bf16[384,384]{1,0:T(8,128)(2,1)S(1)}, u32[]{:S(2)}, u32[]{:S(2)}) %collective-permute-start.4) | collective-permute-done | bytes 294944 | tf_op jit(solution)/shard_map/ppermute | solution.py:162
  67.1 16.1 %collective-permute-done.6.refs_6_ = bf16[384,384]{1,0:T(8,128)(2,1)S(1)} collective-permute-done((bf16[384,384]{1,0:T(8,128)(2,1)}, bf16[384,384]{1,0:T(8,128)(2,1)S(1)}, u32[]{:S(2)}, u32[]{:S(2)}) %collective-permute-start.6) | collective-permute-done | bytes 294944 | tf_op jit(solution)/shard_map/ppermute | solution.py:162
  83.2 10.4 %collective-permute-done.44.refs_7_ = bf16[384,384]{1,0:T(8,128)(2,1)S(1)} collective-permute-done((bf16[384,384]{1,0:T(8,128)(2,1)}, bf16[384,384]{1,0:T(8,128)(2,1)S(1)}, u32[]{:S(2)}, u32[]{:S(2)}) %collective-permute-start.44) | collective-permute-done | bytes 294944 | tf_op jit(solution)/shard_map/ppermute | solution.py:162
  100.8 10.1 %collective-permute-done.41.refs_4_ = bf16[384,384]{1,0:T(8,128)(2,1)S(1)} collective-permute-done((bf16[384,384]{1,0:T(8,128)(2,1)}, bf16[384,384]{1,0:T(8,128)(2,1)S(1)}, u32[]{:S(2)}, u32[]{:S(2)}) %collective-permute-start.41) | collective-permute-done | bytes 294944 | tf_op jit(solution)/shard_map/ppermute | solution.py:162
  144.5 7.6 %collective-permute-done.14 = bf16[256,768]{1,0:T(8,128)(2,1)S(1)} collective-permute-done((bf16[256,768]{1,0:T(8,128)(2,1)S(1)}, bf16[256,768]{1,0:T(8,128)(2,1)S(1)}, u32[]{:S(2)}, u32[]{:S(2)}) %collective-permute-start.14) | collective-permute-done | bytes 393248 | tf_op jit(solution)/shard_map/ppermute | solution.py:34
  164.5 6.7 %collective-permute-done.18 = bf16[256,768]{1,0:T(8,128)(2,1)S(1)} collective-permute-done((bf16[256,768]{1,0:T(8,128)(2,1)S(1)}, bf16[256,768]{1,0:T(8,128)(2,1)S(1)}, u32[]{:S(2)}, u32[]{:S(2)}) %collective-permute-start.18) | collective-permute-done | bytes 393248 | tf_op jit(solution)/shard_map/ppermute | solution.py:34
  174.2 6.7 %collective-permute-done.24 = bf16[256,768]{1,0:T(8,128)(2,1)S(1)} collective-permute-done((bf16[256,768]{1,0:T(8,128)(2,1)S(1)}, bf16[256,768]{1,0:T(8,128)(2,1)S(1)}, u32[]{:S(2)}, u32[]{:S(2)}) %collective-permute-start.24) | collective-permute-done | bytes 393248 | tf_op jit(solution)/shard_map/ppermute | solution.py:34
  184.5 10.1 %collective-permute-done.25 = bf16[256,768]{1,0:T(8,128)(2,1)S(1)} collective-permute-done((bf16[256,768]{1,0:T(8,128)(2,1)S(1)}, bf16[256,768]{1,0:T(8,128)(2,1)S(1)}, u32[]{:S(2)}, u32[]{:S(2)}) %collective-permute-start.25) | collective-permute-done | bytes 393248 | tf_op jit(solution)/shard_map/ppermute | solution.py:34
  248.5 7.0 %collective-permute-done.58 = bf16[256,768]{1,0:T(8,128)(2,1)S(1)} collective-permute-done((bf16[256,768]{1,0:T(8,128)(2,1)S(1)}, bf16[256,768]{1,0:T(8,128)(2,1)S(1)}, u32[]{:S(2)}, u32[]{:S(2)}) %collective-permute-start.58) | collective-permute-done | bytes 393248 | tf_op jit(solution)/shard_map/ppermute | solution.py:34
  289.1 7.7 %collective-permute-done.49 = bf16[256,768]{1,0:T(8,128)(2,1)S(1)} collective-permute-done((bf16[256,768]{1,0:T(8,128)(2,1)S(1)}, bf16[256,768]{1,0:T(8,128)(2,1)S(1)}, u32[]{:S(2)}, u32[]{:S(2)}) %collective-permute-start.49) | collective-permute-done | bytes 393248 | tf_op jit(solution)/shard_map/ppermute | solution.py:34
  300.3 11.0 %collective-permute-done.61 = bf16[256,768]{1,0:T(8,128)(2,1)S(1)} collective-permute-done((bf16[256,768]{1,0:T(8,128)(2,1)S(1)}, bf16[256,768]{1,0:T(8,128)(2,1)S(1)}, u32[]{:S(2)}, u32[]{:S(2)}) %collective-permute-start.61) | collective-permute-done | bytes 393248 | tf_op jit(solution)/shard_map/ppermute | solution.py:224
  311.3 6.8 %collective-permute-done.62 = bf16[256,768]{1,0:T(8,128)(2,1)S(1)} collective-permute-done((bf16[256,768]{1,0:T(8,128)(2,1)S(1)}, bf16[256,768]{1,0:T(8,128)(2,1)S(1)}, u32[]{:S(2)}, u32[]{:S(2)}) %collective-permute-start.62) | collective-permute-done | bytes 393248 | tf_op jit(solution)/shard_map/ppermute | solution.py:224
  342.9 10.6 %collective-permute-done.85 = bf16[256,768]{1,0:T(8,128)(2,1)S(1)} collective-permute-done((bf16[256,768]{1,0:T(8,128)(2,1)S(1)}, bf16[256,768]{1,0:T(8,128)(2,1)S(1)}, u32[]{:S(2)}, u32[]{:S(2)}) %collective-permute-start.85) | collective-permute-done | bytes 393248 | tf_op jit(solution)/shard_map/ppermute | solution.py:34
  355.0 8.3 %collective-permute-done.70 = bf16[256,768]{1,0:T(8,128)(2,1)S(1)} collective-permute-done((bf16[256,768]{1,0:T(8,128)(2,1)S(1)}, bf16[256,768]{1,0:T(8,128)(2,1)S(1)}, u32[]{:S(2)}, u32[]{:S(2)}) %collective-permute-start.70) | collective-permute-done | bytes 393248 | tf_op jit(solution)/shard_map/ppermute | solution.py:34
  368.5 8.9 %collective-permute-done.74 = bf16[256,768]{1,0:T(8,128)(2,1)S(1)} collective-permute-done((bf16[256,768]{1,0:T(8,128)(2,1)S(1)}, bf16[256,768]{1,0:T(8,128)(2,1)S(1)}, u32[]{:S(2)}, u32[]{:S(2)}) %collective-permute-start.74) | collective-permute-done | bytes 393248 | tf_op jit(solution)/shard_map/ppermute | solution.py:34
  381.1 8.6 %collective-permute-done.86 = bf16[256,768]{1,0:T(8,128)(2,1)S(1)} collective-permute-done((bf16[256,768]{1,0:T(8,128)(2,1)S(1)}, bf16[256,768]{1,0:T(8,128)(2,1)S(1)}, u32[]{:S(2)}, u32[]{:S(2)}) %collective-permute-start.86) | collective-permute-done | bytes 393248 | tf_op jit(solution)/shard_map/ppermute | solution.py:34
  393.6 8.1 %collective-permute-done.80 = bf16[256,768]{1,0:T(8,128)(2,1)S(1)} collective-permute-done((bf16[256,768]{1,0:T(8,128)(2,1)S(1)}, bf16[256,768]{1,0:T(8,128)(2,1)S(1)}, u32[]{:S(2)}, u32[]{:S(2)}) %collective-permute-start.80) | collective-permute-done | bytes 393248 | tf_op jit(solution)/shard_map/ppermute | solution.py:34
  442.7 9.2 %collective-permute-start.98 = (bf16[384,384]{1,0:T(8,128)(2,1)S(1)}, bf16[384,384]{1,0:T(8,128)(2,1)S(1)}, u32[]{:S(2)}, u32[]{:S(2)}) collective-permute-start(bf16[384,384]{1,0:T(8,128)(2,1)S(1)} %pad_maximum_fusion.8), channel_id=1, source_target_pairs={{1,12},{5,8},{9,4},{13,0},{17,28},{21,24},{25,20},{29,16},{3,14},{... | collective-permute-start | bytes 884744 | tf_op jit(solution)/shard_map/ppermute | solution.py:162
  451.9 8.7 %collective-permute-start.99 = (bf16[384,384]{1,0:T(8,128)(2,1)S(1)}, bf16[384,384]{1,0:T(8,128)(2,1)S(1)}, u32[]{:S(2)}, u32[]{:S(2)}) collective-permute-start(bf16[384,384]{1,0:T(8,128)(2,1)S(1)} %pad_maximum_fusion.9), channel_id=1, source_target_pairs={{1,13},{5,9},{9,5},{13,1},{17,29},{21,25},{25,21},{29,17},{3,15},{... | collective-permute-start | bytes 884744 | tf_op jit(solution)/shard_map/ppermute | solution.py:162
  473.6 34.6 %collective-permute-done.100.refs_8_ = bf16[384,384]{1,0:T(8,128)(2,1)S(1)} collective-permute-done((bf16[384,384]{1,0:T(8,128)(2,1)S(1)}, bf16[384,384]{1,0:T(8,128)(2,1)S(1)}, u32[]{:S(2)}, u32[]{:S(2)}) %collective-permute-start.100) | collective-permute-done | bytes 294944 | tf_op jit(solution)/shard_map/ppermute | solution.py:162
  511.1 9.8 %collective-permute-done.101.refs_9_ = bf16[384,384]{1,0:T(8,128)(2,1)S(1)} collective-permute-done((bf16[384,384]{1,0:T(8,128)(2,1)S(1)}, bf16[384,384]{1,0:T(8,128)(2,1)S(1)}, u32[]{:S(2)}, u32[]{:S(2)}) %collective-permute-start.101) | collective-permute-done | bytes 294944 | tf_op jit(solution)/shard_map/ppermute | solution.py:162
  522.2 11.2 %collective-permute-done.102.refs_10_ = bf16[384,384]{1,0:T(8,128)(2,1)S(1)} collective-permute-done((bf16[384,384]{1,0:T(8,128)(2,1)S(1)}, bf16[384,384]{1,0:T(8,128)(2,1)S(1)}, u32[]{:S(2)}, u32[]{:S(2)}) %collective-permute-start.102) | collective-permute-done | bytes 294944 | tf_op jit(solution)/shard_map/ppermute | solution.py:162
  546.2 7.8 %collective-permute-done.105.refs_13_ = bf16[384,384]{1,0:T(8,128)(2,1)S(1)} collective-permute-done((bf16[384,384]{1,0:T(8,128)(2,1)S(1)}, bf16[384,384]{1,0:T(8,128)(2,1)S(1)}, u32[]{:S(2)}, u32[]{:S(2)}) %collective-permute-start.105) | collective-permute-done | bytes 294944 | tf_op jit(solution)/shard_map/ppermute | solution.py:162
  (519 shorter events, 303.4 us)
Async XLA Ops:
  6.3 33.5 %collective-permute-start.7 = (bf16[384,384]{1,0:T(8,128)(2,1)S(1)}, bf16[384,384]{1,0:T(8,128)(2,1)S(1)}, u32[]{:S(2)}, u32[]{:S(2)}) collective-permute-start(bf16[384,384]{1,0:T(8,128)(2,1)S(1)} %get-tuple-element.69), channel_id=1, source_target_pairs={{0,28},{4,24},{8,20},{12,16},{16,12},{20,8},{24,4},{28,0},{1,29},{... | collective-permute-start | bytes 884744 | tf_op jit(solution)/shard_map/ppermute | solution.py:162
  8.8 35.5 %collective-permute-start.5 = (bf16[384,384]{1,0:T(8,128)(2,1)}, bf16[384,384]{1,0:T(8,128)(2,1)S(1)}, u32[]{:S(2)}, u32[]{:S(2)}) collective-permute-start(bf16[384,384]{1,0:T(8,128)(2,1)} %get-tuple-element.70), channel_id=1, source_target_pairs={{0,20},{4,16},{8,28},{12,24},{16,4},{20,0},{24,12},{28,8},{1,21},{... | collective-permute-start | bytes 884744 | tf_op jit(solution)/shard_map/ppermute | solution.py:162
  10.0 46.8 %collective-permute-start.4 = (bf16[384,384]{1,0:T(8,128)(2,1)S(1)}, bf16[384,384]{1,0:T(8,128)(2,1)S(1)}, u32[]{:S(2)}, u32[]{:S(2)}) collective-permute-start(bf16[384,384]{1,0:T(8,128)(2,1)S(1)} %get-tuple-element.71), channel_id=1, source_target_pairs={{0,16},{4,20},{8,24},{12,28},{16,0},{20,4},{24,8},{28,12},{1,17},{... | collective-permute-start | bytes 884744 | tf_op jit(solution)/shard_map/ppermute | solution.py:162
  11.7 45.7 %collective-permute-start.3 = (bf16[384,384]{1,0:T(8,128)(2,1)S(1)}, bf16[384,384]{1,0:T(8,128)(2,1)S(1)}, u32[]{:S(2)}, u32[]{:S(2)}) collective-permute-start(bf16[384,384]{1,0:T(8,128)(2,1)S(1)} %get-tuple-element.72), channel_id=1, source_target_pairs={{0,12},{4,8},{8,4},{12,0},{16,28},{20,24},{24,20},{28,16},{1,13},{... | collective-permute-start | bytes 884744 | tf_op jit(solution)/shard_map/ppermute | solution.py:162
  19.5 43.2 %collective-permute-start.2 = (bf16[384,384]{1,0:T(8,128)(2,1)S(1)}, bf16[384,384]{1,0:T(8,128)(2,1)S(1)}, u32[]{:S(2)}, u32[]{:S(2)}) collective-permute-start(bf16[384,384]{1,0:T(8,128)(2,1)S(1)} %get-tuple-element.73), channel_id=1, source_target_pairs={{0,8},{4,12},{8,0},{12,4},{16,24},{20,28},{24,16},{28,20},{1,9},{5... | collective-permute-start | bytes 884744 | tf_op jit(solution)/shard_map/ppermute | solution.py:162
  44.3 38.9 %collective-permute-start.6 = (bf16[384,384]{1,0:T(8,128)(2,1)}, bf16[384,384]{1,0:T(8,128)(2,1)S(1)}, u32[]{:S(2)}, u32[]{:S(2)}) collective-permute-start(bf16[384,384]{1,0:T(8,128)(2,1)} %get-tuple-element.76), channel_id=1, source_target_pairs={{0,24},{4,28},{8,16},{12,20},{16,8},{20,12},{24,0},{28,4},{1,25},{... | collective-permute-start | bytes 884744 | tf_op jit(solution)/shard_map/ppermute | solution.py:162
  56.9 36.7 %collective-permute-start.44 = (bf16[384,384]{1,0:T(8,128)(2,1)}, bf16[384,384]{1,0:T(8,128)(2,1)S(1)}, u32[]{:S(2)}, u32[]{:S(2)}) collective-permute-start(bf16[384,384]{1,0:T(8,128)(2,1)} %get-tuple-element.61), channel_id=1, source_target_pairs={{0,28},{4,24},{8,20},{12,16},{16,12},{20,8},{24,4},{28,0},{1,29},{... | collective-permute-start | bytes 884744 | tf_op jit(solution)/shard_map/ppermute | solution.py:162
  57.4 40.8 %collective-permute-start.42 = (bf16[384,384]{1,0:T(8,128)(2,1)}, bf16[384,384]{1,0:T(8,128)(2,1)S(1)}, u32[]{:S(2)}, u32[]{:S(2)}) collective-permute-start(bf16[384,384]{1,0:T(8,128)(2,1)} %get-tuple-element.62), channel_id=1, source_target_pairs={{0,20},{4,16},{8,28},{12,24},{16,4},{20,0},{24,12},{28,8},{1,21},{... | collective-permute-start | bytes 884744 | tf_op jit(solution)/shard_map/ppermute | solution.py:162
  62.6 48.2 %collective-permute-start.41 = (bf16[384,384]{1,0:T(8,128)(2,1)}, bf16[384,384]{1,0:T(8,128)(2,1)S(1)}, u32[]{:S(2)}, u32[]{:S(2)}) collective-permute-start(bf16[384,384]{1,0:T(8,128)(2,1)} %get-tuple-element.63), channel_id=1, source_target_pairs={{0,16},{4,20},{8,24},{12,28},{16,0},{20,4},{24,8},{28,12},{1,17},{... | collective-permute-start | bytes 884744 | tf_op jit(solution)/shard_map/ppermute | solution.py:162
  64.2 51.6 %collective-permute-start.40 = (bf16[384,384]{1,0:T(8,128)(2,1)}, bf16[384,384]{1,0:T(8,128)(2,1)S(1)}, u32[]{:S(2)}, u32[]{:S(2)}) collective-permute-start(bf16[384,384]{1,0:T(8,128)(2,1)} %get-tuple-element.64), channel_id=1, source_target_pairs={{0,12},{4,8},{8,4},{12,0},{16,28},{20,24},{24,20},{28,16},{1,13},{... | collective-permute-start | bytes 884744 | tf_op jit(solution)/shard_map/ppermute | solution.py:162
  83.2 33.4 %collective-permute-start.39 = (bf16[384,384]{1,0:T(8,128)(2,1)}, bf16[384,384]{1,0:T(8,128)(2,1)}, u32[]{:S(2)}, u32[]{:S(2)}) collective-permute-start(bf16[384,384]{1,0:T(8,128)(2,1)} %get-tuple-element.65), channel_id=1, source_target_pairs={{0,8},{4,12},{8,0},{12,4},{16,24},{20,28},{24,16},{28,20},{1,9},{5... | collective-permute-start | bytes 884744 | tf_op jit(solution)/shard_map/ppermute | solution.py:162
  139.4 58.9 %collective-permute-start.36 = (bf16[256,768]{1,0:T(8,128)(2,1)S(1)}, bf16[256,768]{1,0:T(8,128)(2,1)S(1)}, u32[]{:S(2)}, u32[]{:S(2)}) collective-permute-start(bf16[256,768]{1,0:T(8,128)(2,1)S(1)} %collective-permute-done.22), channel_id=1, source_target_pairs={{2,0},{0,2},{3,1},{1,3},{6,4},{4,6},{7,5},{5,7},{10,8},{8,10},{11,... | collective-permute-start | bytes 1179656 | tf_op jit(solution)/shard_map/ppermute | solution.py:39
  164.1 33.8 %collective-permute-start.34 = (bf16[256,768]{1,0:T(8,128)(2,1)S(1)}, bf16[256,768]{1,0:T(8,128)(2,1)S(1)}, u32[]{:S(2)}, u32[]{:S(2)}) collective-permute-start(bf16[256,768]{1,0:T(8,128)(2,1)S(1)} %collective-permute-done.23), channel_id=1, source_target_pairs={{2,0},{0,2},{3,1},{1,3},{6,4},{4,6},{7,5},{5,7},{10,8},{8,10},{11,... | collective-permute-start | bytes 1179656 | tf_op jit(solution)/shard_map/ppermute | solution.py:39
  328.8 83.8 %collective-permute-start.91 = (bf16[256,768]{1,0:T(8,128)(2,1)S(1)}, bf16[256,768]{1,0:T(8,128)(2,1)S(1)}, u32[]{:S(2)}, u32[]{:S(2)}) collective-permute-start(bf16[256,768]{1,0:T(8,128)(2,1)S(1)} %collective-permute-done.77), channel_id=1, source_target_pairs={{2,0},{0,2},{3,1},{1,3},{6,4},{4,6},{7,5},{5,7},{10,8},{8,10},{11,... | collective-permute-start | bytes 1179656 | tf_op jit(solution)/shard_map/ppermute | solution.py:39
  331.8 34.6 %collective-permute-start.69 = (bf16[256,768]{1,0:T(8,128)(2,1)S(1)}, bf16[256,768]{1,0:T(8,128)(2,1)S(1)}, u32[]{:S(2)}, u32[]{:S(2)}) collective-permute-start(bf16[256,768]{1,0:T(8,128)(2,1)S(1)} %collective-permute-done.65), channel_id=1, source_target_pairs={{0,4},{8,0},{16,8},{24,16},{28,24},{20,28},{12,20},{4,12},{1,5},{9... | collective-permute-start | bytes 1179656 | tf_op jit(solution)/shard_map/ppermute | solution.py:34
  363.6 48.6 %collective-permute-start.89 = (bf16[256,768]{1,0:T(8,128)(2,1)S(1)}, bf16[256,768]{1,0:T(8,128)(2,1)S(1)}, u32[]{:S(2)}, u32[]{:S(2)}) collective-permute-start(bf16[256,768]{1,0:T(8,128)(2,1)S(1)} %collective-permute-done.78), channel_id=1, source_target_pairs={{2,0},{0,2},{3,1},{1,3},{6,4},{4,6},{7,5},{5,7},{10,8},{8,10},{11,... | collective-permute-start | bytes 1179656 | tf_op jit(solution)/shard_map/ppermute | solution.py:39
  460.6 47.6 %collective-permute-start.100 = (bf16[384,384]{1,0:T(8,128)(2,1)S(1)}, bf16[384,384]{1,0:T(8,128)(2,1)S(1)}, u32[]{:S(2)}, u32[]{:S(2)}) collective-permute-start(bf16[384,384]{1,0:T(8,128)(2,1)S(1)} %pad_maximum_fusion.10), channel_id=1, source_target_pairs={{1,16},{5,20},{9,24},{13,28},{17,0},{21,4},{25,8},{29,12},{3,18},{... | collective-permute-start | bytes 884744 | tf_op jit(solution)/shard_map/ppermute | solution.py:162
  463.8 57.0 %collective-permute-start.101 = (bf16[384,384]{1,0:T(8,128)(2,1)S(1)}, bf16[384,384]{1,0:T(8,128)(2,1)S(1)}, u32[]{:S(2)}, u32[]{:S(2)}) collective-permute-start(bf16[384,384]{1,0:T(8,128)(2,1)S(1)} %pad_maximum_fusion.11), channel_id=1, source_target_pairs={{1,17},{5,21},{9,25},{13,29},{17,1},{21,5},{25,9},{29,13},{3,19},{... | collective-permute-start | bytes 884744 | tf_op jit(solution)/shard_map/ppermute | solution.py:162
  465.8 67.6 %collective-permute-start.102 = (bf16[384,384]{1,0:T(8,128)(2,1)S(1)}, bf16[384,384]{1,0:T(8,128)(2,1)S(1)}, u32[]{:S(2)}, u32[]{:S(2)}) collective-permute-start(bf16[384,384]{1,0:T(8,128)(2,1)S(1)} %pad_maximum_fusion.12), channel_id=1, source_target_pairs={{1,20},{5,16},{9,28},{13,24},{17,4},{21,0},{25,12},{29,8},{3,22},{... | collective-permute-start | bytes 884744 | tf_op jit(solution)/shard_map/ppermute | solution.py:162
  467.2 72.6 %collective-permute-start.103 = (bf16[384,384]{1,0:T(8,128)(2,1)S(1)}, bf16[384,384]{1,0:T(8,128)(2,1)S(1)}, u32[]{:S(2)}, u32[]{:S(2)}) collective-permute-start(bf16[384,384]{1,0:T(8,128)(2,1)S(1)} %pad_maximum_fusion.13), channel_id=1, source_target_pairs={{1,21},{5,17},{9,29},{13,25},{17,5},{21,1},{25,13},{29,9},{3,23},{... | collective-permute-start | bytes 884744 | tf_op jit(solution)/shard_map/ppermute | solution.py:162
  472.3 73.8 %collective-permute-start.104 = (bf16[384,384]{1,0:T(8,128)(2,1)S(1)}, bf16[384,384]{1,0:T(8,128)(2,1)S(1)}, u32[]{:S(2)}, u32[]{:S(2)}) collective-permute-start(bf16[384,384]{1,0:T(8,128)(2,1)S(1)} %pad_maximum_fusion.14), channel_id=1, source_target_pairs={{1,24},{5,28},{9,16},{13,20},{17,8},{21,12},{25,0},{29,4},{3,26},{... | collective-permute-start | bytes 884744 | tf_op jit(solution)/shard_map/ppermute | solution.py:162
  508.2 45.7 %collective-permute-start.105 = (bf16[384,384]{1,0:T(8,128)(2,1)S(1)}, bf16[384,384]{1,0:T(8,128)(2,1)S(1)}, u32[]{:S(2)}, u32[]{:S(2)}) collective-permute-start(bf16[384,384]{1,0:T(8,128)(2,1)S(1)} %pad_maximum_fusion.15), channel_id=1, source_target_pairs={{1,25},{5,29},{9,17},{13,21},{17,9},{21,13},{25,1},{29,5},{3,27},{... | collective-permute-start | bytes 884744 | tf_op jit(solution)/shard_map/ppermute | solution.py:162
  520.9 36.2 %collective-permute-start.106 = (bf16[384,384]{1,0:T(8,128)(2,1)S(1)}, bf16[384,384]{1,0:T(8,128)(2,1)S(1)}, u32[]{:S(2)}, u32[]{:S(2)}) collective-permute-start(bf16[384,384]{1,0:T(8,128)(2,1)S(1)} %pad_maximum_fusion.16), channel_id=1, source_target_pairs={{1,28},{5,24},{9,20},{13,16},{17,12},{21,8},{25,4},{29,0},{3,30},{... | collective-permute-start | bytes 884744 | tf_op jit(solution)/shard_map/ppermute | solution.py:162
  533.4 29.0 %collective-permute-start.107 = (bf16[384,384]{1,0:T(8,128)(2,1)S(1)}, bf16[384,384]{1,0:T(8,128)(2,1)S(1)}, u32[]{:S(2)}, u32[]{:S(2)}) collective-permute-start(bf16[384,384]{1,0:T(8,128)(2,1)S(1)} %pad_maximum_fusion.17), channel_id=1, source_target_pairs={{1,29},{5,25},{9,21},{13,17},{17,13},{21,9},{25,5},{29,1},{3,31},{... | collective-permute-start | bytes 884744 | tf_op jit(solution)/shard_map/ppermute | solution.py:162
  (152 other events, 1711.2 us)

commit v2 on v1

v2 whole, which is shorter than its diff:
```python
import jax
import jax.numpy as jnp
from jax import lax
from jax.experimental import pallas as pl
from jax.experimental.pallas import tpu as pltpu
from jax.sharding import PartitionSpec as P

LANES = 128
TILE_ROWS = 16
DIGIT = 256


NO_COST = pl.CostEstimate(flops=0, bytes_accessed=0, transcendentals=0)


def gelu_tanh(values):
    return jax.nn.gelu(values, approximate=True)


def product(left, right):
    return jnp.dot(left, right, preferred_element_type=jnp.float32)


def over_tokens(left, right):
    return lax.dot_general(left, right, (((0,), (0,)), ((), ())), preferred_element_type=jnp.float32)


def across(left, right):
    return lax.dot_general(left, right, (((1,), (1,)), ((), ())), preferred_element_type=jnp.float32)


def ring_order(count):
    return list(range(0, count, 2)) + list(range(1, count, 2))[::-1]


def ring_shift(x, by):
    order = ring_order(lax.axis_size("dp"))
    count = len(order)
    return lax.ppermute(x, "dp", [(order[p], order[(p + by) % count]) for p in range(count)])


def from_core(x, by):
    count = lax.axis_size("mp")
    return lax.ppermute(x, "mp", [((c + by) % count, c) for c in range(count)])


def ring_gather(x, sign):
    count = lax.axis_size("dp")
    found = [x] * count
    there = back = x
    for hop in range(1, count // 2 + 1):
        there = ring_shift(there, sign)
        found[(-sign * hop) % count] = there
        if hop <= (count - 1) // 2:
            back = ring_shift(back, -sign)
            found[(sign * hop) % count] = back
    return found


def ring_scatter(terms, sign):
    count = lax.axis_size("dp")
    total = terms[0]
    for way, hops in ((sign, count // 2), (-sign, (count - 1) // 2)):
        if hops:
            running = terms[(way * hops) % count]
            for hop in range(hops - 1, -1, -1):
                arrived = ring_shift(running.astype(jnp.bfloat16), way).astype(jnp.float32)
                if hop:
                    running = arrived + terms[(way * hop) % count]
                else:
                    total = total + arrived
    return total


def in_vmem(count):
    return [pl.BlockSpec(memory_space=pltpu.VMEM)] * count


def placed_along(axis, offsets, pieces, length):
    shape = list(pieces[0].shape)
    shape[axis] = length
    result = jnp.zeros(shape, pieces[0].dtype)
    for k, piece in enumerate(pieces):
        result = lax.dynamic_update_slice_in_dim(result, piece, offsets[k], axis)
    return result


def placed(axis, scalars, arrays, pieces, shape):
    count = len(pieces)

    def kernel(scalar_ref, *refs):
        *taken, result, semaphores = refs
        copies = []
        for k, piece in enumerate(pieces):
            source = piece(taken, scalar_ref)
            extent = source.shape[axis]
            where = pl.ds(pl.multiple_of(scalar_ref[k], extent), extent)
            target = result.at[where, :] if axis == 0 else result.at[:, where]
            copies.append(pltpu.make_async_copy(source, target, semaphores.at[k]))
            copies[-1].start()
        for copy in copies:
            copy.wait()

    return pl.pallas_call(
        kernel,
        out_shape=jax.ShapeDtypeStruct(shape, arrays[0].dtype),
        in_specs=[pl.BlockSpec(memory_space=pltpu.SMEM)] + [pl.BlockSpec(memory_space=pl.ANY)] * len(arrays),
        out_specs=pl.BlockSpec(memory_space=pltpu.VMEM),
        scratch_shapes=[pltpu.SemaphoreType.DMA((count,))],
        compiler_params=pltpu.CompilerParams(vmem_limit_bytes=16 << 20),
        cost_estimate=NO_COST,
        name="placed",
    )(jnp.stack(scalars).astype(jnp.int32), *arrays)


def stacked(pieces):
    rows, columns = pieces[0].shape
    if columns % LANES:
        return jnp.concatenate(pieces, axis=0)

    def kernel(*refs):
        for k, ref in enumerate(refs[:-1]):
            refs[-1][k * rows : k * rows + rows, :] = ref[...]

    return pl.pallas_call(
        kernel,
        out_shape=jax.ShapeDtypeStruct((rows * len(pieces), columns), pieces[0].dtype),
        in_specs=in_vmem(len(pieces)),
        out_specs=pl.BlockSpec(memory_space=pltpu.VMEM),
        compiler_params=pltpu.CompilerParams(vmem_limit_bytes=16 << 20),
        cost_estimate=NO_COST,
        name="stacked",
    )(*pieces)


def stacked_parts(parts):
    rows, columns = parts[0][0].shape
    count = len(parts[0])
    flat = [piece for pieces in parts for piece in pieces]

    def kernel(*refs):
        for k, ref in enumerate(refs[:-1]):
            at = k % count * rows
            refs[-1][k // count, at : at + rows, :] = ref[...]

    return pl.pallas_call(
        kernel,
        out_shape=jax.ShapeDtypeStruct((len(parts), rows * count, columns), parts[0][0].dtype),
        in_specs=in_vmem(len(flat)),
        out_specs=pl.BlockSpec(memory_space=pltpu.VMEM),
        compiler_params=pltpu.CompilerParams(vmem_limit_bytes=24 << 20),
        cost_estimate=NO_COST,
        name="stacked_parts",
    )(*flat)


def modulated_up(tokens, rows, timesteps, places, table, up):
    _, kinds, features = table.shape
    images = timesteps.shape[0]
    _, sent_rows, part = tokens[0].shape
    total_rows = images * rows
    units = up.shape[1]
    halves = len(tokens) // 2

    def kernel(step_ref, place_ref, table_ref, up_ref, *refs):
        taken, (own_out, other_out, pre_ref, act_ref) = refs[: 2 * halves], refs[2 * halves :]
        total = sum(jnp.sum(ref[0, :rows].astype(jnp.float32), axis=-1, keepdims=True) for ref in taken)
        average = total / features
        squares = sum(
            jnp.sum((ref[0, :rows].astype(jnp.float32) - average) ** 2, axis=-1, keepdims=True) for ref in taken
        )
        inverse = lax.rsqrt(squares / features + 1e-06)
        pre = jnp.zeros((rows, units), jnp.float32)
        for place, ref in enumerate(taken):
            where = slice(place * part, (place + 1) * part)
            scaled = (ref[0, :rows].astype(jnp.float32) - average) * inverse
            here = pl.ds(pl.multiple_of(place_ref[place], LANES), part)
            value = scaled * (1.0 + table_ref[0, 1:2, here]) + table_ref[0, 0:1, here]
            value = value.astype(jnp.bfloat16)
            (own_out, other_out)[place // halves][place % halves] = value
            pre = pre + jnp.dot(value, up_ref[where, :], preferred_element_type=jnp.float32)
        pre_ref[...] = pre
        act_ref[...] = gelu_tanh(pre).astype(jnp.bfloat16)

    rows_of = pl.BlockSpec((halves, rows, part), lambda i, step_ref, place_ref: (0, i, 0))
    units_of = pl.BlockSpec((rows, units), lambda i, step_ref, place_ref: (i, 0))
    return pl.pallas_call(
        kernel,
        grid_spec=pltpu.PrefetchScalarGridSpec(
            num_scalar_prefetch=2,
            grid=(images,),
            in_specs=[
                pl.BlockSpec((1, kinds, features), lambda i, step_ref, place_ref: (step_ref[i], 0, 0)),
                pl.BlockSpec((features, units), lambda i, step_ref, place_ref: (0, 0)),
            ]
            + [pl.BlockSpec((1, sent_rows, part), lambda i, step_ref, place_ref: (i, 0, 0))] * len(tokens),
            out_specs=[rows_of, rows_of, units_of, units_of],
        ),
        out_shape=[jax.ShapeDtypeStruct((halves, total_rows, part), jnp.bfloat16)] * 2
        + [jax.ShapeDtypeStruct((total_rows, units), kind) for kind in (jnp.float32, jnp.bfloat16)],
        compiler_params=pltpu.CompilerParams(vmem_limit_bytes=40 << 20),
        cost_estimate=NO_COST,
        name="modulated_up",
    )(timesteps, places, table, up, *tokens)


def act_gradient(own, other, down, pre, rows):
    halves, total_rows, part = own.shape
    units, features = down.shape

    def kernel(down_ref, pre_ref, own_ref, other_ref, out_ref):
        total = jnp.zeros((rows, units), jnp.float32)
        for place in range(2 * halves):
            ref = (own_ref, other_ref)[place // halves]
            total = total + across(ref[place % halves], down_ref[:, place * part : (place + 1) * part])
        unused, pullback = jax.vjp(gelu_tanh, pre_ref[...])
        out_ref[...] = pullback(total)[0].astype(jnp.bfloat16)

    rows_of = pl.BlockSpec((halves, rows, part), lambda i: (0, i, 0))
    return pl.pallas_call(
        kernel,
        grid=(total_rows // rows,),
        in_specs=[
            pl.BlockSpec((units, features), lambda i: (0, 0)),
            pl.BlockSpec((rows, units), lambda i: (i, 0)),
            rows_of,
            rows_of,
        ],
        out_specs=pl.BlockSpec((rows, units), lambda i: (i, 0)),
        out_shape=jax.ShapeDtypeStruct((total_rows, units), jnp.bfloat16),
        compiler_params=pltpu.CompilerParams(vmem_limit_bytes=32 << 20),
        cost_estimate=NO_COST,
        name="act_gradient",
    )(down, pre, own, other)


def weight_gradient(lefts, rights, steps, block, one_side):
    halves, _, part = lefts[0][0].shape
    units = rights[0].shape[1]
    each = part // block
    count = halves * each
    half = block // 2
    groups = len(lefts)
    skipped = half // LANES * LANES

    def kernel(step_ref, *refs):
        left_refs, right_refs, outs = refs[: 2 * groups], refs[2 * groups : 3 * groups], refs[3 * groups :]

        def found(which, begin, end):
            return sum(
                over_tokens(left_refs[2 * g + which][0, :, begin:end], right_refs[g][...]) for g in range(groups)
            ).astype(jnp.bfloat16)

        for which in range(2):
            step = step_ref[which * count + pl.program_id(0)]
            if not one_side:
                value = found(which, 0, block)
                outs[0][step] = value[:half]
                outs[1][step] = value[half:]
                continue

            @pl.when(step_ref[2 * count] == 0)
            def _():
                outs[0][step] = found(which, 0, block - skipped)[:half]

            @pl.when(step_ref[2 * count] == 1)
            def _():
                outs[0][step] = found(which, skipped, block)[half - skipped :]

    left_specs = [
        pl.BlockSpec((1, x.shape[1], block), lambda i, step_ref: (i // each, 0, i % each)) for pair in lefts for x in pair
    ]
    right_specs = [pl.BlockSpec(x.shape, lambda i, step_ref: (0, 0)) for x in rights]
    results = 1 if one_side else 2
    return pl.pallas_call(
        kernel,
        grid_spec=pltpu.PrefetchScalarGridSpec(
            num_scalar_prefetch=1,
            grid=(count,),
            in_specs=left_specs + right_specs,
            out_specs=[pl.BlockSpec((2 * count, half, units), lambda i, step_ref: (0, 0, 0))] * results,
        ),
        out_shape=[jax.ShapeDtypeStruct((2 * count, half, units), jnp.bfloat16)] * results,
        compiler_params=pltpu.CompilerParams(vmem_limit_bytes=40 << 20),
        cost_estimate=NO_COST,
        name="weight_gradient",
    )(steps, *[x for pair in lefts for x in pair], *rights)


def after(x, *others):
    return lax.optimization_barrier((x, others))[0]


def received(offsets, arrivals, width):
    rows, share = arrivals[0].shape
    if share % LANES:
        result = jnp.zeros((rows, width), jnp.float32)
        for k, piece in enumerate(arrivals):
            result = lax.dynamic_update_slice_in_dim(result, piece.astype(jnp.float32), offsets[k], 1)
        return result

    def kernel(offset_ref, *refs):
        for k, ref in enumerate(refs[:-1]):
            where = pl.ds(pl.multiple_of(offset_ref[k], share), share)
            refs[-1][:, where] = ref[...].astype(jnp.float32)

    return pl.pallas_call(
        kernel,
        out_shape=jax.ShapeDtypeStruct((rows, width), jnp.float32),
        in_specs=[pl.BlockSpec(memory_space=pltpu.SMEM)] + in_vmem(len(arrivals)),
        out_specs=pl.BlockSpec(memory_space=pltpu.VMEM),
        compiler_params=pltpu.CompilerParams(vmem_limit_bytes=16 << 20),
        cost_estimate=NO_COST,
        name="received",
    )(jnp.stack(offsets).astype(jnp.int32), *arrivals)


def partner(index, step, count):
    return index ^ step if count & (count - 1) == 0 else (step - index) % count


def shards(tokens, up_weight, down_weight, mod_table, timesteps, valid_counts):
    count, cores, sides = lax.axis_size("dp"), lax.axis_size("mp"), lax.axis_size("side")
    me, core, side = lax.axis_index("dp"), lax.axis_index("mp"), lax.axis_index("side")
    is_student = side == 1
    rows, width = tokens.shape
    pieces = 2 if width % (2 * LANES) == 0 and cores == 2 else 1
    part = width // pieces
    block, hidden = up_weight.shape[1:]
    share = hidden // count
    features = block * count
    first = core * width if cores == 2 else 0
    peers = [partner(me, step, count) for step in range(count)]
    feature_offsets = [(peer * block - first) % features for peer in peers]

    def sent(step, piece):
        pairs = [(i, partner(i, step, count)) for i in range(count)]
        return piece if all(i == j for i, j in pairs) else lax.ppermute(piece, "dp", pairs)

    wide = tokens.astype(jnp.float32)
    own_mean = jnp.mean(wide, axis=-1, keepdims=True)
    own_spread = jnp.sum((wide - own_mean) ** 2, axis=-1, keepdims=True)
    moments = jnp.concatenate([own_mean, own_spread], axis=1)
    if cores == 2:
        all_moments = jnp.stack([moments, from_core(moments, 1)])
    else:
        all_moments = lax.all_gather(moments, "mp")
    average = jnp.mean(all_moments[:, :, :1], axis=0)
    spread = jnp.sum(all_moments[:, :, 1:] + width * (all_moments[:, :, :1] - average) ** 2, axis=0)
    scaled = (wide - average) * lax.rsqrt(spread / features + 1e-06)
    modulation = lax.dynamic_slice(
        mod_table[0], (timesteps[0], 0, core * width), (1, mod_table.shape[2], width)
    )[0]
    normed = (scaled * (1.0 + modulation[1]) + modulation[0]).astype(jnp.bfloat16)
    gate = modulation[2]

    def own_features(array):
        return [ring_gather(array[:, c * part : (c + 1) * part], 1 if c % 2 == 0 else -1) for c in range(pieces)]

    def widened(found):
        own = stacked(found)
        if cores == 2:
            return [own, from_core(own, 1)]
        everything = lax.all_gather(own, "mp")
        return [everything[t] for t in range(cores)]

    def at(t, c):
        start = t * width + c * part
        return slice(start, start + part)

    parts = [(t, c) for t in range(cores) for c in range(pieces)]

    normed_found = own_features(normed)
    ups = [sent(k, lax.dynamic_slice_in_dim(up_weight[0], peers[k] * share, share, 1)) for k in range(count)]
    downs = []
    for k in range(count):
        piece = lax.dynamic_slice_in_dim(down_weight[0], peers[k] * share, share, 0)
        hop = min((k + 1) // 2, (count - 1) // 2)
        if k and hop:
            piece = after(piece, *[found[way] for found in normed_found for way in (hop, count - hop)])
        downs.append(sent(k, piece))
    up = placed_along(0, feature_offsets, ups, features)
    down = placed_along(1, feature_offsets, downs, features)

    all_normed = [widened(found) for found in normed_found]
    hidden_pre = sum(product(all_normed[c][t], up[at(t, c)]) for t, c in parts)
    hidden_act = gelu_tanh(hidden_pre).astype(jnp.bfloat16)

    valid_col = (jnp.arange(rows, dtype=jnp.int32) < valid_counts[me]).astype(jnp.float32)[:, None]
    valid_total = jnp.sum(valid_counts).astype(jnp.float32)

    def of_student(x):
        return jnp.where(is_student, x, lax.ppermute(x, "side", [(1, 0)]))

    student_gate = of_student(gate)
    student_act = of_student(hidden_act)

    outs, grads = [], []
    for c in range(pieces):
        if cores == 2:
            away = product(hidden_act, down[:, at(1, c)]).astype(jnp.bfloat16)
            term = product(hidden_act, down[:, at(0, c)]) + from_core(away, 1).astype(jnp.float32)
        else:
            term = lax.psum_scatter(
                product(hidden_act, down).astype(jnp.bfloat16), "mp", scatter_dimension=1, tiled=True
            ).astype(jnp.float32)
        mixed = ring_scatter([term[r * rows : (r + 1) * rows] for r in range(count)], 1 if c % 2 == 0 else -1)
        own = slice(c * part, (c + 1) * part)
        out = (wide[:, own] + gate[own] * mixed).astype(jnp.bfloat16)
        other = lax.ppermute(out, "side", [(0, 1), (1, 0)])
        differ = out.astype(jnp.float32) - other.astype(jnp.float32)
        differ = jnp.where(is_student, differ, -differ)
        grad = (student_gate[own] * differ * valid_col / jnp.sqrt(valid_total)).astype(jnp.bfloat16)
        outs.append(out)
        grads.append(grad)

    grads_found = lax.optimization_barrier(own_features(jnp.concatenate(grads, axis=1)))
    all_grads = [widened(found) for found in grads_found]

    def over_all_tokens(found, right):
        return jnp.concatenate([over_tokens(found[c][t], right).astype(jnp.bfloat16) for t, c in parts], axis=0)

    taken = block // sides

    def delivered(own):
        own = own.reshape(count * taken, share)
        arrivals = [
            sent(k, lax.dynamic_slice_in_dim(own, feature_offsets[k] // sides, taken, 0)) for k in range(count)
        ]
        return received([peer * share for peer in peers], arrivals, hidden)

    down_found = over_all_tokens(all_grads, student_act).reshape(count, sides, taken, share)
    down_share = delivered(lax.dynamic_index_in_dim(down_found, side, 1, keepdims=False))
    grad_act = sum(across(all_grads[c][t], down[:, at(t, c)]) for t, c in parts)
    unused, pullback = jax.vjp(gelu_tanh, hidden_pre)
    grad_pre = pullback(grad_act)[0].astype(jnp.bfloat16)
    if cores > 2:
        own_normed, grad_pre = lax.optimization_barrier((normed, grad_pre))
        all_normed = [widened(found) for found in own_features(own_normed)]
    up_found = over_all_tokens(all_normed, grad_pre).reshape(count, sides, taken, share)
    up_share = delivered(jnp.where(is_student, up_found[:, 1], lax.ppermute(up_found[:, 0], "side", [(1, 0)])))
    return (jnp.concatenate(outs, axis=1)[None], up_share, down_share.T)


def paired_shards(tokens, up_weight, down_weight, mod_table, timesteps, valid_counts):
    count = lax.axis_size("dp")
    me, core, side = lax.axis_index("dp"), lax.axis_index("mp"), lax.axis_index("side")
    is_student = side == 1
    rows, width = tokens.shape
    part = width // 2
    block, hidden = up_weight.shape[1:]
    share = hidden // count
    features = block * count
    taken = block // 2
    peers = [partner(me, step, count) for step in range(count)]
    swap = [(0, 1), (1, 0)]

    def feature_offset(owner):
        start = owner * block
        t, c = (start // width + core) % 2, (start // part % 2 + side) % 2
        return (2 * t + c) * part + start % part

    feature_offsets = [feature_offset(peer) for peer in peers]

    def sent(step, piece):
        pairs = [(i, partner(i, step, count)) for i in range(count)]
        return piece if all(i == j for i, j in pairs) else lax.ppermute(piece, "dp", pairs)

    def halves(array):
        return [lax.dynamic_slice_in_dim(array, ((side + c) % 2) * part, part, array.ndim - 1) for c in range(2)]

    def of_student(x):
        return jnp.where(is_student, x, lax.ppermute(x, "side", [(1, 0)]))

    part_places = jnp.stack([(core + t) % 2 * width + (side + c) % 2 * part for t in range(2) for c in range(2)])
    part_places = part_places.astype(jnp.int32)
    gate = lax.dynamic_slice(mod_table[0], (timesteps[0], 2, core * width), (1, 1, width)).reshape(width)
    gates = halves(gate)
    student_gate = of_student(gate)

    farthest = count // 2
    near_images = [r for r in range(count) if min(r, count - r) <= farthest - 2]
    far_images = [farthest, farthest - 1, farthest + 1]
    steps = jnp.zeros((count,), jnp.int32).at[jnp.stack(feature_offsets) // block].set(jnp.arange(count, dtype=jnp.int32))
    steps = jnp.concatenate([steps, side[None].astype(jnp.int32)])

    token_halves = halves(tokens)
    column = lax.broadcasted_iota(jnp.int32, (TILE_ROWS, part), 1)
    digits = jnp.where(column == 0, timesteps[0] % DIGIT, jnp.where(column == 1, timesteps[0] // DIGIT, 0))
    there = back = jnp.concatenate([token_halves[0], digits.astype(jnp.bfloat16)], axis=0)
    round_ring = [there] + [None] * (count - 1)
    far, near = list(range(count - 1, farthest - 1, -1)), list(range(farthest - 1, 0, -1))
    arrived = []
    for hop in range(1, farthest + 1):
        there = ring_shift(there, 1)
        round_ring[-hop % count] = there
        if hop <= (count - 1) // 2:
            back = ring_shift(back, -1)
            round_ring[hop] = back
        arrived.append([there, back])

    columns, column, row = count // 2, me // 2, me % 2

    def over_columns(step, piece):
        pairs = [(i, 2 * partner(i // 2, step, columns) + i % 2) for i in range(count)]
        return lax.ppermute(piece, "dp", pairs) if step else piece

    def over_rows(piece):
        return lax.ppermute(piece, "dp", [(i, i ^ 1) for i in range(count)])

    column_peers = [partner(column, step, columns) for step in range(columns)]
    steps_out = list(range(columns - 1, -1, -1))
    up_pairs = [None] * columns
    for step in steps_out:
        piece = lax.dynamic_slice_in_dim(up_weight[0], column_peers[step] * 2 * share, 2 * share, 1)
        up_pairs[step] = over_columns(step, piece)
    up_passed = over_rows(jnp.stack([lax.dynamic_slice_in_dim(x, (1 - row) * share, share, 1) for x in up_pairs]))
    by_row = down_weight[0].reshape(columns, 2, share, block)
    down_kept = lax.dynamic_index_in_dim(by_row, row, 1, keepdims=False)
    down_passed = over_rows(lax.dynamic_index_in_dim(by_row, 1 - row, 1, keepdims=False))
    down_pairs = [None] * columns
    for step in steps_out:
        piece = jnp.stack(
            [lax.dynamic_index_in_dim(x, column_peers[step], 0, keepdims=False) for x in (down_kept, down_passed)]
        )
        down_pairs[step] = over_columns(step, after(piece, *up_pairs[1:]))

    def up_piece(k):
        if k % 2:
            return lambda refs, scalar_ref: refs[columns].at[k // 2]
        return lambda refs, scalar_ref: refs[k // 2].at[
            :, pl.ds(pl.multiple_of(scalar_ref[count] * share, share), share)
        ]

    def down_piece(k):
        return lambda refs, scalar_ref: refs[k // 2].at[k % 2]

    def all_features(images):
        first = stacked([round_ring[r] for r in images])
        crossed = after(lax.ppermute(first, "side", swap), *up_pairs[1:])
        pair = [first, crossed]
        steps_taken = first.reshape(len(images), rows + TILE_ROWS, part)[:, rows, :2].astype(jnp.int32)
        shaped = [x.reshape(len(images), rows + TILE_ROWS, part) for x in pair + [from_core(x, 1) for x in pair]]
        return shaped, steps_taken[:, 0] + DIGIT * steps_taken[:, 1]

    near_tokens, near_steps = all_features(near_images)
    far_tokens, far_steps = all_features(far_images)
    scalars = feature_offsets + [row]
    up = placed(0, scalars, up_pairs + [up_passed], [up_piece(k) for k in range(count)], (features, share))
    table = mod_table[0]
    *far_normed, far_pre, far_act = modulated_up(far_tokens, rows, far_steps, part_places, table, up)
    near_tokens = after(near_tokens, far_act)
    *near_normed, near_pre, near_act = modulated_up(near_tokens, rows, near_steps, part_places, table, up)
    down_pairs = after(down_pairs, near_act)
    down = placed(1, scalars, down_pairs, [down_piece(k) for k in range(count)], (share, features))

    student_acts = [of_student(near_act), of_student(far_act)]
    valid_col = (jnp.arange(rows, dtype=jnp.int32) < valid_counts[me]).astype(jnp.float32)[:, None]
    valid_total = jnp.sum(valid_counts).astype(jnp.float32)
    terms = [[None] * count, [None] * count]
    earlier = []
    groups = [(far_images[:1], far_act[:rows]), (far_images[1:], far_act[rows:]), (near_images, near_act)]
    earlier = []
    for images, act in groups:
        act = after(act, *earlier)
        from_other = from_core(product(act, down[:, width:]).astype(jnp.bfloat16), 1)
        earlier = [from_other]
        for c in range(2):
            here = slice(c * part, (c + 1) * part)
            term = product(act, down[:, here]) + from_other[:, here].astype(jnp.float32)
            for k, r in enumerate(images):
                terms[c][r] = term[k * rows : (k + 1) * rows]
    mixed = [ring_scatter(terms[c], 1 if c == 0 else -1) for c in range(2)]
    mixed, student_acts, student_gate = lax.optimization_barrier((mixed, student_acts, student_gate))
    student_gates = halves(student_gate)
    outs = [(token_halves[c].astype(jnp.float32) + gates[c] * mixed[c]).astype(jnp.bfloat16) for c in range(2)]
    found = []
    for c in range(2):
        differ = outs[c].astype(jnp.float32) - lax.ppermute(outs[1 - c], "side", swap).astype(jnp.float32)
        differ = jnp.where(is_student, differ, -differ)
        grad = (student_gates[c] * differ * valid_col / jnp.sqrt(valid_total)).astype(jnp.bfloat16)
        found.append([grad] + [None] * (count - 1))

    there, back = [found[c][0] for c in range(2)], [found[c][0] for c in range(2)]
    for hop in range(1, farthest + 1):
        if hop == farthest:
            near_own = stacked_parts([[found[c][r] for r in near_images] for c in range(2)])
            near_grads = [near_own, from_core(near_own, 1)]
            there = after(there, *near_grads)
        for c, way in ((0, 1), (1, -1)):
            there[c] = ring_shift(there[c], way)
            found[c][(-way * hop) % count] = there[c]
            if hop <= (count - 1) // 2:
                back[c] = ring_shift(back[c], -way)
                found[c][(way * hop) % count] = back[c]
    near_grad_pre = act_gradient(*near_grads, down, near_pre, rows)
    far_found = [[found[c][r] for r in far_images] for c in range(2)]
    far_own = stacked_parts(after(far_found, *there, near_grad_pre))
    far_grads = [far_own, from_core(far_own, 1)]

    (down_found,) = weight_gradient([near_grads, far_grads], student_acts, steps, block, True)
    down_arrived = [sent(k, down_found[k]) for k in range(count)]
    far_grad_pre = act_gradient(*after(far_grads, down_found), down, far_pre, rows)
    far_grad_pre = after(far_grad_pre, down_arrived[far[0]])
    up_found = weight_gradient([near_normed, far_normed], [near_grad_pre, far_grad_pre], steps, block, False)
    handed = after(up_found[0], down_arrived[far[2]])
    split = count // 2
    handed = [lax.ppermute(x, "side", [(1, 0)]) for x in (handed[split:], handed[:split])]
    first = jnp.where(is_student, up_found[1][split:], after(handed[0], *[down_arrived[k] for k in near]))
    up_arrived = [None] * split + [sent(k, first[k - split]) for k in range(split, count)]
    second = jnp.where(is_student, up_found[1][:split], after(handed[1], up_arrived[far[0]]))
    up_arrived[:split] = [sent(k, second[k]) for k in range(split)]
    places = [peer * share for peer in peers]
    out = jnp.concatenate(
        [jnp.where(side == 0, outs[0], outs[1]), jnp.where(side == 0, outs[1], outs[0])], axis=1
    )
    return (out[None], received(places, up_arrived, hidden), received(places, down_arrived, hidden).T)


def solution(mesh):
    placed = (
        P("dp", "mp"),
        P("side", "dp", "mp"),
        P("side", "mp", "dp"),
        P("side", None, None, None),
        P("dp"),
        P(),
    )
    paired = mesh.shape["mp"] == mesh.shape["side"] == 2 and mesh.shape["dp"] in (8, 16, 32)
    return jax.shard_map(
        paired_shards if paired else shards,
        mesh=mesh,
        in_specs=placed,
        out_specs=(P("side", "dp", "mp"), P(("dp", "side"), "mp"), P("mp", ("dp", "side"))),
        check_vma=False,
    )
```

time: 575 us -> 458 us (0.80)
  waiting for transfers between devices: 336 us -> 228 us
  Pallas kernels: 5.26 us -> 62.9 us
  matrix products: 54.4 us -> 17.4 us
  starting transfers between devices: 120 us -> 86.8 us
  local copies, waits for them, and re-layouts: 31.1 us -> 38.8 us
    ppermute x31, waiting for transfers between devices: 173 us -> 95.6 us  [the longest x6 37.1 us: over_columns(): return lax.ppermute(piece, 'dp', pairs) if step else piece]
    pallas_call x3 -> x14, Pallas kernels: 5.26 us -> 62.9 us  [the longest x2 21.2 us: modulated_up(): pl.pallas_call(kernel, grid_spec=pltpu.PrefetchScalarGridSpec(num_scalar_...]
    ppermute x42 -> x35, waiting for transfers between devices: 159 us -> 123 us  [ring_shift(): lax.ppermute(x, 'dp', [(order[p], order[(p + by) % count]) for p in range...]
    dot_general x40 -> x0, matrix products: 27.1 us -> none  [the longest x8 14.6 us: over_tokens(): lax.dot_general(left, right, (((0,), (0,)), ((), ())), preferred_element_...]
    ppermute x31, starting transfers between devices: 74.7 us -> 50.7 us  [the longest x14 20.9 us: sent(): lax.ppermute(piece, 'dp', pairs)]
    dot_general x36 -> x9, matrix products: 27.3 us -> 17.4 us  [product(): return jnp.dot(left, right, preferred_element_type=jnp.float32)]
    squeeze x0 -> x5, local copies, waits for them, and re-layouts: none -> 6.14 us  [the longest x1 2.67 us: paired_shards(): mod_table[0]]
    ppermute x35 -> x9, waiting for transfers between devices: 3.53 us -> 9.55 us  [from_core(): return lax.ppermute(x, 'mp', [((c + by) % count, c) for c in range(count)])]
  transfers between devices with their start and end apart: 108 -> 75, of which waited for: 57 -> 48; matrix products, arithmetic and copies ran while one was open for 12% -> 10% of each run, Pallas kernels for 0% -> 10%
where the time goes in v2:
time: 458 us; the launch traced here: 451 us
  waiting for transfers between devices  228 us (50%)
  starting transfers between devices  86.8 us (19%)
  Pallas kernels  62.9 us (14%)
  local copies, waits for them, and re-layouts  38.8 us (8%)
  matrix products  17.4 us (4%)
  other arithmetic  14 us (3%)
    ppermute x35, waiting for transfers between devices, ring_shift(): lax.ppermute(x, 'dp', [(order[p], order[(p + by) % count]) for p in range...  123 us
    ppermute x6, waiting for transfers between devices, over_columns(): return lax.ppermute(piece, 'dp', pairs) if step else piece  37.1 us
    ppermute x35, starting transfers between devices, ring_shift(): lax.ppermute(x, 'dp', [(order[p], order[(p + by) % count]) for p in range...  35 us
    ppermute x14, waiting for transfers between devices, sent(): lax.ppermute(piece, 'dp', pairs)  24.1 us
    pallas_call x2, Pallas kernels, modulated_up(): pl.pallas_call(kernel, grid_spec=pltpu.PrefetchScalarGridSpec(num_scalar_...  21.2 us
    ppermute x14, starting transfers between devices, sent(): lax.ppermute(piece, 'dp', pairs)  20.9 us
    pallas_call x2, Pallas kernels, weight_gradient(): pl.pallas_call(kernel, grid_spec=pltpu.PrefetchScalarGridSpec(num_scalar_...  18.3 us
    dot_general x9, matrix products, product(): return jnp.dot(left, right, preferred_element_type=jnp.float32)  17.4 us
  transfers between devices with their start and end apart: 75, of which 48 were waited for; matrix products, arithmetic and copies ran while one was open for 10% of the time, Pallas kernels for 10%

profile of v2, /device:TPU:10, one launch (start us, length us, event | category | flops | bytes accessed | tf_op | source)
XLA Modules:
  0.0 450.6 jit_solution(16023163622411072105)
XLA Ops:
  4.5 9.4 %collective-permute-done.refs_1_ = bf16[272,768]{1,0:T(8,128)(2,1)S(1)} collective-permute-done((bf16[272,768]{1,0:T(8,128)(2,1)S(1)}, bf16[272,768]{1,0:T(8,128)(2,1)S(1)}, u32[]{:S(2)}, u32[]{:S(2)}) %collective-permute-start) | collective-permute-done | bytes 417824 | tf_op jit(solution)/shard_map/ppermute | solution.py:39
  15.9 8.6 %collective-permute-done.1.refs_2_ = bf16[272,768]{1,0:T(8,128)(2,1)} collective-permute-done((bf16[272,768]{1,0:T(8,128)(2,1)S(1)}, bf16[272,768]{1,0:T(8,128)(2,1)}, u32[]{:S(2)}, u32[]{:S(2)}) %collective-permute-start.1) | collective-permute-done | bytes 417824 | tf_op jit(solution)/shard_map/ppermute | solution.py:39
  28.5 7.7 %collective-permute-done.11.refs_2_ = bf16[272,768]{1,0:T(8,128)(2,1)S(1)} collective-permute-done((bf16[272,768]{1,0:T(8,128)(2,1)S(1)}, bf16[272,768]{1,0:T(8,128)(2,1)S(1)}, u32[]{:S(2)}, u32[]{:S(2)}) %collective-permute-start.11) | collective-permute-done | bytes 417824 | tf_op jit(solution)/shard_map/ppermute | solution.py:39
  43.0 23.6 %collective-permute-done.12.refs_0_ = bf16[272,768]{1,0:T(8,128)(2,1)S(1)} collective-permute-done((bf16[272,768]{1,0:T(8,128)(2,1)S(1)}, bf16[272,768]{1,0:T(8,128)(2,1)S(1)}, u32[]{:S(2)}, u32[]{:S(2)}) %collective-permute-start.12) | collective-permute-done | bytes 417824 | tf_op jit(solution)/shard_map/ppermute | solution.py:39
  81.6 12.8 %collective-permute-done.5.refs_2_ = bf16[384,768]{1,0:T(8,128)(2,1)} collective-permute-done((bf16[384,768]{1,0:T(8,128)(2,1)}, bf16[384,768]{1,0:T(8,128)(2,1)}, u32[]{:S(2)}, u32[]{:S(2)}) %collective-permute-start.5) | collective-permute-done | bytes 589856 | tf_op jit(solution)/shard_map/ppermute | solution.py:506
  113.5 16.0 %collective-permute-done.7.refs_4_ = bf16[4,384,384]{2,1,0:T(8,128)(2,1)} collective-permute-done((bf16[4,384,384]{2,1,0:T(8,128)(2,1)}, bf16[4,384,384]{2,1,0:T(8,128)(2,1)}, u32[]{:S(2)}, u32[]{:S(2)}) %collective-permute-start.7) | collective-permute-done | bytes 1179680 | tf_op jit(solution)/shard_map/ppermute | solution.py:509
  137.0 8.1 %modulated_up.2 = (bf16[2,768,768]{2,1,0:T(8,128)(2,1)S(1)}, bf16[2,768,768]{2,1,0:T(8,128)(2,1)S(1)}, f32[768,384]{1,0:T(8,128)S(1)}, bf16[768,384]{1,0:T(8,128)(2,1)S(1)}) custom-call(s32[3]{0:T(128)S(1)} %add_bitcast_fusion.step_ref, s32[4]{0:T(128)S(1)} %pad_add_fusion.place_ref, f32[50,3,3072]{2,1,0:T(4,128)} %copy.20.table_ref, ...), custom_call_target="tpu_custom_call" | custom-call | tf_op jit(solution)/shard_map/modulated_up/pallas_call | solution.py:187
  149.0 13.0 %modulated_up.3 = (bf16[2,1280,768]{2,1,0:T(8,128)(2,1)}, bf16[2,1280,768]{2,1,0:T(8,128)(2,1)}, f32[1280,384]{1,0:T(8,128)S(1)}, bf16[1280,384]{1,0:T(8,128)(2,1)S(1)}) custom-call(s32[5]{0:T(128)S(1)} %add_bitcast_fusion.1.step_ref, s32[4]{0:T(128)S(1)} %pad_add_fusion.place_ref, f32[50,3,3072]{2,1,0:T(4,128)} %copy.20.table_ref, ...), custom_call_target="tpu_custom_call" | custom-call | tf_op jit(solution)/shard_map/modulated_up/pallas_call | solution.py:187
  162.0 9.6 %collective-permute-done.19.refs_2_ = bf16[2,384,384]{2,1,0:T(8,128)(2,1)} collective-permute-done((bf16[2,384,384]{2,1,0:T(8,128)(2,1)}, bf16[2,384,384]{2,1,0:T(8,128)(2,1)}, u32[]{:S(2)}, u32[]{:S(2)}) %collective-permute-start.19) | collective-permute-done | bytes 589856 | tf_op jit(solution)/shard_map/ppermute | solution.py:506
  171.7 13.1 %collective-permute-done.20.refs_3_ = bf16[2,384,384]{2,1,0:T(8,128)(2,1)} collective-permute-done((bf16[2,384,384]{2,1,0:T(8,128)(2,1)}, bf16[2,384,384]{2,1,0:T(8,128)(2,1)}, u32[]{:S(2)}, u32[]{:S(2)}) %collective-permute-start.20) | collective-permute-done | bytes 589856 | tf_op jit(solution)/shard_map/ppermute | solution.py:506
  247.5 5.0 %collective-permute-done.26 = bf16[256,768]{1,0:T(8,128)(2,1)S(1)} collective-permute-done((bf16[256,768]{1,0:T(8,128)(2,1)S(1)}, bf16[256,768]{1,0:T(8,128)(2,1)S(1)}, u32[]{:S(2)}, u32[]{:S(2)}) %collective-permute-start.26) | collective-permute-done | bytes 393248 | tf_op jit(solution)/shard_map/ppermute | solution.py:39
  257.1 6.2 %collective-permute-done.33 = bf16[256,768]{1,0:T(8,128)(2,1)S(1)} collective-permute-done((bf16[256,768]{1,0:T(8,128)(2,1)S(1)}, bf16[256,768]{1,0:T(8,128)(2,1)S(1)}, u32[]{:S(2)}, u32[]{:S(2)}) %collective-permute-start.33) | collective-permute-done | bytes 393248 | tf_op jit(solution)/shard_map/ppermute | solution.py:39
  266.7 5.0 %collective-permute-done.30 = bf16[256,768]{1,0:T(8,128)(2,1)S(1)} collective-permute-done((bf16[256,768]{1,0:T(8,128)(2,1)S(1)}, bf16[256,768]{1,0:T(8,128)(2,1)S(1)}, u32[]{:S(2)}, u32[]{:S(2)}) %collective-permute-start.30) | collective-permute-done | bytes 393248 | tf_op jit(solution)/shard_map/ppermute | solution.py:39
  280.1 4.9 %collective-permute-done.46 = bf16[256,768]{1,0:T(8,128)(2,1)S(1)} collective-permute-done((bf16[256,768]{1,0:T(8,128)(2,1)S(1)}, bf16[256,768]{1,0:T(8,128)(2,1)S(1)}, u32[]{:S(2)}, u32[]{:S(2)}) %collective-permute-start.46) | collective-permute-done | bytes 393248 | tf_op jit(solution)/shard_map/ppermute | solution.py:579
  289.6 5.7 %collective-permute-done.41 = bf16[256,768]{1,0:T(8,128)(2,1)S(1)} collective-permute-done((bf16[256,768]{1,0:T(8,128)(2,1)S(1)}, bf16[256,768]{1,0:T(8,128)(2,1)S(1)}, u32[]{:S(2)}, u32[]{:S(2)}) %collective-permute-start.41) | collective-permute-done | bytes 393248 | tf_op jit(solution)/shard_map/ppermute | solution.py:579
  301.2 6.4 %collective-permute-done.42.refs_1_ = bf16[256,768]{1,0:T(8,128)(2,1)S(1)} collective-permute-done((bf16[256,768]{1,0:T(8,128)(2,1)S(1)}, bf16[256,768]{1,0:T(8,128)(2,1)S(1)}, u32[]{:S(2)}, u32[]{:S(2)}) %collective-permute-start.42) | collective-permute-done | bytes 393248 | tf_op jit(solution)/shard_map/ppermute | solution.py:39
  309.6 6.4 %collective-permute-done.48.refs_7_ = bf16[256,768]{1,0:T(8,128)(2,1)S(1)} collective-permute-done((bf16[256,768]{1,0:T(8,128)(2,1)S(1)}, bf16[256,768]{1,0:T(8,128)(2,1)S(1)}, u32[]{:S(2)}, u32[]{:S(2)}) %collective-permute-start.48) | collective-permute-done | bytes 393248 | tf_op jit(solution)/shard_map/ppermute | solution.py:39
  326.5 7.9 %collective-permute-done.53.refs_4_ = bf16[256,768]{1,0:T(8,128)(2,1)S(1)} collective-permute-done((bf16[256,768]{1,0:T(8,128)(2,1)S(1)}, bf16[256,768]{1,0:T(8,128)(2,1)S(1)}, u32[]{:S(2)}, u32[]{:S(2)}) %collective-permute-start.53) | collective-permute-done | bytes 393248 | tf_op jit(solution)/shard_map/ppermute | solution.py:39
  336.8 6.1 %act_gradient.2.refs_4_ = bf16[1280,384]{1,0:T(8,128)(2,1)S(1)} custom-call(bf16[384,3072]{1,0:T(8,128)(2,1)S(1)} %placed.3.down_ref, f32[1280,384]{1,0:T(8,128)S(1)} %copy-done.17, bf16[2,1280,768]{2,1,0:T(8,128)(2,1)S(1)} %stacked_parts.2.own_ref.refs_0_, bf16[2,1280,768]{2,1,0:T(8,128)(2,1)S(1)} %collective-permute-done.51.other_ref.refs_1_), custom_call_target="tpu_custom_call" | custom-call | tf_op jit(solution)/shard_map/act_gradient/pallas_call | solution.py:220
  343.2 7.6 %collective-permute-done.54.refs_0_ = bf16[256,768]{1,0:T(8,128)(2,1)S(1)} collective-permute-done((bf16[256,768]{1,0:T(8,128)(2,1)S(1)}, bf16[256,768]{1,0:T(8,128)(2,1)S(1)}, u32[]{:S(2)}, u32[]{:S(2)}) %collective-permute-start.54) | collective-permute-done | bytes 393248 | tf_op jit(solution)/shard_map/ppermute | solution.py:39
  360.5 8.6 %weight_gradient.2 = bf16[8,192,384]{2,1,0:T(8,128)(2,1)S(1)} custom-call(s32[9]{0:T(128)S(1)} %pad_add_fusion.1.step_ref, bf16[2,1280,768]{2,1,0:T(8,128)(2,1)S(1)} %copy-done.1, bf16[2,1280,768]{2,1,0:T(8,128)(2,1)} %copy-done.2, bf16[2,768,768]{2,1,0:T(8,128)(2,1)} %stacked_parts.3.refs_2_.own_ref, ...), custom_call_target="tpu_custom_call" | custom-call | tf_op jit(solution)/shard_map/weight_gradient/pallas_call | solution.py:275
  375.0 5.6 %act_gradient.3.refs_5_ = bf16[768,384]{1,0:T(8,128)(2,1)S(1)} custom-call(bf16[384,3072]{1,0:T(8,128)(2,1)S(1)} %placed.3.down_ref, f32[768,384]{1,0:T(8,128)S(1)} %copy-done.19, bf16[2,768,768]{2,1,0:T(8,128)(2,1)} %stacked_parts.3.refs_2_.own_ref, bf16[2,768,768]{2,1,0:T(8,128)(2,1)} %collective-permute-done.58.refs_3_.other_ref), custom_call_target="tpu_custom_call" | custom-call | tf_op jit(solution)/shard_map/act_gradient/pallas_call | solution.py:220
  384.6 9.7 %weight_gradient.3 = (bf16[8,192,384]{2,1,0:T(8,128)(2,1)S(1)}, bf16[8,192,384]{2,1,0:T(8,128)(2,1)S(1)}) custom-call(s32[9]{0:T(128)S(1)} %pad_add_fusion.1.step_ref, bf16[2,1280,768]{2,1,0:T(8,128)(2,1)S(1)} %copy-done.4, bf16[2,1280,768]{2,1,0:T(8,128)(2,1)} %get-tuple-element.69.refs_1_, bf16[2,768,768]{2,1,0:T(8,128)(2,1)S(1)} %copy-done.13, ...), custom_call_target="tpu_custom_call" | custom-call | tf_op jit(solution)/shard_map/weight_gradient/pallas_call | solution.py:275
  422.2 12.2 %collective-permute-done.66.refs_7_ = bf16[192,384]{1,0:T(8,128)(2,1)S(1)} collective-permute-done((bf16[192,384]{1,0:T(8,128)(2,1)S(1)}, bf16[192,384]{1,0:T(8,128)(2,1)S(1)}, u32[]{:S(2)}, u32[]{:S(2)}) %collective-permute-start.66) | collective-permute-done | bytes 147488 | tf_op jit(solution)/shard_map/ppermute | solution.py:467
  (301 shorter events, 228.4 us)
Async XLA Ops:
  25.7 69.9 %collective-permute-start.8 = (bf16[1360,768]{1,0:T(8,128)(2,1)S(1)}, bf16[1360,768]{1,0:T(8,128)(2,1)}, u32[]{:S(2)}, u32[]{:S(2)}) collective-permute-start(bf16[1360,768]{1,0:T(8,128)(2,1)S(1)} %stacked.2), channel_id=1, source_target_pairs={{0,1},{1,0},{2,3},{3,2},{4,5},{5,4},{6,7},{7,6},{8,9},{9,8},{10,11... | collective-permute-start | bytes 6266888 | tf_op jit(solution)/shard_map/ppermute | solution.py:540
  36.2 30.5 %collective-permute-start.12 = (bf16[272,768]{1,0:T(8,128)(2,1)S(1)}, bf16[272,768]{1,0:T(8,128)(2,1)S(1)}, u32[]{:S(2)}, u32[]{:S(2)}) collective-permute-start(bf16[272,768]{1,0:T(8,128)(2,1)S(1)} %collective-permute-done.11.refs_2_), channel_id=1, source_target_pairs={{0,8},{8,16},{16,24},{24,28},{28,20},{20,12},{12,4},{4,0},{1,9},{9... | collective-permute-start | bytes 1253384 | tf_op jit(solution)/shard_map/ppermute | solution.py:39
  40.7 38.7 %collective-permute-start.6 = (bf16[384,768]{1,0:T(8,128)(2,1)}, bf16[384,768]{1,0:T(8,128)(2,1)}, u32[]{:S(2)}, u32[]{:S(2)}) collective-permute-start(bf16[384,768]{1,0:T(8,128)(2,1)} %get-tuple-element.109), channel_id=1, source_target_pairs={{0,24},{4,28},{8,16},{12,20},{16,8},{20,12},{24,0},{28,4},{1,25},{... | collective-permute-start | bytes 1769480 | tf_op jit(solution)/shard_map/ppermute | solution.py:506
  70.5 27.6 %collective-permute-start.14 = (bf16[816,768]{1,0:T(8,128)(2,1)S(1)}, bf16[816,768]{1,0:T(8,128)(2,1)}, u32[]{:S(2)}, u32[]{:S(2)}) collective-permute-start(bf16[816,768]{1,0:T(8,128)(2,1)S(1)} %stacked.3), channel_id=1, source_target_pairs={{0,1},{1,0},{2,3},{3,2},{4,5},{5,4},{6,7},{7,6},{8,9},{9,8},{10,11... | collective-permute-start | bytes 3760136 | tf_op jit(solution)/shard_map/ppermute | solution.py:540
  74.5 24.8 %collective-permute-start.17 = (bf16[4,384,384]{2,1,0:T(8,128)(2,1)}, bf16[4,384,384]{2,1,0:T(8,128)(2,1)}, u32[]{:S(2)}, u32[]{:S(2)}) collective-permute-start(bf16[4,384,384]{2,1,0:T(8,128)(2,1)} %dynamic-slice_bitcast_fusion), channel_id=1, source_target_pairs={{0,4},{4,0},{8,12},{12,8},{16,20},{20,16},{24,28},{28,24},{1,5},{5... | collective-permute-start | bytes 3538952 | tf_op jit(solution)/shard_map/ppermute | solution.py:509
  95.3 53.6 %collective-permute-start.9 = (bf16[1360,768]{1,0:T(8,128)(2,1)S(1)}, bf16[1360,768]{1,0:T(8,128)(2,1)}, u32[]{:S(2)}, u32[]{:S(2)}) collective-permute-start(bf16[1360,768]{1,0:T(8,128)(2,1)S(1)} %stacked.2), channel_id=1, source_target_pairs={{2,0},{0,2},{3,1},{1,3},{6,4},{4,6},{7,5},{5,7},{10,8},{8,10},{11,... | collective-permute-start | bytes 6266888 | tf_op jit(solution)/shard_map/ppermute | solution.py:44
  95.6 53.4 %collective-permute-start.10 = (bf16[1360,768]{1,0:T(8,128)(2,1)}, bf16[1360,768]{1,0:T(8,128)(2,1)}, u32[]{:S(2)}, u32[]{:S(2)}) collective-permute-start(bf16[1360,768]{1,0:T(8,128)(2,1)} %collective-permute-done.8), channel_id=1, source_target_pairs={{2,0},{0,2},{3,1},{1,3},{6,4},{4,6},{7,5},{5,7},{10,8},{8,10},{11,... | collective-permute-start | bytes 6266888 | tf_op jit(solution)/shard_map/ppermute | solution.py:44
  96.9 35.1 %collective-permute-start.15 = (bf16[816,768]{1,0:T(8,128)(2,1)S(1)}, bf16[816,768]{1,0:T(8,128)(2,1)}, u32[]{:S(2)}, u32[]{:S(2)}) collective-permute-start(bf16[816,768]{1,0:T(8,128)(2,1)S(1)} %stacked.3), channel_id=1, source_target_pairs={{2,0},{0,2},{3,1},{1,3},{6,4},{4,6},{7,5},{5,7},{10,8},{8,10},{11,... | collective-permute-start | bytes 3760136 | tf_op jit(solution)/shard_map/ppermute | solution.py:44
  98.1 34.2 %collective-permute-start.16 = (bf16[816,768]{1,0:T(8,128)(2,1)}, bf16[816,768]{1,0:T(8,128)(2,1)}, u32[]{:S(2)}, u32[]{:S(2)}) collective-permute-start(bf16[816,768]{1,0:T(8,128)(2,1)} %collective-permute-done.14), channel_id=1, source_target_pairs={{2,0},{0,2},{3,1},{1,3},{6,4},{4,6},{7,5},{5,7},{10,8},{8,10},{11,... | collective-permute-start | bytes 3760136 | tf_op jit(solution)/shard_map/ppermute | solution.py:44
  99.3 30.2 %collective-permute-start.7 = (bf16[4,384,384]{2,1,0:T(8,128)(2,1)}, bf16[4,384,384]{2,1,0:T(8,128)(2,1)}, u32[]{:S(2)}, u32[]{:S(2)}) collective-permute-start(bf16[4,384,384]{2,1,0:T(8,128)(2,1)} %pad_maximum_fusion), channel_id=1, source_target_pairs={{0,4},{4,0},{8,12},{12,8},{16,20},{20,16},{24,28},{28,24},{1,5},{5... | collective-permute-start | bytes 3538952 | tf_op jit(solution)/shard_map/ppermute | solution.py:509
  129.5 32.6 %collective-permute-start.18 = (bf16[2,384,384]{2,1,0:T(8,128)(2,1)}, bf16[2,384,384]{2,1,0:T(8,128)(2,1)}, u32[]{:S(2)}, u32[]{:S(2)}) collective-permute-start(bf16[2,384,384]{2,1,0:T(8,128)(2,1)} %get-tuple-element.57), channel_id=1, source_target_pairs={{0,8},{4,12},{8,0},{12,4},{16,24},{20,28},{24,16},{28,20},{1,9},{5... | collective-permute-start | bytes 1769480 | tf_op jit(solution)/shard_map/ppermute | solution.py:506
  132.0 39.7 %collective-permute-start.19 = (bf16[2,384,384]{2,1,0:T(8,128)(2,1)}, bf16[2,384,384]{2,1,0:T(8,128)(2,1)}, u32[]{:S(2)}, u32[]{:S(2)}) collective-permute-start(bf16[2,384,384]{2,1,0:T(8,128)(2,1)} %get-tuple-element.58), channel_id=1, source_target_pairs={{0,16},{4,20},{8,24},{12,28},{16,0},{20,4},{24,8},{28,12},{1,17},{... | collective-permute-start | bytes 1769480 | tf_op jit(solution)/shard_map/ppermute | solution.py:506
  132.3 52.5 %collective-permute-start.20 = (bf16[2,384,384]{2,1,0:T(8,128)(2,1)}, bf16[2,384,384]{2,1,0:T(8,128)(2,1)}, u32[]{:S(2)}, u32[]{:S(2)}) collective-permute-start(bf16[2,384,384]{2,1,0:T(8,128)(2,1)} %get-tuple-element.59), channel_id=1, source_target_pairs={{0,24},{4,28},{8,16},{12,20},{16,8},{20,12},{24,0},{28,4},{1,25},{... | collective-permute-start | bytes 1769480 | tf_op jit(solution)/shard_map/ppermute | solution.py:506
  198.8 27.8 %collective-permute-start.23 = (bf16[1280,1536]{1,0:T(8,128)(2,1)}, bf16[1280,1536]{1,0:T(8,128)(2,1)}, u32[]{:S(2)}, u32[]{:S(2)}) collective-permute-start(bf16[1280,1536]{1,0:T(8,128)(2,1)} %convolution_convert_fusion), channel_id=1, source_target_pairs={{2,0},{0,2},{3,1},{1,3},{6,4},{4,6},{7,5},{5,7},{10,8},{8,10},{11,... | collective-permute-start | bytes 11796488 | tf_op jit(solution)/shard_map/ppermute | solution.py:44
  205.6 38.9 %collective-permute-start.39 = (bf16[768,384]{1,0:T(8,128)(2,1)}, bf16[768,384]{1,0:T(8,128)(2,1)S(1)}, u32[]{:S(2)}, u32[]{:S(2)}) collective-permute-start(bf16[768,384]{1,0:T(8,128)(2,1)} %copy-done.10), channel_id=1, source_target_pairs={{1,0},{3,2},{5,4},{7,6},{9,8},{11,10},{13,12},{15,14},{17,16},{19,... | collective-permute-start | bytes 1769480 | tf_op jit(solution)/shard_map/ppermute | solution.py:473
  209.8 55.7 %collective-permute-start.38 = (bf16[1280,384]{1,0:T(8,128)(2,1)S(1)}, bf16[1280,384]{1,0:T(8,128)(2,1)S(1)}, u32[]{:S(2)}, u32[]{:S(2)}) collective-permute-start(bf16[1280,384]{1,0:T(8,128)(2,1)S(1)} %get-tuple-element.65), channel_id=1, source_target_pairs={{1,0},{3,2},{5,4},{7,6},{9,8},{11,10},{13,12},{15,14},{17,16},{19,... | collective-permute-start | bytes 2949128 | tf_op jit(solution)/shard_map/ppermute | solution.py:473
  244.4 18.8 %collective-permute-start.33 = (bf16[256,768]{1,0:T(8,128)(2,1)S(1)}, bf16[256,768]{1,0:T(8,128)(2,1)S(1)}, u32[]{:S(2)}, u32[]{:S(2)}) collective-permute-start(bf16[256,768]{1,0:T(8,128)(2,1)S(1)} %get-tuple-element.99), channel_id=1, source_target_pairs={{0,4},{8,0},{16,8},{24,16},{28,24},{20,28},{12,20},{4,12},{1,5},{9... | collective-permute-start | bytes 1179656 | tf_op jit(solution)/shard_map/ppermute | solution.py:39
  371.6 22.8 %collective-permute-start.60 = (bf16[192,384]{1,0:T(8,128)(2,1)S(1)}, bf16[192,384]{1,0:T(8,128)(2,1)S(1)}, u32[]{:S(2)}, u32[]{:S(2)}) collective-permute-start(bf16[192,384]{1,0:T(8,128)(2,1)S(1)} %get-tuple-element.119), channel_id=1, source_target_pairs={{0,20},{4,16},{8,28},{12,24},{16,4},{20,0},{24,12},{28,8},{1,21},{... | collective-permute-start | bytes 442376 | tf_op jit(solution)/shard_map/ppermute | solution.py:467
  402.6 19.6 %collective-permute-start.61 = (bf16[4,192,384]{2,1,0:T(8,128)(2,1)}, bf16[4,192,384]{2,1,0:T(8,128)(2,1)S(1)}, u32[]{:S(2)}, u32[]{:S(2)}) collective-permute-start(bf16[4,192,384]{2,1,0:T(8,128)(2,1)} %get-tuple-element.122), channel_id=1, source_target_pairs={{1,0},{3,2},{5,4},{7,6},{9,8},{11,10},{13,12},{15,14},{17,16},{19,... | collective-permute-start | bytes 1769480 | tf_op jit(solution)/shard_map/ppermute | solution.py:608
  412.2 22.3 %collective-permute-start.66 = (bf16[192,384]{1,0:T(8,128)(2,1)S(1)}, bf16[192,384]{1,0:T(8,128)(2,1)S(1)}, u32[]{:S(2)}, u32[]{:S(2)}) collective-permute-start(bf16[192,384]{1,0:T(8,128)(2,1)S(1)} %get-tuple-element.132), channel_id=1, source_target_pairs={{0,28},{4,24},{8,20},{12,16},{16,12},{20,8},{24,4},{28,0},{1,29},{... | collective-permute-start | bytes 442376 | tf_op jit(solution)/shard_map/ppermute | solution.py:467
  414.6 20.6 %collective-permute-start.73 = (bf16[192,384]{1,0:T(8,128)(2,1)S(1)}, bf16[192,384]{1,0:T(8,128)(2,1)S(1)}, u32[]{:S(2)}, u32[]{:S(2)}) collective-permute-start(bf16[192,384]{1,0:T(8,128)(2,1)S(1)} %copy-done.41), channel_id=1, source_target_pairs={{0,16},{4,20},{8,24},{12,28},{16,0},{20,4},{24,8},{28,12},{1,17},{... | collective-permute-start | bytes 442376 | tf_op jit(solution)/shard_map/ppermute | solution.py:467
  414.7 25.3 %collective-permute-start.74 = (bf16[192,384]{1,0:T(8,128)(2,1)S(1)}, bf16[192,384]{1,0:T(8,128)(2,1)S(1)}, u32[]{:S(2)}, u32[]{:S(2)}) collective-permute-start(bf16[192,384]{1,0:T(8,128)(2,1)S(1)} %get-tuple-element.113), channel_id=1, source_target_pairs={{0,24},{4,28},{8,16},{12,20},{16,8},{20,12},{24,0},{28,4},{1,25},{... | collective-permute-start | bytes 442376 | tf_op jit(solution)/shard_map/ppermute | solution.py:467
  416.2 25.2 %collective-permute-start.70 = (bf16[192,384]{1,0:T(8,128)(2,1)S(1)}, bf16[192,384]{1,0:T(8,128)(2,1)S(1)}, u32[]{:S(2)}, u32[]{:S(2)}) collective-permute-start(bf16[192,384]{1,0:T(8,128)(2,1)S(1)} %get-tuple-element.131), channel_id=1, source_target_pairs={{0,16},{4,20},{8,24},{12,28},{16,0},{20,4},{24,8},{28,12},{1,17},{... | collective-permute-start | bytes 442376 | tf_op jit(solution)/shard_map/ppermute | solution.py:467
  422.2 26.2 %collective-permute-start.71 = (bf16[192,384]{1,0:T(8,128)(2,1)S(1)}, bf16[192,384]{1,0:T(8,128)(2,1)S(1)}, u32[]{:S(2)}, u32[]{:S(2)}) collective-permute-start(bf16[192,384]{1,0:T(8,128)(2,1)S(1)} %get-tuple-element.130), channel_id=1, source_target_pairs={{0,20},{4,16},{8,28},{12,24},{16,4},{20,0},{24,12},{28,8},{1,21},{... | collective-permute-start | bytes 442376 | tf_op jit(solution)/shard_map/ppermute | solution.py:467
  (95 other events, 1051.8 us)

commit v3 on v2

--- a/solution.py
+++ b/solution.py
@@ -10,7 +10,7 @@
 DIGIT = 256
 
 
-NO_COST = pl.CostEstimate(flops=0, bytes_accessed=0, transcendentals=0)
+NO_COST = pl.CostEstimate(flops=1, bytes_accessed=1, transcendentals=0)
 
 
 def gelu_tanh(values):
@@ -113,18 +113,38 @@
     )(jnp.stack(scalars).astype(jnp.int32), *arrays)
 
 
+def by_columns(x, count):
+    rows, columns = x.shape
+    columns //= count
+
+    def kernel(x_ref, result_ref):
+        for k in range(count):
+            result_ref[k * rows : (k + 1) * rows, :] = x_ref[:, k * columns : (k + 1) * columns]
+
+    return pl.pallas_call(
+        kernel,
+        out_shape=jax.ShapeDtypeStruct((rows * count, columns), x.dtype),
+        in_specs=in_vmem(1),
+        out_specs=pl.BlockSpec(memory_space=pltpu.VMEM),
+        compiler_params=pltpu.CompilerParams(vmem_limit_bytes=16 << 20),
+        cost_estimate=NO_COST,
+        name="by_columns",
+    )(x)
+
+
 def stacked(pieces):
-    rows, columns = pieces[0].shape
+    columns = pieces[0].shape[1]
+    starts = [sum(piece.shape[0] for piece in pieces[:k]) for k in range(len(pieces) + 1)]
     if columns % LANES:
         return jnp.concatenate(pieces, axis=0)
 
     def kernel(*refs):
         for k, ref in enumerate(refs[:-1]):
-            refs[-1][k * rows : k * rows + rows, :] = ref[...]
-
-    return pl.pallas_call(
-        kernel,
-        out_shape=jax.ShapeDtypeStruct((rows * len(pieces), columns), pieces[0].dtype),
+            refs[-1][starts[k] : starts[k + 1], :] = ref[...]
+
+    return pl.pallas_call(
+        kernel,
+        out_shape=jax.ShapeDtypeStruct((starts[-1], columns), pieces[0].dtype),
         in_specs=in_vmem(len(pieces)),
         out_specs=pl.BlockSpec(memory_space=pltpu.VMEM),
         compiler_params=pltpu.CompilerParams(vmem_limit_bytes=16 << 20),
@@ -172,13 +192,12 @@
         inverse = lax.rsqrt(squares / features + 1e-06)
         pre = jnp.zeros((rows, units), jnp.float32)
         for place, ref in enumerate(taken):
-            where = slice(place * part, (place + 1) * part)
             scaled = (ref[0, :rows].astype(jnp.float32) - average) * inverse
             here = pl.ds(pl.multiple_of(place_ref[place], LANES), part)
             value = scaled * (1.0 + table_ref[0, 1:2, here]) + table_ref[0, 0:1, here]
             value = value.astype(jnp.bfloat16)
             (own_out, other_out)[place // halves][place % halves] = value
-            pre = pre + jnp.dot(value, up_ref[where, :], preferred_element_type=jnp.float32)
+            pre = pre + jnp.dot(value, up_ref[here, :], preferred_element_type=jnp.float32)
         pre_ref[...] = pre
         act_ref[...] = gelu_tanh(pre).astype(jnp.bfloat16)
 
@@ -198,7 +217,7 @@
         ),
         out_shape=[jax.ShapeDtypeStruct((halves, total_rows, part), jnp.bfloat16)] * 2
         + [jax.ShapeDtypeStruct((total_rows, units), kind) for kind in (jnp.float32, jnp.bfloat16)],
-        compiler_params=pltpu.CompilerParams(vmem_limit_bytes=40 << 20),
+        compiler_params=pltpu.CompilerParams(vmem_limit_bytes=24 << 20),
         cost_estimate=NO_COST,
         name="modulated_up",
     )(timesteps, places, table, up, *tokens)
@@ -228,91 +247,89 @@
         ],
         out_specs=pl.BlockSpec((rows, units), lambda i: (i, 0)),
         out_shape=jax.ShapeDtypeStruct((total_rows, units), jnp.bfloat16),
-        compiler_params=pltpu.CompilerParams(vmem_limit_bytes=32 << 20),
+        compiler_params=pltpu.CompilerParams(vmem_limit_bytes=16 << 20),
         cost_estimate=NO_COST,
         name="act_gradient",
     )(down, pre, own, other)
 
 
-def weight_gradient(lefts, rights, steps, block, one_side):
-    halves, _, part = lefts[0][0].shape
-    units = rights[0].shape[1]
+def weight_gradient(own, other, right, steps, block, one_side, added=None):
+    halves, _, part = own.shape
+    units = right.shape[1]
     each = part // block
     count = halves * each
     half = block // 2
-    groups = len(lefts)
+    kept = half if one_side else block
     skipped = half // LANES * LANES
+    given = [own, other, right] + list(added or [])
+    results, rows_out = (1, half) if one_side else (2, half)
 
     def kernel(step_ref, *refs):
-        left_refs, right_refs, outs = refs[: 2 * groups], refs[2 * groups : 3 * groups], refs[3 * groups :]
-
-        def found(which, begin, end):
-            return sum(
-                over_tokens(left_refs[2 * g + which][0, :, begin:end], right_refs[g][...]) for g in range(groups)
-            ).astype(jnp.bfloat16)
+        ins, outs = refs[: len(given)], refs[len(given) :]
+
+        def keep(which, value):
+            if added is None:
+                outs[which][0] = value
+                return
+            value = (value + ins[3 + which][0]).astype(jnp.bfloat16)
+            step = step_ref[which * count + pl.program_id(0)]
+            for k, out in enumerate(outs):
+                out[step] = value[k * rows_out : (k + 1) * rows_out]
 
         for which in range(2):
-            step = step_ref[which * count + pl.program_id(0)]
             if not one_side:
-                value = found(which, 0, block)
-                outs[0][step] = value[:half]
-                outs[1][step] = value[half:]
+                keep(which, over_tokens(ins[which][0], ins[2][...]))
                 continue
 
             @pl.when(step_ref[2 * count] == 0)
             def _():
-                outs[0][step] = found(which, 0, block - skipped)[:half]
+                keep(which, over_tokens(ins[which][0, :, : block - skipped], ins[2][...])[:half])
 
             @pl.when(step_ref[2 * count] == 1)
             def _():
-                outs[0][step] = found(which, skipped, block)[half - skipped :]
-
-    left_specs = [
-        pl.BlockSpec((1, x.shape[1], block), lambda i, step_ref: (i // each, 0, i % each)) for pair in lefts for x in pair
-    ]
-    right_specs = [pl.BlockSpec(x.shape, lambda i, step_ref: (0, 0)) for x in rights]
-    results = 1 if one_side else 2
+                keep(which, over_tokens(ins[which][0, :, skipped:], ins[2][...])[half - skipped :])
+
+    block_of = pl.BlockSpec((1, kept, units), lambda i, step_ref: (i, 0, 0))
+    in_specs = [pl.BlockSpec((1, own.shape[1], block), lambda i, step_ref: (i // each, 0, i % each))] * 2
+    in_specs += [pl.BlockSpec(right.shape, lambda i, step_ref: (0, 0))] + [block_of] * (len(given) - 3)
+    if added is None:
+        out_specs, out_shape = [block_of] * 2, [jax.ShapeDtypeStruct((count, kept, units), jnp.float32)] * 2
+    else:
+        out_specs = [pl.BlockSpec((2 * count, rows_out, units), lambda i, step_ref: (0, 0, 0))] * results
+        out_shape = [jax.ShapeDtypeStruct((2 * count, rows_out, units), jnp.bfloat16)] * results
     return pl.pallas_call(
         kernel,
         grid_spec=pltpu.PrefetchScalarGridSpec(
-            num_scalar_prefetch=1,
-            grid=(count,),
-            in_specs=left_specs + right_specs,
-            out_specs=[pl.BlockSpec((2 * count, half, units), lambda i, step_ref: (0, 0, 0))] * results,
+            num_scalar_prefetch=1, grid=(count,), in_specs=in_specs, out_specs=out_specs
         ),
-        out_shape=[jax.ShapeDtypeStruct((2 * count, half, units), jnp.bfloat16)] * results,
-        compiler_params=pltpu.CompilerParams(vmem_limit_bytes=40 << 20),
+        out_shape=out_shape,
+        compiler_params=pltpu.CompilerParams(vmem_limit_bytes=20 << 20),
         cost_estimate=NO_COST,
         name="weight_gradient",
-    )(steps, *[x for pair in lefts for x in pair], *rights)
+    )(steps, *given)
 
 
 def after(x, *others):
     return lax.optimization_barrier((x, others))[0]
 
 
-def received(offsets, arrivals, width):
-    rows, share = arrivals[0].shape
-    if share % LANES:
-        result = jnp.zeros((rows, width), jnp.float32)
-        for k, piece in enumerate(arrivals):
-            result = lax.dynamic_update_slice_in_dim(result, piece.astype(jnp.float32), offsets[k], 1)
-        return result
-
-    def kernel(offset_ref, *refs):
-        for k, ref in enumerate(refs[:-1]):
-            where = pl.ds(pl.multiple_of(offset_ref[k], share), share)
-            refs[-1][:, where] = ref[...].astype(jnp.float32)
-
-    return pl.pallas_call(
-        kernel,
-        out_shape=jax.ShapeDtypeStruct((rows, width), jnp.float32),
-        in_specs=[pl.BlockSpec(memory_space=pltpu.SMEM)] + in_vmem(len(arrivals)),
+def received(arrivals):
+    pieces, rows, share = arrivals[0].shape
+
+    def kernel(*refs):
+        for h, ref in enumerate(refs[:-1]):
+            for k in range(pieces):
+                refs[-1][h * rows : (h + 1) * rows, k * share : (k + 1) * share] = ref[k].astype(jnp.float32)
+
+    return pl.pallas_call(
+        kernel,
+        out_shape=jax.ShapeDtypeStruct((rows * len(arrivals), pieces * share), jnp.float32),
+        in_specs=in_vmem(len(arrivals)),
         out_specs=pl.BlockSpec(memory_space=pltpu.VMEM),
         compiler_params=pltpu.CompilerParams(vmem_limit_bytes=16 << 20),
         cost_estimate=NO_COST,
         name="received",
-    )(jnp.stack(offsets).astype(jnp.int32), *arrivals)
+    )(*arrivals)
 
 
 def partner(index, step, count):
@@ -427,7 +444,10 @@
         arrivals = [
             sent(k, lax.dynamic_slice_in_dim(own, feature_offsets[k] // sides, taken, 0)) for k in range(count)
         ]
-        return received([peer * share for peer in peers], arrivals, hidden)
+        result = jnp.zeros((taken, hidden), jnp.float32)
+        for peer, piece in zip(peers, arrivals):
+            result = lax.dynamic_update_slice_in_dim(result, piece.astype(jnp.float32), peer * share, 1)
+        return result
 
     down_found = over_all_tokens(all_grads, student_act).reshape(count, sides, taken, share)
     down_share = delivered(lax.dynamic_index_in_dim(down_found, side, 1, keepdims=False))
@@ -479,99 +499,98 @@
     student_gate = of_student(gate)
 
     farthest = count // 2
-    near_images = [r for r in range(count) if min(r, count - r) <= farthest - 2]
+    near_images = [0] + [r for hop in range(1, farthest - 1) for r in (hop, count - hop)]
     far_images = [farthest, farthest - 1, farthest + 1]
-    steps = jnp.zeros((count,), jnp.int32).at[jnp.stack(feature_offsets) // block].set(jnp.arange(count, dtype=jnp.int32))
+    steps = jnp.stack([part_places[p] // block + b for p in range(4) for b in range(part // block)])
     steps = jnp.concatenate([steps, side[None].astype(jnp.int32)])
 
     token_halves = halves(tokens)
     column = lax.broadcasted_iota(jnp.int32, (TILE_ROWS, part), 1)
     digits = jnp.where(column == 0, timesteps[0] % DIGIT, jnp.where(column == 1, timesteps[0] // DIGIT, 0))
-    there = back = jnp.concatenate([token_halves[0], digits.astype(jnp.bfloat16)], axis=0)
+    digits = digits.astype(jnp.bfloat16)
+    there = back = jnp.concatenate([token_halves[0], digits], axis=0)
     round_ring = [there] + [None] * (count - 1)
-    far, near = list(range(count - 1, farthest - 1, -1)), list(range(farthest - 1, 0, -1))
+    crossed = [jnp.concatenate([token_halves[1], digits], axis=0)]
+    table = jnp.pad(mod_table[0], ((0, 0), (0, -mod_table.shape[2] % 8), (0, 0)))
+
+    def cross_over(images):
+        return lax.ppermute(stacked([round_ring[r] for r in images]), "side", swap)
+
     arrived = []
     for hop in range(1, farthest + 1):
+        if hop == 2:
+            there = after(there, table)
+        if hop == farthest:
+            there = after(there, crossed[1])
         there = ring_shift(there, 1)
         round_ring[-hop % count] = there
         if hop <= (count - 1) // 2:
             back = ring_shift(back, -1)
             round_ring[hop] = back
         arrived.append([there, back])
-
-    columns, column, row = count // 2, me // 2, me % 2
-
-    def over_columns(step, piece):
-        pairs = [(i, 2 * partner(i // 2, step, columns) + i % 2) for i in range(count)]
-        return lax.ppermute(piece, "dp", pairs) if step else piece
-
-    def over_rows(piece):
-        return lax.ppermute(piece, "dp", [(i, i ^ 1) for i in range(count)])
-
-    column_peers = [partner(column, step, columns) for step in range(columns)]
-    steps_out = list(range(columns - 1, -1, -1))
-    up_pairs = [None] * columns
-    for step in steps_out:
-        piece = lax.dynamic_slice_in_dim(up_weight[0], column_peers[step] * 2 * share, 2 * share, 1)
-        up_pairs[step] = over_columns(step, piece)
-    up_passed = over_rows(jnp.stack([lax.dynamic_slice_in_dim(x, (1 - row) * share, share, 1) for x in up_pairs]))
-    by_row = down_weight[0].reshape(columns, 2, share, block)
-    down_kept = lax.dynamic_index_in_dim(by_row, row, 1, keepdims=False)
-    down_passed = over_rows(lax.dynamic_index_in_dim(by_row, 1 - row, 1, keepdims=False))
-    down_pairs = [None] * columns
-    for step in steps_out:
-        piece = jnp.stack(
-            [lax.dynamic_index_in_dim(x, column_peers[step], 0, keepdims=False) for x in (down_kept, down_passed)]
-        )
-        down_pairs[step] = over_columns(step, after(piece, *up_pairs[1:]))
-
-    def up_piece(k):
-        if k % 2:
-            return lambda refs, scalar_ref: refs[columns].at[k // 2]
-        return lambda refs, scalar_ref: refs[k // 2].at[
-            :, pl.ds(pl.multiple_of(scalar_ref[count] * share, share), share)
-        ]
-
-    def down_piece(k):
-        return lambda refs, scalar_ref: refs[k // 2].at[k % 2]
-
-    def all_features(images):
+        if hop <= farthest - 2:
+            crossed.append(cross_over([hop, count - hop]))
+    far_crossed = cross_over(far_images)
+
+    def exchanged(x):
+        return lax.all_to_all(x, "dp", split_axis=0, concat_axis=0, tiled=True)
+
+    up = exchanged(after(by_columns(up_weight[0], count), *arrived[-1]))
+    down_blocks = exchanged(after(down_weight[0], up, crossed, far_crossed))
+
+    def all_features(images, crossed):
         first = stacked([round_ring[r] for r in images])
-        crossed = after(lax.ppermute(first, "side", swap), *up_pairs[1:])
+        steps_taken = first.reshape(len(images), rows + TILE_ROWS, part)[:, rows, :2].astype(jnp.int32)
         pair = [first, crossed]
-        steps_taken = first.reshape(len(images), rows + TILE_ROWS, part)[:, rows, :2].astype(jnp.int32)
         shaped = [x.reshape(len(images), rows + TILE_ROWS, part) for x in pair + [from_core(x, 1) for x in pair]]
         return shaped, steps_taken[:, 0] + DIGIT * steps_taken[:, 1]
 
-    near_tokens, near_steps = all_features(near_images)
-    far_tokens, far_steps = all_features(far_images)
-    scalars = feature_offsets + [row]
-    up = placed(0, scalars, up_pairs + [up_passed], [up_piece(k) for k in range(count)], (features, share))
-    table = mod_table[0]
+    near_tokens, near_steps = all_features(near_images, stacked(crossed))
+    far_tokens, far_steps = all_features(far_images, far_crossed)
     *far_normed, far_pre, far_act = modulated_up(far_tokens, rows, far_steps, part_places, table, up)
-    near_tokens = after(near_tokens, far_act)
     *near_normed, near_pre, near_act = modulated_up(near_tokens, rows, near_steps, part_places, table, up)
-    down_pairs = after(down_pairs, near_act)
-    down = placed(1, scalars, down_pairs, [down_piece(k) for k in range(count)], (share, features))
-
-    student_acts = [of_student(near_act), of_student(far_act)]
+
+    def down_piece(k):
+        return lambda refs, scalar_ref: refs[0].at[k * share : (k + 1) * share, :]
+
+    offsets = [feature_offset(i) for i in range(count)]
+    down = placed(1, offsets, [after(down_blocks, near_act, far_act)], [down_piece(k) for k in range(count)], (share, features))
+
     valid_col = (jnp.arange(rows, dtype=jnp.int32) < valid_counts[me]).astype(jnp.float32)[:, None]
     valid_total = jnp.sum(valid_counts).astype(jnp.float32)
-    terms = [[None] * count, [None] * count]
-    earlier = []
-    groups = [(far_images[:1], far_act[:rows]), (far_images[1:], far_act[rows:]), (near_images, near_act)]
-    earlier = []
-    for images, act in groups:
-        act = after(act, *earlier)
-        from_other = from_core(product(act, down[:, width:]).astype(jnp.bfloat16), 1)
-        earlier = [from_other]
+    shares = {}
+
+    def other_share(images, act):
+        found = from_core(product(act, down[:, width:]).astype(jnp.bfloat16), 1)
+        for k, r in enumerate(images):
+            here = slice(k * rows, (k + 1) * rows)
+            shares[r] = (act[here], found[here])
+        return found
+
+    def term(r, c):
+        act, found = shares[r % count]
+        here = slice(c * part, (c + 1) * part)
+        return product(act, down[:, here]) + found[:, here].astype(jnp.float32)
+
+    ways = (1, -1)
+    far_share = other_share(far_images[:1], far_act[:rows])
+    there = [ring_shift(term(farthest, c).astype(jnp.bfloat16), ways[c]) for c in range(2)]
+    middle_share = other_share(far_images[1:], after(far_act[rows:], far_share))
+    student_act = of_student(jnp.concatenate([near_act, far_act], axis=0))
+    back = [None, None]
+    other_share(near_images, after(near_act, middle_share))
+    for hop in range(farthest - 1, 0, -1):
+        if hop < farthest - 1:
+            there = after(there, back)
         for c in range(2):
-            here = slice(c * part, (c + 1) * part)
-            term = product(act, down[:, here]) + from_other[:, here].astype(jnp.float32)
-            for k, r in enumerate(images):
-                terms[c][r] = term[k * rows : (k + 1) * rows]
-    mixed = [ring_scatter(terms[c], 1 if c == 0 else -1) for c in range(2)]
-    mixed, student_acts, student_gate = lax.optimization_barrier((mixed, student_acts, student_gate))
+            there[c] = term(ways[c] * hop, c) + there[c].astype(jnp.float32)
+            there[c] = ring_shift(there[c].astype(jnp.bfloat16), ways[c])
+            value = term(-ways[c] * hop, c)
+            value = value if back[c] is None else value + back[c].astype(jnp.float32)
+            back[c] = ring_shift(value.astype(jnp.bfloat16), -ways[c])
+    mixed = [term(0, c) + there[c].astype(jnp.float32) + back[c].astype(jnp.float32) for c in range(2)]
+    mixed, student_act = lax.optimization_barrier((mixed, student_act))
+    student_acts = [student_act[: len(near_images) * rows], student_act[len(near_images) * rows :]]
     student_gates = halves(student_gate)
     outs = [(token_halves[c].astype(jnp.float32) + gates[c] * mixed[c]).astype(jnp.bfloat16) for c in range(2)]
     found = []
@@ -583,10 +602,12 @@
 
     there, back = [found[c][0] for c in range(2)], [found[c][0] for c in range(2)]
     for hop in range(1, farthest + 1):
+        if hop == 2:
+            there = after(there, student_acts)
         if hop == farthest:
             near_own = stacked_parts([[found[c][r] for r in near_images] for c in range(2)])
             near_grads = [near_own, from_core(near_own, 1)]
-            there = after(there, *near_grads)
+            there = after(there, near_grads)
         for c, way in ((0, 1), (1, -1)):
             there[c] = ring_shift(there[c], way)
             found[c][(-way * hop) % count] = there[c]
@@ -595,26 +616,25 @@
                 found[c][(way * hop) % count] = back[c]
     near_grad_pre = act_gradient(*near_grads, down, near_pre, rows)
     far_found = [[found[c][r] for r in far_images] for c in range(2)]
-    far_own = stacked_parts(after(far_found, *there, near_grad_pre))
+    near_up = weight_gradient(*near_normed, near_grad_pre, steps, block, False)
+    far_own = stacked_parts(after(far_found, *there, near_up))
     far_grads = [far_own, from_core(far_own, 1)]
-
-    (down_found,) = weight_gradient([near_grads, far_grads], student_acts, steps, block, True)
-    down_arrived = [sent(k, down_found[k]) for k in range(count)]
+    near_down = weight_gradient(*after(near_grads, far_own), student_acts[0], steps, block, True)
+
+    def delivered(found):
+        return exchanged(found.reshape(-1, share)).reshape(found.shape)
+
+    (down_found,) = weight_gradient(*far_grads, student_acts[1], steps, block, True, near_down)
+    down_arrived = delivered(down_found)
     far_grad_pre = act_gradient(*after(far_grads, down_found), down, far_pre, rows)
-    far_grad_pre = after(far_grad_pre, down_arrived[far[0]])
-    up_found = weight_gradient([near_normed, far_normed], [near_grad_pre, far_grad_pre], steps, block, False)
-    handed = after(up_found[0], down_arrived[far[2]])
-    split = count // 2
-    handed = [lax.ppermute(x, "side", [(1, 0)]) for x in (handed[split:], handed[:split])]
-    first = jnp.where(is_student, up_found[1][split:], after(handed[0], *[down_arrived[k] for k in near]))
-    up_arrived = [None] * split + [sent(k, first[k - split]) for k in range(split, count)]
-    second = jnp.where(is_student, up_found[1][:split], after(handed[1], up_arrived[far[0]]))
-    up_arrived[:split] = [sent(k, second[k]) for k in range(split)]
-    places = [peer * share for peer in peers]
+    up_found = weight_gradient(*far_normed, far_grad_pre, steps, block, False, near_up)
+    handed = lax.ppermute(up_found[0], "side", [(1, 0)])
+    up_arrived = [delivered(jnp.where(is_student, up_found[1], handed))]
+    up_share, down_share = received(up_arrived), received([down_arrived])
     out = jnp.concatenate(
         [jnp.where(side == 0, outs[0], outs[1]), jnp.where(side == 0, outs[1], outs[0])], axis=1
     )
-    return (out[None], received(places, up_arrived, hidden), received(places, down_arrived, hidden).T)
+    return (out[None], up_share, down_share.T)
 
 
 def solution(mesh):

time: 458 us -> 436 us (0.952)
  waiting for transfers between devices: 228 us -> 198 us
  local copies, waits for them, and re-layouts: 38.8 us -> 56.3 us
  starting transfers between devices: 86.8 us -> 74.4 us
    ppermute x35, waiting for transfers between devices: 123 us -> 81 us  [ring_shift(): lax.ppermute(x, 'dp', [(order[p], order[(p + by) % count]) for p in range...]
    ppermute x26 -> x4, starting transfers between devices: 40.6 us -> 6.42 us  [the longest x1 3.73 us: paired_shards(): handed = lax.ppermute(up_found[0], 'side', [(1, 0)])]
    unnamed x89 -> x134, local copies, waits for them, and re-layouts: 16 us -> 46.5 us
    all_to_all x0 -> x4, waiting for transfers between devices: none -> 24.6 us  [exchanged(): return lax.all_to_all(x, 'dp', split_axis=0, concat_axis=0, tiled=True)]
    all_to_all x0 -> x4, starting transfers between devices: none -> 22.6 us  [exchanged(): return lax.all_to_all(x, 'dp', split_axis=0, concat_axis=0, tiled=True)]
    ppermute x26 -> x4, waiting for transfers between devices: 85 us -> 72.6 us  [the longest x3 48.5 us: cross_over(): return lax.ppermute(stacked([round_ring[r] for r in images]), 'side', swap)]
    dynamic_slice x4 -> x0, local copies, waits for them, and re-layouts: 7.99 us -> none  [the longest x2 3.74 us: paired_shards(): lax.dynamic_index_in_dim(x, column_peers[step], 0, keepdims=False)]
    ppermute x3 -> x2, starting transfers between devices: 9.88 us -> 5.15 us  [of_student(): return jnp.where(is_student, x, lax.ppermute(x, 'side', [(1, 0)]))]
  transfers between devices with their start and end apart: 75 -> 56, of which waited for: 48 -> 31; matrix products, arithmetic and copies ran while one was open for 10% -> 8% of each run, Pallas kernels for 10% -> 12%
where the time goes in v3:
time: 436 us; the launch traced here: 429 us
  waiting for transfers between devices  198 us (45%)
  starting transfers between devices  74.4 us (17%)
  Pallas kernels  66 us (15%)
  local copies, waits for them, and re-layouts  56.3 us (13%)
  matrix products  20.3 us (5%)
  other arithmetic  10.6 us (2%)
    ppermute x35, waiting for transfers between devices, ring_shift(): lax.ppermute(x, 'dp', [(order[p], order[(p + by) % count]) for p in range...  81 us
    ppermute x3, waiting for transfers between devices, cross_over(): return lax.ppermute(stacked([round_ring[r] for r in images]), 'side', swap)  48.5 us
    unnamed x134, local copies, waits for them, and re-layouts  46.5 us
    ppermute x35, starting transfers between devices, ring_shift(): lax.ppermute(x, 'dp', [(order[p], order[(p + by) % count]) for p in range...  38.5 us
    all_to_all x4, waiting for transfers between devices, exchanged(): return lax.all_to_all(x, 'dp', split_axis=0, concat_axis=0, tiled=True)  24.6 us
    ppermute x1, waiting for transfers between devices, paired_shards(): handed = lax.ppermute(up_found[0], 'side', [(1, 0)])  24.1 us
    all_to_all x4, starting transfers between devices, exchanged(): return lax.all_to_all(x, 'dp', split_axis=0, concat_axis=0, tiled=True)  22.6 us
    pallas_call x4, Pallas kernels, weight_gradient(): pl.pallas_call(kernel, grid_spec=pltpu.PrefetchScalarGridSpec(num_scalar_...  22.1 us
  transfers between devices with their start and end apart: 56, of which 31 were waited for; matrix products, arithmetic and copies ran while one was open for 8% of the time, Pallas kernels for 12%

profile of v3, /device:TPU:10, one launch (start us, length us, event | category | flops | bytes accessed | tf_op | source)
XLA Modules:
  0.0 428.6 jit_solution(17455309263798676934)
XLA Ops:
  10.0 5.1 %collective-permute-done.1.refs_2_.refs_1_ = bf16[272,768]{1,0:T(8,128)(2,1)S(1)} collective-permute-done((bf16[272,768]{1,0:T(8,128)(2,1)S(1)}, bf16[272,768]{1,0:T(8,128)(2,1)S(1)}, u32[]{:S(2)}, u32[]{:S(2)}) %collective-permute-start.1) | collective-permute-done | bytes 417824 | tf_op jit(solution)/shard_map/ppermute | solution.py:39
  19.0 7.9 %collective-permute-done.3.refs_4_.refs_1_ = bf16[272,768]{1,0:T(8,128)(2,1)S(1)} collective-permute-done((bf16[272,768]{1,0:T(8,128)(2,1)S(1)}, bf16[272,768]{1,0:T(8,128)(2,1)S(1)}, u32[]{:S(2)}, u32[]{:S(2)}) %collective-permute-start.3) | collective-permute-done | bytes 417824 | tf_op jit(solution)/shard_map/ppermute | solution.py:39
  29.0 6.7 %collective-permute-done.5.refs_1_ = bf16[544,768]{1,0:T(8,128)(2,1)S(1)} collective-permute-done((bf16[544,768]{1,0:T(8,128)(2,1)S(1)}, bf16[544,768]{1,0:T(8,128)(2,1)S(1)}, u32[]{:S(2)}, u32[]{:S(2)}) %collective-permute-start.5) | collective-permute-done | bytes 835616 | tf_op jit(solution)/shard_map/ppermute | solution.py:517
  39.2 6.6 %collective-permute-done.6.refs_0_ = bf16[272,768]{1,0:T(8,128)(2,1)S(1)} collective-permute-done((bf16[272,768]{1,0:T(8,128)(2,1)S(1)}, bf16[272,768]{1,0:T(8,128)(2,1)S(1)}, u32[]{:S(2)}, u32[]{:S(2)}) %collective-permute-start.6) | collective-permute-done | bytes 417824 | tf_op jit(solution)/shard_map/ppermute | solution.py:39
  46.5 5.5 %all-to-all-start = ((bf16[8,384,384]{2,1,0:T(8,128)(2,1)}), bf16[8,384,384]{2,1,0:T(8,128)(2,1)S(1)}, u32[]{:S(2)}, u32[]{:S(2)}) async-start(bf16[8,384,384]{2,1,0:T(8,128)(2,1)} %bitcast.61), calls=%async_computation | async-start | bytes 4718592 | tf_op jit(solution)/shard_map/all_to_all | solution.py:536
  58.3 41.8 %collective-permute-done.8.refs_2_ = bf16[544,768]{1,0:T(8,128)(2,1)S(1)} collective-permute-done((bf16[544,768]{1,0:T(8,128)(2,1)S(1)}, bf16[544,768]{1,0:T(8,128)(2,1)S(1)}, u32[]{:S(2)}, u32[]{:S(2)}) %collective-permute-start.8) | collective-permute-done | bytes 835616 | tf_op jit(solution)/shard_map/ppermute | solution.py:517
  101.0 6.5 %all-to-all-start.1 = ((bf16[8,384,384]{2,1,0:T(8,128)(2,1)}), bf16[8,384,384]{2,1,0:T(8,128)(2,1)}, u32[]{:S(2)}, u32[]{:S(2)}) async-start(bf16[8,384,384]{2,1,0:T(8,128)(2,1)} %bitcast.64), calls=%async_computation.1 | async-start | bytes 4718592 | tf_op jit(solution)/shard_map/all_to_all | solution.py:536
  122.8 12.4 %modulated_up.2 = (bf16[2,1280,768]{2,1,0:T(8,128)(2,1)S(1)}, bf16[2,1280,768]{2,1,0:T(8,128)(2,1)S(1)}, f32[1280,384]{1,0:T(8,128)S(1)}, bf16[1280,384]{1,0:T(8,128)(2,1)S(1)}) custom-call(s32[5]{0:T(128)S(1)} %add_bitcast_fusion.1.step_ref, s32[4]{0:T(128)S(1)} %pad_add_fusion.place_ref, f32[50,8,3072]{2,1,0:T(8,128)S(1)} %copy-done, ...), custom_call_target="tpu_custom_call" | custom-call | flops 1 | bytes 1 | tf_op jit(solution)/shard_map/modulated_up/pallas_call | solution.py:206
  141.5 8.0 %modulated_up.3 = (bf16[2,768,768]{2,1,0:T(8,128)(2,1)S(1)}, bf16[2,768,768]{2,1,0:T(8,128)(2,1)S(1)}, f32[768,384]{1,0:T(8,128)S(1)}, bf16[768,384]{1,0:T(8,128)(2,1)S(1)}) custom-call(s32[3]{0:T(128)S(1)} %add_bitcast_fusion.step_ref, s32[4]{0:T(128)S(1)} %pad_add_fusion.place_ref, f32[50,8,3072]{2,1,0:T(8,128)S(1)} %bitcast.58, ...), custom_call_target="tpu_custom_call" | custom-call | flops 1 | bytes 1 | tf_op jit(solution)/shard_map/modulated_up/pallas_call | solution.py:206
  175.3 7.0 %collective-permute-done.19 = bf16[256,768]{1,0:T(8,128)(2,1)S(1)} collective-permute-done((bf16[256,768]{1,0:T(8,128)(2,1)S(1)}, bf16[256,768]{1,0:T(8,128)(2,1)S(1)}, u32[]{:S(2)}, u32[]{:S(2)}) %collective-permute-start.19) | collective-permute-done | bytes 393248 | tf_op jit(solution)/shard_map/ppermute | solution.py:39
  248.9 5.9 %collective-permute-done.35 = bf16[256,768]{1,0:T(8,128)(2,1)S(1)} collective-permute-done((bf16[256,768]{1,0:T(8,128)(2,1)S(1)}, bf16[256,768]{1,0:T(8,128)(2,1)S(1)}, u32[]{:S(2)}, u32[]{:S(2)}) %collective-permute-start.35) | collective-permute-done | bytes 393248 | tf_op jit(solution)/shard_map/ppermute | solution.py:598
  258.6 5.5 %collective-permute-done.33 = bf16[256,768]{1,0:T(8,128)(2,1)S(1)} collective-permute-done((bf16[256,768]{1,0:T(8,128)(2,1)S(1)}, bf16[256,768]{1,0:T(8,128)(2,1)S(1)}, u32[]{:S(2)}, u32[]{:S(2)}) %collective-permute-start.33) | collective-permute-done | bytes 393248 | tf_op jit(solution)/shard_map/ppermute | solution.py:598
  270.2 8.4 %collective-permute-done.34.refs_2_ = bf16[256,768]{1,0:T(8,128)(2,1)S(1)} collective-permute-done((bf16[256,768]{1,0:T(8,128)(2,1)S(1)}, bf16[256,768]{1,0:T(8,128)(2,1)S(1)}, u32[]{:S(2)}, u32[]{:S(2)}) %collective-permute-start.34) | collective-permute-done | bytes 393248 | tf_op jit(solution)/shard_map/ppermute | solution.py:39
  282.1 4.7 %collective-permute-done.44.refs_9_ = bf16[256,768]{1,0:T(8,128)(2,1)} collective-permute-done((bf16[256,768]{1,0:T(8,128)(2,1)S(1)}, bf16[256,768]{1,0:T(8,128)(2,1)}, u32[]{:S(2)}, u32[]{:S(2)}) %collective-permute-start.44) | collective-permute-done | bytes 393248 | tf_op jit(solution)/shard_map/ppermute | solution.py:39
  298.3 8.0 %collective-permute-done.38.refs_2_ = bf16[256,768]{1,0:T(8,128)(2,1)} collective-permute-done((bf16[256,768]{1,0:T(8,128)(2,1)S(1)}, bf16[256,768]{1,0:T(8,128)(2,1)}, u32[]{:S(2)}, u32[]{:S(2)}) %collective-permute-start.38) | collective-permute-done | bytes 393248 | tf_op jit(solution)/shard_map/ppermute | solution.py:39
  317.8 6.2 %act_gradient.2.refs_2_ = bf16[1280,384]{1,0:T(8,128)(2,1)S(1)} custom-call(bf16[384,3072]{1,0:T(8,128)(2,1)S(1)} %placed.1.down_ref, f32[1280,384]{1,0:T(8,128)S(1)} %copy-done.27, bf16[2,1280,768]{2,1,0:T(8,128)(2,1)S(1)} %copy-done.2, bf16[2,1280,768]{2,1,0:T(8,128)(2,1)S(1)} %copy-done.7), custom_call_target="tpu_custom_call" | custom-call | flops 1 | bytes 1 | tf_op jit(solution)/shard_map/act_gradient/pallas_call | solution.py:239
  324.0 6.4 %weight_gradient.4 = (f32[4,384,384]{2,1,0:T(8,128)S(1)}, f32[4,384,384]{2,1,0:T(8,128)S(1)}) custom-call(s32[9]{0:T(128)S(1)} %concatenate.19.step_ref, bf16[2,1280,768]{2,1,0:T(8,128)(2,1)S(1)} %copy-done.13, bf16[2,1280,768]{2,1,0:T(8,128)(2,1)S(1)} %copy-done.15, bf16[1280,384]{1,0:T(8,128)(2,1)S(1)} %act_gradient.2.refs_2_), custom_call_target="tpu_custom_call" | custom-call | flops 1 | bytes 1 | tf_op jit(solution)/shard_map/weight_gradient/pallas_call | solution.py:300
  335.7 5.8 %weight_gradient.5 = (f32[4,192,384]{2,1,0:T(8,128)S(1)}, f32[4,192,384]{2,1,0:T(8,128)S(1)}) custom-call(s32[9]{0:T(128)S(1)} %concatenate.19.step_ref, bf16[2,1280,768]{2,1,0:T(8,128)(2,1)S(1)} %copy-done.3, bf16[2,1280,768]{2,1,0:T(8,128)(2,1)S(1)} %copy-done.8, bf16[1280,384]{1,0:T(8,128)(2,1)S(1)} %slice.179.refs_2_), custom_call_target="tpu_custom_call" | custom-call | flops 1 | bytes 1 | tf_op jit(solution)/shard_map/weight_gradient/pallas_call | solution.py:300
  341.6 5.5 %weight_gradient.6 = bf16[8,192,384]{2,1,0:T(8,128)(2,1)} custom-call(s32[9]{0:T(128)S(1)} %concatenate.19.step_ref, bf16[2,768,768]{2,1,0:T(8,128)(2,1)S(1)} %stacked_parts.3.refs_0_.own_ref, bf16[2,768,768]{2,1,0:T(8,128)(2,1)S(1)} %collective-permute-done.50.refs_1_.other_ref, bf16[768,384]{1,0:T(8,128)(2,1)S(1)} %copy-done.16, ...), custom_call_target="tpu_custom_call" | custom-call | flops 1 | bytes 1 | tf_op jit(solution)/shard_map/weight_gradient/pallas_call | solution.py:300
  348.4 4.7 %all-to-all-start.3 = ((bf16[8,192,384]{2,1,0:T(8,128)(2,1)}), bf16[8,192,384]{2,1,0:T(8,128)(2,1)S(1)}, u32[]{:S(2)}, u32[]{:S(2)}) async-start(bf16[8,192,384]{2,1,0:T(8,128)(2,1)} %weight_gradient.6), calls=%async_computation.3 | async-start | bytes 2359296 | tf_op jit(solution)/shard_map/all_to_all | solution.py:536
  363.1 4.4 %weight_gradient.7 = (bf16[8,192,384]{2,1,0:T(8,128)(2,1)S(1)}, bf16[8,192,384]{2,1,0:T(8,128)(2,1)S(1)}) custom-call(s32[9]{0:T(128)S(1)} %concatenate.19.step_ref, bf16[2,768,768]{2,1,0:T(8,128)(2,1)S(1)} %copy-done.18, bf16[2,768,768]{2,1,0:T(8,128)(2,1)S(1)} %copy-done.20, bf16[768,384]{1,0:T(8,128)(2,1)S(1)} %act_gradient.3.refs_2_, ...), custom_call_target="tpu_custom_call" | custom-call | flops 1 | bytes 1 | tf_op jit(solution)/shard_map/weight_gradient/pallas_call | solution.py:300
  371.3 24.1 %collective-permute-done.51 = bf16[8,192,384]{2,1,0:T(8,128)(2,1)S(1)} collective-permute-done((bf16[8,192,384]{2,1,0:T(8,128)(2,1)S(1)}, bf16[8,192,384]{2,1,0:T(8,128)(2,1)S(1)}, u32[]{:S(2)}, u32[]{:S(2)}) %collective-permute-start.51) | collective-permute-done | bytes 1179680 | tf_op jit(solution)/shard_map/ppermute | solution.py:631
  396.6 6.0 %all-to-all-start.2 = ((bf16[8,192,384]{2,1,0:T(8,128)(2,1)}), bf16[8,192,384]{2,1,0:T(8,128)(2,1)S(1)}, u32[]{:S(2)}, u32[]{:S(2)}) async-start(bf16[8,192,384]{2,1,0:T(8,128)(2,1)} %broadcast_select_fusion.1), calls=%async_computation.2 | async-start | bytes 2359296 | tf_op jit(solution)/shard_map/all_to_all | solution.py:536
  406.1 20.9 %all-to-all-done.2.refs_0_ = bf16[8,192,384]{2,1,0:T(8,128)(2,1)S(1)} async-done(((bf16[8,192,384]{2,1,0:T(8,128)(2,1)}), bf16[8,192,384]{2,1,0:T(8,128)(2,1)S(1)}, u32[]{:S(2)}, u32[]{:S(2)}) %all-to-all-start.2) | async-done | bytes 1179680 | tf_op jit(solution)/shard_map/all_to_all | solution.py:536
  (295 shorter events, 201.9 us)
Async XLA Ops:
  16.4 19.2 %collective-permute-start.5 = (bf16[544,768]{1,0:T(8,128)(2,1)S(1)}, bf16[544,768]{1,0:T(8,128)(2,1)S(1)}, u32[]{:S(2)}, u32[]{:S(2)}) collective-permute-start(bf16[544,768]{1,0:T(8,128)(2,1)S(1)} %stacked.6), channel_id=1, source_target_pairs={{0,1},{1,0},{2,3},{3,2},{4,5},{5,4},{6,7},{7,6},{8,9},{9,8},{10,11... | collective-permute-start | bytes 2506760 | tf_op jit(solution)/shard_map/ppermute | solution.py:517
  46.5 54.5 %all-to-all-start = ((bf16[8,384,384]{2,1,0:T(8,128)(2,1)}), bf16[8,384,384]{2,1,0:T(8,128)(2,1)S(1)}, u32[]{:S(2)}, u32[]{:S(2)}) async-start(bf16[8,384,384]{2,1,0:T(8,128)(2,1)} %bitcast.61), calls=%async_computation | async-start | bytes 4718592 | tf_op jit(solution)/shard_map/all_to_all | solution.py:536
  56.2 44.9 %collective-permute-start.11 = (bf16[816,768]{1,0:T(8,128)(2,1)}, bf16[816,768]{1,0:T(8,128)(2,1)}, u32[]{:S(2)}, u32[]{:S(2)}) collective-permute-start(bf16[816,768]{1,0:T(8,128)(2,1)} %stacked.9), channel_id=1, source_target_pairs={{0,1},{1,0},{2,3},{3,2},{4,5},{5,4},{6,7},{7,6},{8,9},{9,8},{10,11... | collective-permute-start | bytes 3760136 | tf_op jit(solution)/shard_map/ppermute | solution.py:517
  56.8 43.3 %collective-permute-start.8 = (bf16[544,768]{1,0:T(8,128)(2,1)S(1)}, bf16[544,768]{1,0:T(8,128)(2,1)S(1)}, u32[]{:S(2)}, u32[]{:S(2)}) collective-permute-start(bf16[544,768]{1,0:T(8,128)(2,1)S(1)} %stacked.7), channel_id=1, source_target_pairs={{0,1},{1,0},{2,3},{3,2},{4,5},{5,4},{6,7},{7,6},{8,9},{9,8},{10,11... | collective-permute-start | bytes 2506760 | tf_op jit(solution)/shard_map/ppermute | solution.py:517
  101.0 57.0 %all-to-all-start.1 = ((bf16[8,384,384]{2,1,0:T(8,128)(2,1)}), bf16[8,384,384]{2,1,0:T(8,128)(2,1)}, u32[]{:S(2)}, u32[]{:S(2)}) async-start(bf16[8,384,384]{2,1,0:T(8,128)(2,1)} %bitcast.64), calls=%async_computation.1 | async-start | bytes 4718592 | tf_op jit(solution)/shard_map/all_to_all | solution.py:536
  115.1 26.4 %collective-permute-start.12 = (bf16[816,768]{1,0:T(8,128)(2,1)}, bf16[816,768]{1,0:T(8,128)(2,1)}, u32[]{:S(2)}, u32[]{:S(2)}) collective-permute-start(bf16[816,768]{1,0:T(8,128)(2,1)} %stacked.9), channel_id=1, source_target_pairs={{2,0},{0,2},{3,1},{1,3},{6,4},{4,6},{7,5},{5,7},{10,8},{8,10},{11,... | collective-permute-start | bytes 3760136 | tf_op jit(solution)/shard_map/ppermute | solution.py:44
  115.6 25.9 %collective-permute-start.13 = (bf16[816,768]{1,0:T(8,128)(2,1)}, bf16[816,768]{1,0:T(8,128)(2,1)}, u32[]{:S(2)}, u32[]{:S(2)}) collective-permute-start(bf16[816,768]{1,0:T(8,128)(2,1)} %collective-permute-done.11), channel_id=1, source_target_pairs={{2,0},{0,2},{3,1},{1,3},{6,4},{4,6},{7,5},{5,7},{10,8},{8,10},{11,... | collective-permute-start | bytes 3760136 | tf_op jit(solution)/shard_map/ppermute | solution.py:44
  169.8 32.1 %collective-permute-start.16 = (bf16[1280,1536]{1,0:T(8,128)(2,1)S(1)}, bf16[1280,1536]{1,0:T(8,128)(2,1)S(1)}, u32[]{:S(2)}, u32[]{:S(2)}) collective-permute-start(bf16[1280,1536]{1,0:T(8,128)(2,1)S(1)} %convolution_convert_fusion), channel_id=1, source_target_pairs={{2,0},{0,2},{3,1},{1,3},{6,4},{4,6},{7,5},{5,7},{10,8},{8,10},{11,... | collective-permute-start | bytes 11796488 | tf_op jit(solution)/shard_map/ppermute | solution.py:44
  174.2 20.0 %collective-permute-start.22 = (bf16[256,768]{1,0:T(8,128)(2,1)S(1)}, bf16[256,768]{1,0:T(8,128)(2,1)S(1)}, u32[]{:S(2)}, u32[]{:S(2)}) collective-permute-start(bf16[256,768]{1,0:T(8,128)(2,1)S(1)} %fusion.27), channel_id=1, source_target_pairs={{0,8},{8,16},{16,24},{24,28},{28,20},{20,12},{12,4},{4,0},{1,9},{9... | collective-permute-start | bytes 1179656 | tf_op jit(solution)/shard_map/ppermute | solution.py:39
  182.6 14.7 %collective-permute-start.20 = (bf16[256,768]{1,0:T(8,128)(2,1)S(1)}, bf16[256,768]{1,0:T(8,128)(2,1)S(1)}, u32[]{:S(2)}, u32[]{:S(2)}) collective-permute-start(bf16[256,768]{1,0:T(8,128)(2,1)S(1)} %fusion.20), channel_id=1, source_target_pairs={{0,4},{8,0},{16,8},{24,16},{28,24},{20,28},{12,20},{4,12},{1,5},{9... | collective-permute-start | bytes 1179656 | tf_op jit(solution)/shard_map/ppermute | solution.py:39
  186.1 15.6 %collective-permute-start.18 = (bf16[256,768]{1,0:T(8,128)(2,1)S(1)}, bf16[256,768]{1,0:T(8,128)(2,1)S(1)}, u32[]{:S(2)}, u32[]{:S(2)}) collective-permute-start(bf16[256,768]{1,0:T(8,128)(2,1)S(1)} %fusion.21), channel_id=1, source_target_pairs={{0,8},{8,16},{16,24},{24,28},{28,20},{20,12},{12,4},{4,0},{1,9},{9... | collective-permute-start | bytes 1179656 | tf_op jit(solution)/shard_map/ppermute | solution.py:39
  186.5 15.4 %collective-permute-start.21 = (bf16[256,768]{1,0:T(8,128)(2,1)S(1)}, bf16[256,768]{1,0:T(8,128)(2,1)S(1)}, u32[]{:S(2)}, u32[]{:S(2)}) collective-permute-start(bf16[256,768]{1,0:T(8,128)(2,1)S(1)} %fusion.26), channel_id=1, source_target_pairs={{0,4},{8,0},{16,8},{24,16},{28,24},{20,28},{12,20},{4,12},{1,5},{9... | collective-permute-start | bytes 1179656 | tf_op jit(solution)/shard_map/ppermute | solution.py:39
  194.2 39.8 %collective-permute-start.31 = (bf16[2048,384]{1,0:T(8,128)(2,1)}, bf16[2048,384]{1,0:T(8,128)(2,1)}, u32[]{:S(2)}, u32[]{:S(2)}) collective-permute-start(bf16[2048,384]{1,0:T(8,128)(2,1)} %constant_dynamic-update-slice_fusion), channel_id=1, source_target_pairs={{1,0},{3,2},{5,4},{7,6},{9,8},{11,10},{13,12},{15,14},{17,16},{19,... | collective-permute-start | bytes 4718600 | tf_op jit(solution)/shard_map/ppermute | solution.py:493
  215.9 32.9 %collective-permute-start.32 = (f32[1536]{0:T(1024)S(1)}, f32[1536]{0:T(1024)S(1)}, u32[]{:S(2)}, u32[]{:S(2)}) collective-permute-start(f32[1536]{0:T(1024)S(1)} %dynamic-slice_reduce_fusion), channel_id=1, source_target_pairs={{1,0},{3,2},{5,4},{7,6},{9,8},{11,10},{13,12},{15,14},{17,16},{19,... | collective-permute-start | bytes 18440 | tf_op jit(solution)/shard_map/ppermute | solution.py:493
  266.0 14.7 %collective-permute-start.41 = (bf16[256,768]{1,0:T(8,128)(2,1)S(1)}, bf16[256,768]{1,0:T(8,128)(2,1)S(1)}, u32[]{:S(2)}, u32[]{:S(2)}) collective-permute-start(bf16[256,768]{1,0:T(8,128)(2,1)S(1)} %fusion.38.refs_0_), channel_id=1, source_target_pairs={{0,4},{8,0},{16,8},{24,16},{28,24},{20,28},{12,20},{4,12},{1,5},{9... | collective-permute-start | bytes 1179656 | tf_op jit(solution)/shard_map/ppermute | solution.py:39
  270.2 16.5 %collective-permute-start.44 = (bf16[256,768]{1,0:T(8,128)(2,1)S(1)}, bf16[256,768]{1,0:T(8,128)(2,1)}, u32[]{:S(2)}, u32[]{:S(2)}) collective-permute-start(bf16[256,768]{1,0:T(8,128)(2,1)S(1)} %collective-permute-done.43.refs_7_), channel_id=1, source_target_pairs={{0,8},{8,16},{16,24},{24,28},{28,20},{20,12},{12,4},{4,0},{1,9},{9... | collective-permute-start | bytes 1179656 | tf_op jit(solution)/shard_map/ppermute | solution.py:39
  292.2 15.8 %collective-permute-start.45 = (bf16[2,1280,768]{2,1,0:T(8,128)(2,1)S(1)}, bf16[2,1280,768]{2,1,0:T(8,128)(2,1)S(1)}, u32[]{:S(2)}, u32[]{:S(2)}) collective-permute-start(bf16[2,1280,768]{2,1,0:T(8,128)(2,1)S(1)} %stacked_parts.2.own_ref.refs_0_), channel_id=1, source_target_pairs={{2,0},{0,2},{3,1},{1,3},{6,4},{4,6},{7,5},{5,7},{10,8},{8,10},{11,... | collective-permute-start | bytes 11796488 | tf_op jit(solution)/shard_map/ppermute | solution.py:44
  296.3 35.5 %collective-permute-start.49 = (bf16[256,768]{1,0:T(8,128)(2,1)}, bf16[256,768]{1,0:T(8,128)(2,1)}, u32[]{:S(2)}, u32[]{:S(2)}) collective-permute-start(bf16[256,768]{1,0:T(8,128)(2,1)} %collective-permute-done.44.refs_9_), channel_id=1, source_target_pairs={{0,8},{8,16},{16,24},{24,28},{28,20},{20,12},{12,4},{4,0},{1,9},{9... | collective-permute-start | bytes 1179656 | tf_op jit(solution)/shard_map/ppermute | solution.py:39
  298.0 33.8 %collective-permute-start.47 = (bf16[256,768]{1,0:T(8,128)(2,1)}, bf16[256,768]{1,0:T(8,128)(2,1)}, u32[]{:S(2)}, u32[]{:S(2)}) collective-permute-start(bf16[256,768]{1,0:T(8,128)(2,1)} %collective-permute-done.42.refs_3_), channel_id=1, source_target_pairs={{0,4},{8,0},{16,8},{24,16},{28,24},{20,28},{12,20},{4,12},{1,5},{9... | collective-permute-start | bytes 1179656 | tf_op jit(solution)/shard_map/ppermute | solution.py:39
  309.9 21.9 %collective-permute-start.46 = (bf16[256,768]{1,0:T(8,128)(2,1)}, bf16[256,768]{1,0:T(8,128)(2,1)}, u32[]{:S(2)}, u32[]{:S(2)}) collective-permute-start(bf16[256,768]{1,0:T(8,128)(2,1)} %collective-permute-done.38.refs_2_), channel_id=1, source_target_pairs={{0,8},{8,16},{16,24},{24,28},{28,20},{20,12},{12,4},{4,0},{1,9},{9... | collective-permute-start | bytes 1179656 | tf_op jit(solution)/shard_map/ppermute | solution.py:39
  311.2 20.6 %collective-permute-start.48 = (bf16[256,768]{1,0:T(8,128)(2,1)}, bf16[256,768]{1,0:T(8,128)(2,1)}, u32[]{:S(2)}, u32[]{:S(2)}) collective-permute-start(bf16[256,768]{1,0:T(8,128)(2,1)} %collective-permute-done.40.refs_4_), channel_id=1, source_target_pairs={{0,4},{8,0},{16,8},{24,16},{28,24},{20,28},{12,20},{4,12},{1,5},{9... | collective-permute-start | bytes 1179656 | tf_op jit(solution)/shard_map/ppermute | solution.py:39
  348.4 48.2 %all-to-all-start.3 = ((bf16[8,192,384]{2,1,0:T(8,128)(2,1)}), bf16[8,192,384]{2,1,0:T(8,128)(2,1)S(1)}, u32[]{:S(2)}, u32[]{:S(2)}) async-start(bf16[8,192,384]{2,1,0:T(8,128)(2,1)} %weight_gradient.6), calls=%async_computation.3 | async-start | bytes 2359296 | tf_op jit(solution)/shard_map/all_to_all | solution.py:536
  367.5 27.9 %collective-permute-start.51 = (bf16[8,192,384]{2,1,0:T(8,128)(2,1)S(1)}, bf16[8,192,384]{2,1,0:T(8,128)(2,1)S(1)}, u32[]{:S(2)}, u32[]{:S(2)}) collective-permute-start(bf16[8,192,384]{2,1,0:T(8,128)(2,1)S(1)} %get-tuple-element.86), channel_id=1, source_target_pairs={{1,0},{3,2},{5,4},{7,6},{9,8},{11,10},{13,12},{15,14},{17,16},{19,... | collective-permute-start | bytes 3538952 | tf_op jit(solution)/shard_map/ppermute | solution.py:631
  396.6 30.5 %all-to-all-start.2 = ((bf16[8,192,384]{2,1,0:T(8,128)(2,1)}), bf16[8,192,384]{2,1,0:T(8,128)(2,1)S(1)}, u32[]{:S(2)}, u32[]{:S(2)}) async-start(bf16[8,192,384]{2,1,0:T(8,128)(2,1)} %broadcast_select_fusion.1), calls=%async_computation.2 | async-start | bytes 2359296 | tf_op jit(solution)/shard_map/all_to_all | solution.py:536
  (98 other events, 706.3 us)

commit v4 on v3

--- a/solution.py
+++ b/solution.py
@@ -11,6 +11,10 @@
 
 
 NO_COST = pl.CostEstimate(flops=1, bytes_accessed=1, transcendentals=0)
+
+
+def cost(flops, bytes_accessed):
+    return pl.CostEstimate(flops=flops, bytes_accessed=bytes_accessed, transcendentals=0)
 
 
 def gelu_tanh(values):
@@ -168,7 +172,7 @@
         out_shape=jax.ShapeDtypeStruct((len(parts), rows * count, columns), parts[0][0].dtype),
         in_specs=in_vmem(len(flat)),
         out_specs=pl.BlockSpec(memory_space=pltpu.VMEM),
-        compiler_params=pltpu.CompilerParams(vmem_limit_bytes=24 << 20),
+        compiler_params=pltpu.CompilerParams(vmem_limit_bytes=16 << 20),
         cost_estimate=NO_COST,
         name="stacked_parts",
     )(*flat)
@@ -218,7 +222,7 @@
         out_shape=[jax.ShapeDtypeStruct((halves, total_rows, part), jnp.bfloat16)] * 2
         + [jax.ShapeDtypeStruct((total_rows, units), kind) for kind in (jnp.float32, jnp.bfloat16)],
         compiler_params=pltpu.CompilerParams(vmem_limit_bytes=24 << 20),
-        cost_estimate=NO_COST,
+        cost_estimate=cost(2 * total_rows * features * units, 4 * total_rows * features),
         name="modulated_up",
     )(timesteps, places, table, up, *tokens)
 
@@ -248,21 +252,18 @@
         out_specs=pl.BlockSpec((rows, units), lambda i: (i, 0)),
         out_shape=jax.ShapeDtypeStruct((total_rows, units), jnp.bfloat16),
         compiler_params=pltpu.CompilerParams(vmem_limit_bytes=16 << 20),
-        cost_estimate=NO_COST,
+        cost_estimate=cost(2 * total_rows * features * units, 2 * total_rows * features),
         name="act_gradient",
     )(down, pre, own, other)
 
 
-def weight_gradient(own, other, right, steps, block, one_side, added=None):
+def weight_gradient(own, other, right, steps, block, added=None):
     halves, _, part = own.shape
     units = right.shape[1]
     each = part // block
     count = halves * each
     half = block // 2
-    kept = half if one_side else block
-    skipped = half // LANES * LANES
     given = [own, other, right] + list(added or [])
-    results, rows_out = (1, half) if one_side else (2, half)
 
     def kernel(step_ref, *refs):
         ins, outs = refs[: len(given)], refs[len(given) :]
@@ -274,29 +275,19 @@
             value = (value + ins[3 + which][0]).astype(jnp.bfloat16)
             step = step_ref[which * count + pl.program_id(0)]
             for k, out in enumerate(outs):
-                out[step] = value[k * rows_out : (k + 1) * rows_out]
+                out[step] = value[k * half : (k + 1) * half]
 
         for which in range(2):
-            if not one_side:
-                keep(which, over_tokens(ins[which][0], ins[2][...]))
-                continue
-
-            @pl.when(step_ref[2 * count] == 0)
-            def _():
-                keep(which, over_tokens(ins[which][0, :, : block - skipped], ins[2][...])[:half])
-
-            @pl.when(step_ref[2 * count] == 1)
-            def _():
-                keep(which, over_tokens(ins[which][0, :, skipped:], ins[2][...])[half - skipped :])
-
-    block_of = pl.BlockSpec((1, kept, units), lambda i, step_ref: (i, 0, 0))
+            keep(which, over_tokens(ins[which][0], ins[2][...]))
+
+    block_of = pl.BlockSpec((1, block, units), lambda i, step_ref: (i, 0, 0))
     in_specs = [pl.BlockSpec((1, own.shape[1], block), lambda i, step_ref: (i // each, 0, i % each))] * 2
     in_specs += [pl.BlockSpec(right.shape, lambda i, step_ref: (0, 0))] + [block_of] * (len(given) - 3)
     if added is None:
-        out_specs, out_shape = [block_of] * 2, [jax.ShapeDtypeStruct((count, kept, units), jnp.float32)] * 2
+        out_specs, out_shape = [block_of] * 2, [jax.ShapeDtypeStruct((count, block, units), jnp.float32)] * 2
     else:
-        out_specs = [pl.BlockSpec((2 * count, rows_out, units), lambda i, step_ref: (0, 0, 0))] * results
-        out_shape = [jax.ShapeDtypeStruct((2 * count, rows_out, units), jnp.bfloat16)] * results
+        out_specs = [pl.BlockSpec((2 * count, half, units), lambda i, step_ref: (0, 0, 0))] * 2
+        out_shape = [jax.ShapeDtypeStruct((2 * count, half, units), jnp.bfloat16)] * 2
     return pl.pallas_call(
         kernel,
         grid_spec=pltpu.PrefetchScalarGridSpec(
@@ -304,9 +295,56 @@
         ),
         out_shape=out_shape,
         compiler_params=pltpu.CompilerParams(vmem_limit_bytes=20 << 20),
-        cost_estimate=NO_COST,
+        cost_estimate=cost(4 * own.size * units, 4 * own.size),
         name="weight_gradient",
     )(steps, *given)
+
+
+def side_gradient(lefts, rights, steps, block):
+    halves, _, part = lefts[0][0].shape
+    units = rights[0].shape[1]
+    each = part // block
+    count = halves * each
+    half = block // 2
+    groups = len(lefts)
+    skipped = half // LANES * LANES
+
+    def kernel(step_ref, *refs):
+        left_refs, right_refs, out_ref = refs[: 2 * groups], refs[2 * groups : 3 * groups], refs[-1]
+
+        def found(which, begin, end):
+            return sum(
+                over_tokens(left_refs[2 * g + which][0, :, begin:end], right_refs[g][...]) for g in range(groups)
+            ).astype(jnp.bfloat16)
+
+        for which in range(2):
+            step = step_ref[which * count + pl.program_id(0)]
+
+            @pl.when(step_ref[2 * count] == 0)
+            def _():
+                out_ref[step] = found(which, 0, block - skipped)[:half]
+
+            @pl.when(step_ref[2 * count] == 1)
+            def _():
+                out_ref[step] = found(which, skipped, block)[half - skipped :]
+
+    left_specs = [
+        pl.BlockSpec((1, x.shape[1], block), lambda i, step_ref: (i // each, 0, i % each)) for pair in lefts for x in pair
+    ]
+    right_specs = [pl.BlockSpec(x.shape, lambda i, step_ref: (0, 0)) for x in rights]
+    return pl.pallas_call(
+        kernel,
+        grid_spec=pltpu.PrefetchScalarGridSpec(
+            num_scalar_prefetch=1,
+            grid=(count,),
+            in_specs=left_specs + right_specs,
+            out_specs=pl.BlockSpec((2 * count, half, units), lambda i, step_ref: (0, 0, 0)),
+        ),
+        out_shape=jax.ShapeDtypeStruct((2 * count, half, units), jnp.bfloat16),
+        compiler_params=pltpu.CompilerParams(vmem_limit_bytes=24 << 20),
+        cost_estimate=cost(4 * sum(x.size for x in rights) * halves * part, 4 * sum(x.shape[0] for x in rights) * halves * part),
+        name="side_gradient",
+    )(steps, *[x for pair in lefts for x in pair], *rights)
 
 
 def after(x, *others):
@@ -575,10 +613,10 @@
     ways = (1, -1)
     far_share = other_share(far_images[:1], far_act[:rows])
     there = [ring_shift(term(farthest, c).astype(jnp.bfloat16), ways[c]) for c in range(2)]
-    middle_share = other_share(far_images[1:], after(far_act[rows:], far_share))
+    other_share(far_images[1:], after(far_act[rows:], far_share))
     student_act = of_student(jnp.concatenate([near_act, far_act], axis=0))
     back = [None, None]
-    other_share(near_images, after(near_act, middle_share))
+    other_share(near_images, after(near_act, far_share))
     for hop in range(farthest - 1, 0, -1):
         if hop < farthest - 1:
             there = after(there, back)
@@ -616,18 +654,18 @@
                 found[c][(way * hop) % count] = back[c]
     near_grad_pre = act_gradient(*near_grads, down, near_pre, rows)
     far_found = [[found[c][r] for r in far_images] for c in range(2)]
-    near_up = weight_gradient(*near_normed, near_grad_pre, steps, block, False)
+    near_up = weight_gradient(*near_normed, near_grad_pre, steps, block)
     far_own = stacked_parts(after(far_found, *there, near_up))
     far_grads = [far_own, from_core(far_own, 1)]
-    near_down = weight_gradient(*after(near_grads, far_own), student_acts[0], steps, block, True)
 
     def delivered(found):
         return exchanged(found.reshape(-1, share)).reshape(found.shape)
 
-    (down_found,) = weight_gradient(*far_grads, student_acts[1], steps, block, True, near_down)
+    far_grad_pre = act_gradient(*far_grads, down, far_pre, rows)
+    up_found = weight_gradient(*far_normed, far_grad_pre, steps, block, near_up)
+    far_grads = after(far_grads, up_found)
+    down_found = side_gradient([near_grads, far_grads], student_acts, steps, block)
     down_arrived = delivered(down_found)
-    far_grad_pre = act_gradient(*after(far_grads, down_found), down, far_pre, rows)
-    up_found = weight_gradient(*far_normed, far_grad_pre, steps, block, False, near_up)
     handed = lax.ppermute(up_found[0], "side", [(1, 0)])
     up_arrived = [delivered(jnp.where(is_student, up_found[1], handed))]
     up_share, down_share = received(up_arrived), received([down_arrived])

time: 436 us -> 422 us (0.968)
  local copies, waits for them, and re-layouts: 56.3 us -> 38.9 us
    unnamed x134 -> x116, local copies, waits for them, and re-layouts: 46.5 us -> 29.2 us
    pallas_call x4 -> x2, Pallas kernels: 22.1 us -> 10.8 us  [weight_gradient(): pl.pallas_call(kernel, grid_spec=pltpu.PrefetchScalarGridSpec(num_scalar_...]
    pallas_call x0 -> x1, Pallas kernels: none -> 9.52 us  [side_gradient(): pl.pallas_call(kernel, grid_spec=pltpu.PrefetchScalarGridSpec(num_scalar_...]
    ppermute x9, waiting for transfers between devices: 8.54 us -> 17.2 us  [from_core(): return lax.ppermute(x, 'mp', [((c + by) % count, c) for c in range(count)])]
  transfers between devices with their start and end apart: 56 -> 56, of which waited for: 31 -> 33; matrix products, arithmetic and copies ran while one was open for 8% -> 9% of each run, Pallas kernels for 12% -> 10%
where the time goes in v4:
time: 422 us; the launch traced here: 415 us
  waiting for transfers between devices  201 us (48%)
  starting transfers between devices  74.9 us (18%)
  Pallas kernels  67.3 us (16%)
  local copies, waits for them, and re-layouts  38.9 us (9%)
  matrix products  20.3 us (5%)
  other arithmetic  9.66 us (2%)
    ppermute x35, waiting for transfers between devices, ring_shift(): lax.ppermute(x, 'dp', [(order[p], order[(p + by) % count]) for p in range...  76.7 us
    ppermute x3, waiting for transfers between devices, cross_over(): return lax.ppermute(stacked([round_ring[r] for r in images]), 'side', swap)  48.5 us
    ppermute x35, starting transfers between devices, ring_shift(): lax.ppermute(x, 'dp', [(order[p], order[(p + by) % count]) for p in range...  38.8 us
    unnamed x116, local copies, waits for them, and re-layouts  29.2 us
    ppermute x1, waiting for transfers between devices, paired_shards(): handed = lax.ppermute(up_found[0], 'side', [(1, 0)])  24.9 us
    all_to_all x4, starting transfers between devices, exchanged(): return lax.all_to_all(x, 'dp', split_axis=0, concat_axis=0, tiled=True)  22.5 us
    all_to_all x4, waiting for transfers between devices, exchanged(): return lax.all_to_all(x, 'dp', split_axis=0, concat_axis=0, tiled=True)  22.4 us
    pallas_call x2, Pallas kernels, modulated_up(): pl.pallas_call(kernel, grid_spec=pltpu.PrefetchScalarGridSpec(num_scalar_...  20.4 us
  transfers between devices with their start and end apart: 56, of which 33 were waited for; matrix products, arithmetic and copies ran while one was open for 9% of the time, Pallas kernels for 10%

profile of v4, /device:TPU:10, one launch (start us, length us, event | category | flops | bytes accessed | tf_op | source)
XLA Modules:
  0.0 414.7 jit_solution(16547012238384300071)
XLA Ops:
  9.9 5.1 %collective-permute-done.1.refs_2_.refs_1_ = bf16[272,768]{1,0:T(8,128)(2,1)S(1)} collective-permute-done((bf16[272,768]{1,0:T(8,128)(2,1)S(1)}, bf16[272,768]{1,0:T(8,128)(2,1)S(1)}, u32[]{:S(2)}, u32[]{:S(2)}) %collective-permute-start.1) | collective-permute-done | bytes 417824 | tf_op jit(solution)/shard_map/ppermute | solution.py:43
  19.0 7.9 %collective-permute-done.3.refs_4_.refs_1_ = bf16[272,768]{1,0:T(8,128)(2,1)S(1)} collective-permute-done((bf16[272,768]{1,0:T(8,128)(2,1)S(1)}, bf16[272,768]{1,0:T(8,128)(2,1)S(1)}, u32[]{:S(2)}, u32[]{:S(2)}) %collective-permute-start.3) | collective-permute-done | bytes 417824 | tf_op jit(solution)/shard_map/ppermute | solution.py:43
  28.9 6.7 %collective-permute-done.5.refs_1_ = bf16[544,768]{1,0:T(8,128)(2,1)S(1)} collective-permute-done((bf16[544,768]{1,0:T(8,128)(2,1)S(1)}, bf16[544,768]{1,0:T(8,128)(2,1)S(1)}, u32[]{:S(2)}, u32[]{:S(2)}) %collective-permute-start.5) | collective-permute-done | bytes 835616 | tf_op jit(solution)/shard_map/ppermute | solution.py:555
  39.2 6.6 %collective-permute-done.6.refs_0_ = bf16[272,768]{1,0:T(8,128)(2,1)S(1)} collective-permute-done((bf16[272,768]{1,0:T(8,128)(2,1)S(1)}, bf16[272,768]{1,0:T(8,128)(2,1)S(1)}, u32[]{:S(2)}, u32[]{:S(2)}) %collective-permute-start.6) | collective-permute-done | bytes 417824 | tf_op jit(solution)/shard_map/ppermute | solution.py:43
  46.6 5.5 %all-to-all-start = ((bf16[8,384,384]{2,1,0:T(8,128)(2,1)}), bf16[8,384,384]{2,1,0:T(8,128)(2,1)S(1)}, u32[]{:S(2)}, u32[]{:S(2)}) async-start(bf16[8,384,384]{2,1,0:T(8,128)(2,1)} %bitcast.61), calls=%async_computation | async-start | bytes 4718592 | tf_op jit(solution)/shard_map/all_to_all | solution.py:574
  58.3 41.8 %collective-permute-done.8.refs_2_ = bf16[544,768]{1,0:T(8,128)(2,1)S(1)} collective-permute-done((bf16[544,768]{1,0:T(8,128)(2,1)S(1)}, bf16[544,768]{1,0:T(8,128)(2,1)S(1)}, u32[]{:S(2)}, u32[]{:S(2)}) %collective-permute-start.8) | collective-permute-done | bytes 835616 | tf_op jit(solution)/shard_map/ppermute | solution.py:555
  101.1 6.4 %all-to-all-start.1 = ((bf16[8,384,384]{2,1,0:T(8,128)(2,1)}), bf16[8,384,384]{2,1,0:T(8,128)(2,1)}, u32[]{:S(2)}, u32[]{:S(2)}) async-start(bf16[8,384,384]{2,1,0:T(8,128)(2,1)} %bitcast.64), calls=%async_computation.1 | async-start | bytes 4718592 | tf_op jit(solution)/shard_map/all_to_all | solution.py:574
  117.4 4.9 %collective-permute-done.12 = bf16[816,768]{1,0:T(8,128)(2,1)} collective-permute-done((bf16[816,768]{1,0:T(8,128)(2,1)}, bf16[816,768]{1,0:T(8,128)(2,1)}, u32[]{:S(2)}, u32[]{:S(2)}) %collective-permute-start.12) | collective-permute-done | bytes 1253408 | tf_op jit(solution)/shard_map/ppermute | solution.py:48
  126.5 8.3 %modulated_up.3 = (bf16[2,768,768]{2,1,0:T(8,128)(2,1)S(1)}, bf16[2,768,768]{2,1,0:T(8,128)(2,1)S(1)}, f32[768,384]{1,0:T(8,128)S(1)}, bf16[768,384]{1,0:T(8,128)(2,1)S(1)}) custom-call(s32[3]{0:T(128)S(1)} %add_bitcast_fusion.step_ref, s32[4]{0:T(128)S(1)} %pad_add_fusion.place_ref, f32[50,8,3072]{2,1,0:T(8,128)S(1)} %copy-done, ...), custom_call_target="tpu_custom_call" | custom-call | flops 1811939328 | bytes 9437184 | tf_op jit(solution)/shard_map/modulated_up/pallas_call | solution.py:210
  139.5 12.1 %modulated_up.2 = (bf16[2,1280,768]{2,1,0:T(8,128)(2,1)S(1)}, bf16[2,1280,768]{2,1,0:T(8,128)(2,1)S(1)}, f32[1280,384]{1,0:T(8,128)S(1)}, bf16[1280,384]{1,0:T(8,128)(2,1)S(1)}) custom-call(s32[5]{0:T(128)S(1)} %add_bitcast_fusion.1.step_ref, s32[4]{0:T(128)S(1)} %pad_add_fusion.place_ref, f32[50,8,3072]{2,1,0:T(8,128)S(1)} %bitcast.58, ...), custom_call_target="tpu_custom_call" | custom-call | flops 3019898880 | bytes 15728640 | tf_op jit(solution)/shard_map/modulated_up/pallas_call | solution.py:210
  245.6 5.7 %collective-permute-done.35 = bf16[256,768]{1,0:T(8,128)(2,1)S(1)} collective-permute-done((bf16[256,768]{1,0:T(8,128)(2,1)S(1)}, bf16[256,768]{1,0:T(8,128)(2,1)S(1)}, u32[]{:S(2)}, u32[]{:S(2)}) %collective-permute-start.35) | collective-permute-done | bytes 393248 | tf_op jit(solution)/shard_map/ppermute | solution.py:636
  255.1 5.5 %collective-permute-done.33 = bf16[256,768]{1,0:T(8,128)(2,1)S(1)} collective-permute-done((bf16[256,768]{1,0:T(8,128)(2,1)S(1)}, bf16[256,768]{1,0:T(8,128)(2,1)S(1)}, u32[]{:S(2)}, u32[]{:S(2)}) %collective-permute-start.33) | collective-permute-done | bytes 393248 | tf_op jit(solution)/shard_map/ppermute | solution.py:636
  266.7 8.3 %collective-permute-done.34.refs_2_ = bf16[256,768]{1,0:T(8,128)(2,1)S(1)} collective-permute-done((bf16[256,768]{1,0:T(8,128)(2,1)S(1)}, bf16[256,768]{1,0:T(8,128)(2,1)S(1)}, u32[]{:S(2)}, u32[]{:S(2)}) %collective-permute-start.34) | collective-permute-done | bytes 393248 | tf_op jit(solution)/shard_map/ppermute | solution.py:43
  278.5 4.6 %collective-permute-done.44.refs_9_ = bf16[256,768]{1,0:T(8,128)(2,1)S(1)} collective-permute-done((bf16[256,768]{1,0:T(8,128)(2,1)S(1)}, bf16[256,768]{1,0:T(8,128)(2,1)S(1)}, u32[]{:S(2)}, u32[]{:S(2)}) %collective-permute-start.44) | collective-permute-done | bytes 393248 | tf_op jit(solution)/shard_map/ppermute | solution.py:43
  295.1 8.1 %collective-permute-done.38.refs_2_ = bf16[256,768]{1,0:T(8,128)(2,1)} collective-permute-done((bf16[256,768]{1,0:T(8,128)(2,1)}, bf16[256,768]{1,0:T(8,128)(2,1)}, u32[]{:S(2)}, u32[]{:S(2)}) %collective-permute-start.38) | collective-permute-done | bytes 393248 | tf_op jit(solution)/shard_map/ppermute | solution.py:43
  308.5 8.2 %act_gradient.2.refs_2_ = bf16[1280,384]{1,0:T(8,128)(2,1)S(1)} custom-call(bf16[384,3072]{1,0:T(8,128)(2,1)S(1)} %placed.1.down_ref, f32[1280,384]{1,0:T(8,128)S(1)} %copy-done.8, bf16[2,1280,768]{2,1,0:T(8,128)(2,1)} %stacked_parts.2.own_ref.refs_0_, bf16[2,1280,768]{2,1,0:T(8,128)(2,1)} %collective-permute-done.45.other_ref.refs_1_), custom_call_target="tpu_custom_call" | custom-call | flops 3019898880 | bytes 7864320 | tf_op jit(solution)/shard_map/act_gradient/pallas_call | solution.py:243
  316.8 6.4 %weight_gradient.2 = (f32[4,384,384]{2,1,0:T(8,128)S(1)}, f32[4,384,384]{2,1,0:T(8,128)S(1)}) custom-call(s32[9]{0:T(128)S(1)} %concatenate.19.step_ref, bf16[2,1280,768]{2,1,0:T(8,128)(2,1)S(1)} %copy-done.39, bf16[2,1280,768]{2,1,0:T(8,128)(2,1)S(1)} %copy-done.41, bf16[1280,384]{1,0:T(8,128)(2,1)S(1)} %act_gradient.2.refs_2_), custom_call_target="tpu_custom_call" | custom-call | flops 3019898880 | bytes 7864320 | tf_op jit(solution)/shard_map/weight_gradient/pallas_call | solution.py:291
  324.7 4.5 %collective-permute-done.50.other_ref.refs_3_ = bf16[2,768,768]{2,1,0:T(8,128)(2,1)S(1)} collective-permute-done((bf16[2,768,768]{2,1,0:T(8,128)(2,1)S(1)}, bf16[2,768,768]{2,1,0:T(8,128)(2,1)S(1)}, u32[]{:S(2)}, u32[]{:S(2)}) %collective-permute-start.50) | collective-permute-done | bytes 2359328 | tf_op jit(solution)/shard_map/ppermute | solution.py:48
  332.9 4.4 %weight_gradient.3 = (bf16[8,192,384]{2,1,0:T(8,128)(2,1)S(1)}, bf16[8,192,384]{2,1,0:T(8,128)(2,1)S(1)}) custom-call(s32[9]{0:T(128)S(1)} %concatenate.19.step_ref, bf16[2,768,768]{2,1,0:T(8,128)(2,1)S(1)} %copy-done.3, bf16[2,768,768]{2,1,0:T(8,128)(2,1)S(1)} %copy-done.5, bf16[768,384]{1,0:T(8,128)(2,1)S(1)} %act_gradient.3.refs_2_, ...), custom_call_target="tpu_custom_call" | custom-call | flops 1811939328 | bytes 4718592 | tf_op jit(solution)/shard_map/weight_gradient/pallas_call | solution.py:291
  338.4 9.5 %side_gradient.1 = bf16[8,192,384]{2,1,0:T(8,128)(2,1)} custom-call(s32[9]{0:T(128)S(1)} %concatenate.19.step_ref, bf16[2,1280,768]{2,1,0:T(8,128)(2,1)} %stacked_parts.2.own_ref.refs_0_, bf16[2,1280,768]{2,1,0:T(8,128)(2,1)} %collective-permute-done.45.other_ref.refs_1_, bf16[2,768,768]{2,1,0:T(8,128)(2,1)S(1)} %stacked_parts.3.own_ref.refs_2_, ...), custom_call_target="tpu_custom_call" | custom-call | flops 4831838208 | bytes 12582912 | tf_op jit(solution)/shard_map/side_gradient/pallas_call | solution.py:335
  347.9 4.6 %all-to-all-start.3 = ((bf16[8,192,384]{2,1,0:T(8,128)(2,1)}), bf16[8,192,384]{2,1,0:T(8,128)(2,1)S(1)}, u32[]{:S(2)}, u32[]{:S(2)}) async-start(bf16[8,192,384]{2,1,0:T(8,128)(2,1)} %side_gradient.1), calls=%async_computation.3 | async-start | bytes 2359296 | tf_op jit(solution)/shard_map/all_to_all | solution.py:574
  356.3 24.9 %collective-permute-done.51 = bf16[8,192,384]{2,1,0:T(8,128)(2,1)S(1)} collective-permute-done((bf16[8,192,384]{2,1,0:T(8,128)(2,1)S(1)}, bf16[8,192,384]{2,1,0:T(8,128)(2,1)S(1)}, u32[]{:S(2)}, u32[]{:S(2)}) %collective-permute-start.51) | collective-permute-done | bytes 1179680 | tf_op jit(solution)/shard_map/ppermute | solution.py:669
  382.4 6.0 %all-to-all-start.2 = ((bf16[8,192,384]{2,1,0:T(8,128)(2,1)}), bf16[8,192,384]{2,1,0:T(8,128)(2,1)S(1)}, u32[]{:S(2)}, u32[]{:S(2)}) async-start(bf16[8,192,384]{2,1,0:T(8,128)(2,1)} %broadcast_select_fusion.1), calls=%async_computation.2 | async-start | bytes 2359296 | tf_op jit(solution)/shard_map/all_to_all | solution.py:574
  390.9 22.2 %all-to-all-done.2.refs_0_ = bf16[8,192,384]{2,1,0:T(8,128)(2,1)S(1)} async-done(((bf16[8,192,384]{2,1,0:T(8,128)(2,1)}), bf16[8,192,384]{2,1,0:T(8,128)(2,1)S(1)}, u32[]{:S(2)}, u32[]{:S(2)}) %all-to-all-start.2) | async-done | bytes 1179680 | tf_op jit(solution)/shard_map/all_to_all | solution.py:574
  (276 shorter events, 183.6 us)
Async XLA Ops:
  16.4 19.2 %collective-permute-start.5 = (bf16[544,768]{1,0:T(8,128)(2,1)S(1)}, bf16[544,768]{1,0:T(8,128)(2,1)S(1)}, u32[]{:S(2)}, u32[]{:S(2)}) collective-permute-start(bf16[544,768]{1,0:T(8,128)(2,1)S(1)} %stacked.6), channel_id=1, source_target_pairs={{0,1},{1,0},{2,3},{3,2},{4,5},{5,4},{6,7},{7,6},{8,9},{9,8},{10,11... | collective-permute-start | bytes 2506760 | tf_op jit(solution)/shard_map/ppermute | solution.py:555
  46.6 54.5 %all-to-all-start = ((bf16[8,384,384]{2,1,0:T(8,128)(2,1)}), bf16[8,384,384]{2,1,0:T(8,128)(2,1)S(1)}, u32[]{:S(2)}, u32[]{:S(2)}) async-start(bf16[8,384,384]{2,1,0:T(8,128)(2,1)} %bitcast.61), calls=%async_computation | async-start | bytes 4718592 | tf_op jit(solution)/shard_map/all_to_all | solution.py:574
  56.2 44.9 %collective-permute-start.11 = (bf16[816,768]{1,0:T(8,128)(2,1)}, bf16[816,768]{1,0:T(8,128)(2,1)}, u32[]{:S(2)}, u32[]{:S(2)}) collective-permute-start(bf16[816,768]{1,0:T(8,128)(2,1)} %stacked.9), channel_id=1, source_target_pairs={{0,1},{1,0},{2,3},{3,2},{4,5},{5,4},{6,7},{7,6},{8,9},{9,8},{10,11... | collective-permute-start | bytes 3760136 | tf_op jit(solution)/shard_map/ppermute | solution.py:555
  56.8 43.4 %collective-permute-start.8 = (bf16[544,768]{1,0:T(8,128)(2,1)S(1)}, bf16[544,768]{1,0:T(8,128)(2,1)S(1)}, u32[]{:S(2)}, u32[]{:S(2)}) collective-permute-start(bf16[544,768]{1,0:T(8,128)(2,1)S(1)} %stacked.7), channel_id=1, source_target_pairs={{0,1},{1,0},{2,3},{3,2},{4,5},{5,4},{6,7},{7,6},{8,9},{9,8},{10,11... | collective-permute-start | bytes 2506760 | tf_op jit(solution)/shard_map/ppermute | solution.py:555
  101.1 56.9 %all-to-all-start.1 = ((bf16[8,384,384]{2,1,0:T(8,128)(2,1)}), bf16[8,384,384]{2,1,0:T(8,128)(2,1)}, u32[]{:S(2)}, u32[]{:S(2)}) async-start(bf16[8,384,384]{2,1,0:T(8,128)(2,1)} %bitcast.64), calls=%async_computation.1 | async-start | bytes 4718592 | tf_op jit(solution)/shard_map/all_to_all | solution.py:574
  113.0 26.4 %collective-permute-start.9 = (bf16[1360,768]{1,0:T(8,128)(2,1)}, bf16[1360,768]{1,0:T(8,128)(2,1)}, u32[]{:S(2)}, u32[]{:S(2)}) collective-permute-start(bf16[1360,768]{1,0:T(8,128)(2,1)} %stacked.5), channel_id=1, source_target_pairs={{2,0},{0,2},{3,1},{1,3},{6,4},{4,6},{7,5},{5,7},{10,8},{8,10},{11,... | collective-permute-start | bytes 6266888 | tf_op jit(solution)/shard_map/ppermute | solution.py:48
  115.1 24.3 %collective-permute-start.10 = (bf16[1360,768]{1,0:T(8,128)(2,1)}, bf16[1360,768]{1,0:T(8,128)(2,1)}, u32[]{:S(2)}, u32[]{:S(2)}) collective-permute-start(bf16[1360,768]{1,0:T(8,128)(2,1)} %stacked.8), channel_id=1, source_target_pairs={{2,0},{0,2},{3,1},{1,3},{6,4},{4,6},{7,5},{5,7},{10,8},{8,10},{11,... | collective-permute-start | bytes 6266888 | tf_op jit(solution)/shard_map/ppermute | solution.py:48
  165.4 33.2 %collective-permute-start.15 = (bf16[1280,1536]{1,0:T(8,128)(2,1)S(1)}, bf16[1280,1536]{1,0:T(8,128)(2,1)S(1)}, u32[]{:S(2)}, u32[]{:S(2)}) collective-permute-start(bf16[1280,1536]{1,0:T(8,128)(2,1)S(1)} %convolution_convert_fusion), channel_id=1, source_target_pairs={{2,0},{0,2},{3,1},{1,3},{6,4},{4,6},{7,5},{5,7},{10,8},{8,10},{11,... | collective-permute-start | bytes 11796488 | tf_op jit(solution)/shard_map/ppermute | solution.py:48
  174.9 16.3 %collective-permute-start.22 = (bf16[256,768]{1,0:T(8,128)(2,1)S(1)}, bf16[256,768]{1,0:T(8,128)(2,1)S(1)}, u32[]{:S(2)}, u32[]{:S(2)}) collective-permute-start(bf16[256,768]{1,0:T(8,128)(2,1)S(1)} %fusion.27), channel_id=1, source_target_pairs={{0,8},{8,16},{16,24},{24,28},{28,20},{20,12},{12,4},{4,0},{1,9},{9... | collective-permute-start | bytes 1179656 | tf_op jit(solution)/shard_map/ppermute | solution.py:43
  179.4 15.0 %collective-permute-start.20 = (bf16[256,768]{1,0:T(8,128)(2,1)S(1)}, bf16[256,768]{1,0:T(8,128)(2,1)S(1)}, u32[]{:S(2)}, u32[]{:S(2)}) collective-permute-start(bf16[256,768]{1,0:T(8,128)(2,1)S(1)} %fusion.20), channel_id=1, source_target_pairs={{0,4},{8,0},{16,8},{24,16},{28,24},{20,28},{12,20},{4,12},{1,5},{9... | collective-permute-start | bytes 1179656 | tf_op jit(solution)/shard_map/ppermute | solution.py:43
  183.2 15.4 %collective-permute-start.18 = (bf16[256,768]{1,0:T(8,128)(2,1)S(1)}, bf16[256,768]{1,0:T(8,128)(2,1)S(1)}, u32[]{:S(2)}, u32[]{:S(2)}) collective-permute-start(bf16[256,768]{1,0:T(8,128)(2,1)S(1)} %fusion.21), channel_id=1, source_target_pairs={{0,8},{8,16},{16,24},{24,28},{28,20},{20,12},{12,4},{4,0},{1,9},{9... | collective-permute-start | bytes 1179656 | tf_op jit(solution)/shard_map/ppermute | solution.py:43
  183.6 15.0 %collective-permute-start.21 = (bf16[256,768]{1,0:T(8,128)(2,1)S(1)}, bf16[256,768]{1,0:T(8,128)(2,1)S(1)}, u32[]{:S(2)}, u32[]{:S(2)}) collective-permute-start(bf16[256,768]{1,0:T(8,128)(2,1)S(1)} %fusion.26), channel_id=1, source_target_pairs={{0,4},{8,0},{16,8},{24,16},{28,24},{20,28},{12,20},{4,12},{1,5},{9... | collective-permute-start | bytes 1179656 | tf_op jit(solution)/shard_map/ppermute | solution.py:43
  191.2 39.1 %collective-permute-start.31 = (bf16[2048,384]{1,0:T(8,128)(2,1)}, bf16[2048,384]{1,0:T(8,128)(2,1)}, u32[]{:S(2)}, u32[]{:S(2)}) collective-permute-start(bf16[2048,384]{1,0:T(8,128)(2,1)} %constant_dynamic-update-slice_fusion), channel_id=1, source_target_pairs={{1,0},{3,2},{5,4},{7,6},{9,8},{11,10},{13,12},{15,14},{17,16},{19,... | collective-permute-start | bytes 4718600 | tf_op jit(solution)/shard_map/ppermute | solution.py:531
  204.4 14.4 %collective-permute-start.23 = (bf16[256,768]{1,0:T(8,128)(2,1)}, bf16[256,768]{1,0:T(8,128)(2,1)}, u32[]{:S(2)}, u32[]{:S(2)}) collective-permute-start(bf16[256,768]{1,0:T(8,128)(2,1)} %fusion.22), channel_id=1, source_target_pairs={{0,8},{8,16},{16,24},{24,28},{28,20},{20,12},{12,4},{4,0},{1,9},{9... | collective-permute-start | bytes 1179656 | tf_op jit(solution)/shard_map/ppermute | solution.py:43
  212.5 33.0 %collective-permute-start.32 = (f32[1536]{0:T(1024)S(1)}, f32[1536]{0:T(1024)S(1)}, u32[]{:S(2)}, u32[]{:S(2)}) collective-permute-start(f32[1536]{0:T(1024)S(1)} %dynamic-slice_reduce_fusion), channel_id=1, source_target_pairs={{1,0},{3,2},{5,4},{7,6},{9,8},{11,10},{13,12},{15,14},{17,16},{19,... | collective-permute-start | bytes 18440 | tf_op jit(solution)/shard_map/ppermute | solution.py:531
  262.5 14.5 %collective-permute-start.41 = (bf16[256,768]{1,0:T(8,128)(2,1)S(1)}, bf16[256,768]{1,0:T(8,128)(2,1)S(1)}, u32[]{:S(2)}, u32[]{:S(2)}) collective-permute-start(bf16[256,768]{1,0:T(8,128)(2,1)S(1)} %fusion.38.refs_0_), channel_id=1, source_target_pairs={{0,4},{8,0},{16,8},{24,16},{28,24},{20,28},{12,20},{4,12},{1,5},{9... | collective-permute-start | bytes 1179656 | tf_op jit(solution)/shard_map/ppermute | solution.py:43
  266.6 16.5 %collective-permute-start.44 = (bf16[256,768]{1,0:T(8,128)(2,1)S(1)}, bf16[256,768]{1,0:T(8,128)(2,1)S(1)}, u32[]{:S(2)}, u32[]{:S(2)}) collective-permute-start(bf16[256,768]{1,0:T(8,128)(2,1)S(1)} %collective-permute-done.43.refs_7_), channel_id=1, source_target_pairs={{0,8},{8,16},{16,24},{24,28},{28,20},{20,12},{12,4},{4,0},{1,9},{9... | collective-permute-start | bytes 1179656 | tf_op jit(solution)/shard_map/ppermute | solution.py:43
  293.1 30.1 %collective-permute-start.49 = (bf16[256,768]{1,0:T(8,128)(2,1)}, bf16[256,768]{1,0:T(8,128)(2,1)S(1)}, u32[]{:S(2)}, u32[]{:S(2)}) collective-permute-start(bf16[256,768]{1,0:T(8,128)(2,1)} %copy-done.36), channel_id=1, source_target_pairs={{0,8},{8,16},{16,24},{24,28},{28,20},{20,12},{12,4},{4,0},{1,9},{9... | collective-permute-start | bytes 1179656 | tf_op jit(solution)/shard_map/ppermute | solution.py:43
  294.8 28.4 %collective-permute-start.47 = (bf16[256,768]{1,0:T(8,128)(2,1)}, bf16[256,768]{1,0:T(8,128)(2,1)S(1)}, u32[]{:S(2)}, u32[]{:S(2)}) collective-permute-start(bf16[256,768]{1,0:T(8,128)(2,1)} %copy-done.37), channel_id=1, source_target_pairs={{0,4},{8,0},{16,8},{24,16},{28,24},{20,28},{12,20},{4,12},{1,5},{9... | collective-permute-start | bytes 1179656 | tf_op jit(solution)/shard_map/ppermute | solution.py:43
  304.9 18.2 %collective-permute-start.46 = (bf16[256,768]{1,0:T(8,128)(2,1)}, bf16[256,768]{1,0:T(8,128)(2,1)S(1)}, u32[]{:S(2)}, u32[]{:S(2)}) collective-permute-start(bf16[256,768]{1,0:T(8,128)(2,1)} %collective-permute-done.38.refs_2_), channel_id=1, source_target_pairs={{0,8},{8,16},{16,24},{24,28},{28,20},{20,12},{12,4},{4,0},{1,9},{9... | collective-permute-start | bytes 1179656 | tf_op jit(solution)/shard_map/ppermute | solution.py:43
  305.9 17.2 %collective-permute-start.48 = (bf16[256,768]{1,0:T(8,128)(2,1)}, bf16[256,768]{1,0:T(8,128)(2,1)S(1)}, u32[]{:S(2)}, u32[]{:S(2)}) collective-permute-start(bf16[256,768]{1,0:T(8,128)(2,1)} %collective-permute-done.40.refs_4_), channel_id=1, source_target_pairs={{0,4},{8,0},{16,8},{24,16},{28,24},{20,28},{12,20},{4,12},{1,5},{9... | collective-permute-start | bytes 1179656 | tf_op jit(solution)/shard_map/ppermute | solution.py:43
  347.9 34.5 %all-to-all-start.3 = ((bf16[8,192,384]{2,1,0:T(8,128)(2,1)}), bf16[8,192,384]{2,1,0:T(8,128)(2,1)S(1)}, u32[]{:S(2)}, u32[]{:S(2)}) async-start(bf16[8,192,384]{2,1,0:T(8,128)(2,1)} %side_gradient.1), calls=%async_computation.3 | async-start | bytes 2359296 | tf_op jit(solution)/shard_map/all_to_all | solution.py:574
  352.5 28.7 %collective-permute-start.51 = (bf16[8,192,384]{2,1,0:T(8,128)(2,1)S(1)}, bf16[8,192,384]{2,1,0:T(8,128)(2,1)S(1)}, u32[]{:S(2)}, u32[]{:S(2)}) collective-permute-start(bf16[8,192,384]{2,1,0:T(8,128)(2,1)S(1)} %copy-done.43), channel_id=1, source_target_pairs={{1,0},{3,2},{5,4},{7,6},{9,8},{11,10},{13,12},{15,14},{17,16},{19,... | collective-permute-start | bytes 3538952 | tf_op jit(solution)/shard_map/ppermute | solution.py:669
  382.4 30.7 %all-to-all-start.2 = ((bf16[8,192,384]{2,1,0:T(8,128)(2,1)}), bf16[8,192,384]{2,1,0:T(8,128)(2,1)S(1)}, u32[]{:S(2)}, u32[]{:S(2)}) async-start(bf16[8,192,384]{2,1,0:T(8,128)(2,1)} %broadcast_select_fusion.1), calls=%async_computation.2 | async-start | bytes 2359296 | tf_op jit(solution)/shard_map/all_to_all | solution.py:574
  (89 other events, 665.5 us)

commit v5 on v4

--- a/solution.py
+++ b/solution.py
@@ -267,69 +267,67 @@
 
     def kernel(step_ref, *refs):
         ins, outs = refs[: len(given)], refs[len(given) :]
-
-        def keep(which, value):
-            if added is None:
-                outs[which][0] = value
-                return
-            value = (value + ins[3 + which][0]).astype(jnp.bfloat16)
-            step = step_ref[which * count + pl.program_id(0)]
-            for k, out in enumerate(outs):
-                out[step] = value[k * half : (k + 1) * half]
-
-        for which in range(2):
-            keep(which, over_tokens(ins[which][0], ins[2][...]))
-
-    block_of = pl.BlockSpec((1, block, units), lambda i, step_ref: (i, 0, 0))
-    in_specs = [pl.BlockSpec((1, own.shape[1], block), lambda i, step_ref: (i // each, 0, i % each))] * 2
-    in_specs += [pl.BlockSpec(right.shape, lambda i, step_ref: (0, 0))] + [block_of] * (len(given) - 3)
-    if added is None:
-        out_specs, out_shape = [block_of] * 2, [jax.ShapeDtypeStruct((count, block, units), jnp.float32)] * 2
-    else:
-        out_specs = [pl.BlockSpec((2 * count, half, units), lambda i, step_ref: (0, 0, 0))] * 2
-        out_shape = [jax.ShapeDtypeStruct((2 * count, half, units), jnp.bfloat16)] * 2
-    return pl.pallas_call(
-        kernel,
-        grid_spec=pltpu.PrefetchScalarGridSpec(
-            num_scalar_prefetch=1, grid=(count,), in_specs=in_specs, out_specs=out_specs
-        ),
-        out_shape=out_shape,
-        compiler_params=pltpu.CompilerParams(vmem_limit_bytes=20 << 20),
+        for b in range(count):
+            here = slice(b % each * block, (b % each + 1) * block)
+            for which in range(2):
+                value = over_tokens(ins[which][b // each, :, here], ins[2][...])
+                if added is None:
+                    outs[which][b] = value
+                    continue
+                value = (value + ins[3 + which][b]).astype(jnp.bfloat16)
+                step = step_ref[which * count + b]
+                for k, out in enumerate(outs):
+                    out[step] = value[k * half : (k + 1) * half]
+
+    shape, kind = ((count, block, units), jnp.float32) if added is None else ((2 * count, half, units), jnp.bfloat16)
+    return pl.pallas_call(
+        kernel,
+        in_specs=[pl.BlockSpec(memory_space=pltpu.SMEM)] + in_vmem(len(given)),
+        out_specs=in_vmem(2),
+        out_shape=[jax.ShapeDtypeStruct(shape, kind)] * 2,
+        compiler_params=pltpu.CompilerParams(vmem_limit_bytes=28 << 20),
         cost_estimate=cost(4 * own.size * units, 4 * own.size),
         name="weight_gradient",
     )(steps, *given)
 
 
-def side_gradient(lefts, rights, steps, block):
-    halves, _, part = lefts[0][0].shape
+def side_gradient(lefts, rights, steps, first, block, base=None):
+    halves, _, part = lefts[0].shape
     units = rights[0].shape[1]
     each = part // block
     count = halves * each
     half = block // 2
     groups = len(lefts)
     skipped = half // LANES * LANES
+    bases = [] if base is None else [base]
 
     def kernel(step_ref, *refs):
-        left_refs, right_refs, out_ref = refs[: 2 * groups], refs[2 * groups : 3 * groups], refs[-1]
-
-        def found(which, begin, end):
+        left_refs, right_refs, out_ref = refs[:groups], refs[groups : 2 * groups], refs[-1]
+
+        if bases:
+
+            @pl.when(pl.program_id(0) == 0)
+            def _():
+                out_ref[...] = refs[2 * groups][...]
+
+        def found(begin, end):
             return sum(
-                over_tokens(left_refs[2 * g + which][0, :, begin:end], right_refs[g][...]) for g in range(groups)
+                over_tokens(left_refs[g][0, :, begin:end], right_refs[g][...]) for g in range(groups)
             ).astype(jnp.bfloat16)
 
-        for which in range(2):
-            step = step_ref[which * count + pl.program_id(0)]
-
-            @pl.when(step_ref[2 * count] == 0)
-            def _():
-                out_ref[step] = found(which, 0, block - skipped)[:half]
-
-            @pl.when(step_ref[2 * count] == 1)
-            def _():
-                out_ref[step] = found(which, skipped, block)[half - skipped :]
-
+        step = step_ref[first + pl.program_id(0)]
+
+        @pl.when(step_ref[2 * count] == 0)
+        def _():
+            out_ref[step] = found(0, block - skipped)[:half]
+
+        @pl.when(step_ref[2 * count] == 1)
+        def _():
+            out_ref[step] = found(skipped, block)[half - skipped :]
+
+    whole = pl.BlockSpec((2 * count, half, units), lambda i, step_ref: (0, 0, 0))
     left_specs = [
-        pl.BlockSpec((1, x.shape[1], block), lambda i, step_ref: (i // each, 0, i % each)) for pair in lefts for x in pair
+        pl.BlockSpec((1, x.shape[1], block), lambda i, step_ref: (i // each, 0, i % each)) for x in lefts
     ]
     right_specs = [pl.BlockSpec(x.shape, lambda i, step_ref: (0, 0)) for x in rights]
     return pl.pallas_call(
@@ -337,14 +335,16 @@
         grid_spec=pltpu.PrefetchScalarGridSpec(
             num_scalar_prefetch=1,
             grid=(count,),
-            in_specs=left_specs + right_specs,
-            out_specs=pl.BlockSpec((2 * count, half, units), lambda i, step_ref: (0, 0, 0)),
+            in_specs=left_specs + right_specs + [whole] * len(bases),
+            out_specs=whole,
         ),
         out_shape=jax.ShapeDtypeStruct((2 * count, half, units), jnp.bfloat16),
         compiler_params=pltpu.CompilerParams(vmem_limit_bytes=24 << 20),
-        cost_estimate=cost(4 * sum(x.size for x in rights) * halves * part, 4 * sum(x.shape[0] for x in rights) * halves * part),
+        cost_estimate=cost(
+            2 * sum(x.size for x in rights) * halves * part, 2 * sum(x.shape[0] for x in rights) * halves * part
+        ),
         name="side_gradient",
-    )(steps, *[x for pair in lefts for x in pair], *rights)
+    )(steps, *lefts, *rights, *bases)
 
 
 def after(x, *others):
@@ -661,10 +661,12 @@
     def delivered(found):
         return exchanged(found.reshape(-1, share)).reshape(found.shape)
 
+    own_found = side_gradient([near_grads[0], far_own], student_acts, steps, 0, block)
+    far_grads = after(far_grads, own_found)
     far_grad_pre = act_gradient(*far_grads, down, far_pre, rows)
     up_found = weight_gradient(*far_normed, far_grad_pre, steps, block, near_up)
-    far_grads = after(far_grads, up_found)
-    down_found = side_gradient([near_grads, far_grads], student_acts, steps, block)
+    far_other = after(far_grads[1], up_found)
+    down_found = side_gradient([near_grads[1], far_other], student_acts, steps, count // 2, block, own_found)
     down_arrived = delivered(down_found)
     handed = lax.ppermute(up_found[0], "side", [(1, 0)])
     up_arrived = [delivered(jnp.where(is_student, up_found[1], handed))]

time: 422 us -> 418 us (level)
    ppermute x9, waiting for transfers between devices: 17.2 us -> 12.7 us  [from_core(): return lax.ppermute(x, 'mp', [((c + by) % count, c) for c in range(count)])]
    pallas_call x1 -> x2, Pallas kernels: 9.52 us -> 12 us  [side_gradient(): pl.pallas_call(kernel, grid_spec=pltpu.PrefetchScalarGridSpec(num_scalar_...]
    unnamed x116 -> x114, local copies, waits for them, and re-layouts: 29.2 us -> 29.2 us
  transfers between devices with their start and end apart: 56 -> 56, of which waited for: 33 -> 32; matrix products, arithmetic and copies ran while one was open for 9% -> 9% of each run, Pallas kernels for 10% -> 11%
where the time goes in v5:
time: 418 us; the launch traced here: 411 us
  waiting for transfers between devices  198 us (47%)
  starting transfers between devices  74.9 us (18%)
  Pallas kernels  66.8 us (16%)
  local copies, waits for them, and re-layouts  38.9 us (9%)
  matrix products  20.3 us (5%)
  other arithmetic  9.55 us (2%)
    ppermute x35, waiting for transfers between devices, ring_shift(): lax.ppermute(x, 'dp', [(order[p], order[(p + by) % count]) for p in range...  76.7 us
    ppermute x3, waiting for transfers between devices, cross_over(): return lax.ppermute(stacked([round_ring[r] for r in images]), 'side', swap)  48.5 us
    ppermute x35, starting transfers between devices, ring_shift(): lax.ppermute(x, 'dp', [(order[p], order[(p + by) % count]) for p in range...  38.7 us
    unnamed x114, local copies, waits for them, and re-layouts  29.2 us
    ppermute x1, waiting for transfers between devices, paired_shards(): handed = lax.ppermute(up_found[0], 'side', [(1, 0)])  25.5 us
    all_to_all x4, waiting for transfers between devices, exchanged(): return lax.all_to_all(x, 'dp', split_axis=0, concat_axis=0, tiled=True)  22.7 us
    all_to_all x4, starting transfers between devices, exchanged(): return lax.all_to_all(x, 'dp', split_axis=0, concat_axis=0, tiled=True)  22.4 us
    pallas_call x2, Pallas kernels, modulated_up(): pl.pallas_call(kernel, grid_spec=pltpu.PrefetchScalarGridSpec(num_scalar_...  20.4 us
  transfers between devices with their start and end apart: 56, of which 32 were waited for; matrix products, arithmetic and copies ran while one was open for 9% of the time, Pallas kernels for 11%

profile of v5, /device:TPU:10, one launch (start us, length us, event | category | flops | bytes accessed | tf_op | source)
XLA Modules:
  0.0 410.8 jit_solution(10859734923061109583)
XLA Ops:
  9.9 5.1 %collective-permute-done.1.refs_2_.refs_1_ = bf16[272,768]{1,0:T(8,128)(2,1)S(1)} collective-permute-done((bf16[272,768]{1,0:T(8,128)(2,1)S(1)}, bf16[272,768]{1,0:T(8,128)(2,1)S(1)}, u32[]{:S(2)}, u32[]{:S(2)}) %collective-permute-start.1) | collective-permute-done | bytes 417824 | tf_op jit(solution)/shard_map/ppermute | solution.py:43
  19.0 7.9 %collective-permute-done.3.refs_4_.refs_1_ = bf16[272,768]{1,0:T(8,128)(2,1)S(1)} collective-permute-done((bf16[272,768]{1,0:T(8,128)(2,1)S(1)}, bf16[272,768]{1,0:T(8,128)(2,1)S(1)}, u32[]{:S(2)}, u32[]{:S(2)}) %collective-permute-start.3) | collective-permute-done | bytes 417824 | tf_op jit(solution)/shard_map/ppermute | solution.py:43
  28.9 6.7 %collective-permute-done.5.refs_1_ = bf16[544,768]{1,0:T(8,128)(2,1)S(1)} collective-permute-done((bf16[544,768]{1,0:T(8,128)(2,1)S(1)}, bf16[544,768]{1,0:T(8,128)(2,1)S(1)}, u32[]{:S(2)}, u32[]{:S(2)}) %collective-permute-start.5) | collective-permute-done | bytes 835616 | tf_op jit(solution)/shard_map/ppermute | solution.py:555
  39.3 6.6 %collective-permute-done.6.refs_0_ = bf16[272,768]{1,0:T(8,128)(2,1)S(1)} collective-permute-done((bf16[272,768]{1,0:T(8,128)(2,1)S(1)}, bf16[272,768]{1,0:T(8,128)(2,1)S(1)}, u32[]{:S(2)}, u32[]{:S(2)}) %collective-permute-start.6) | collective-permute-done | bytes 417824 | tf_op jit(solution)/shard_map/ppermute | solution.py:43
  46.6 5.5 %all-to-all-start = ((bf16[8,384,384]{2,1,0:T(8,128)(2,1)}), bf16[8,384,384]{2,1,0:T(8,128)(2,1)S(1)}, u32[]{:S(2)}, u32[]{:S(2)}) async-start(bf16[8,384,384]{2,1,0:T(8,128)(2,1)} %bitcast.61), calls=%async_computation | async-start | bytes 4718592 | tf_op jit(solution)/shard_map/all_to_all | solution.py:574
  58.4 41.8 %collective-permute-done.8.refs_2_ = bf16[544,768]{1,0:T(8,128)(2,1)S(1)} collective-permute-done((bf16[544,768]{1,0:T(8,128)(2,1)S(1)}, bf16[544,768]{1,0:T(8,128)(2,1)S(1)}, u32[]{:S(2)}, u32[]{:S(2)}) %collective-permute-start.8) | collective-permute-done | bytes 835616 | tf_op jit(solution)/shard_map/ppermute | solution.py:555
  101.1 6.4 %all-to-all-start.1 = ((bf16[8,384,384]{2,1,0:T(8,128)(2,1)}), bf16[8,384,384]{2,1,0:T(8,128)(2,1)}, u32[]{:S(2)}, u32[]{:S(2)}) async-start(bf16[8,384,384]{2,1,0:T(8,128)(2,1)} %bitcast.64), calls=%async_computation.1 | async-start | bytes 4718592 | tf_op jit(solution)/shard_map/all_to_all | solution.py:574
  117.4 4.9 %collective-permute-done.12 = bf16[816,768]{1,0:T(8,128)(2,1)} collective-permute-done((bf16[816,768]{1,0:T(8,128)(2,1)}, bf16[816,768]{1,0:T(8,128)(2,1)}, u32[]{:S(2)}, u32[]{:S(2)}) %collective-permute-start.12) | collective-permute-done | bytes 1253408 | tf_op jit(solution)/shard_map/ppermute | solution.py:48
  126.5 8.3 %modulated_up.3 = (bf16[2,768,768]{2,1,0:T(8,128)(2,1)S(1)}, bf16[2,768,768]{2,1,0:T(8,128)(2,1)S(1)}, f32[768,384]{1,0:T(8,128)S(1)}, bf16[768,384]{1,0:T(8,128)(2,1)S(1)}) custom-call(s32[3]{0:T(128)S(1)} %add_bitcast_fusion.step_ref, s32[4]{0:T(128)S(1)} %pad_add_fusion.place_ref, f32[50,8,3072]{2,1,0:T(8,128)S(1)} %copy-done, ...), custom_call_target="tpu_custom_call" | custom-call | flops 1811939328 | bytes 9437184 | tf_op jit(solution)/shard_map/modulated_up/pallas_call | solution.py:210
  139.5 12.1 %modulated_up.2 = (bf16[2,1280,768]{2,1,0:T(8,128)(2,1)S(1)}, bf16[2,1280,768]{2,1,0:T(8,128)(2,1)S(1)}, f32[1280,384]{1,0:T(8,128)S(1)}, bf16[1280,384]{1,0:T(8,128)(2,1)S(1)}) custom-call(s32[5]{0:T(128)S(1)} %add_bitcast_fusion.1.step_ref, s32[4]{0:T(128)S(1)} %pad_add_fusion.place_ref, f32[50,8,3072]{2,1,0:T(8,128)S(1)} %bitcast.58, ...), custom_call_target="tpu_custom_call" | custom-call | flops 3019898880 | bytes 15728640 | tf_op jit(solution)/shard_map/modulated_up/pallas_call | solution.py:210
  245.5 5.9 %collective-permute-done.35 = bf16[256,768]{1,0:T(8,128)(2,1)S(1)} collective-permute-done((bf16[256,768]{1,0:T(8,128)(2,1)S(1)}, bf16[256,768]{1,0:T(8,128)(2,1)S(1)}, u32[]{:S(2)}, u32[]{:S(2)}) %collective-permute-start.35) | collective-permute-done | bytes 393248 | tf_op jit(solution)/shard_map/ppermute | solution.py:636
  255.2 5.5 %collective-permute-done.33 = bf16[256,768]{1,0:T(8,128)(2,1)S(1)} collective-permute-done((bf16[256,768]{1,0:T(8,128)(2,1)S(1)}, bf16[256,768]{1,0:T(8,128)(2,1)S(1)}, u32[]{:S(2)}, u32[]{:S(2)}) %collective-permute-start.33) | collective-permute-done | bytes 393248 | tf_op jit(solution)/shard_map/ppermute | solution.py:636
  266.7 8.3 %collective-permute-done.34.refs_2_ = bf16[256,768]{1,0:T(8,128)(2,1)S(1)} collective-permute-done((bf16[256,768]{1,0:T(8,128)(2,1)S(1)}, bf16[256,768]{1,0:T(8,128)(2,1)S(1)}, u32[]{:S(2)}, u32[]{:S(2)}) %collective-permute-start.34) | collective-permute-done | bytes 393248 | tf_op jit(solution)/shard_map/ppermute | solution.py:43
  278.5 4.6 %collective-permute-done.44.refs_9_ = bf16[256,768]{1,0:T(8,128)(2,1)S(1)} collective-permute-done((bf16[256,768]{1,0:T(8,128)(2,1)S(1)}, bf16[256,768]{1,0:T(8,128)(2,1)S(1)}, u32[]{:S(2)}, u32[]{:S(2)}) %collective-permute-start.44) | collective-permute-done | bytes 393248 | tf_op jit(solution)/shard_map/ppermute | solution.py:43
  283.1 4.3 %collective-permute-done.37.refs_4_ = bf16[256,768]{1,0:T(8,128)(2,1)} collective-permute-done((bf16[256,768]{1,0:T(8,128)(2,1)S(1)}, bf16[256,768]{1,0:T(8,128)(2,1)}, u32[]{:S(2)}, u32[]{:S(2)}) %collective-permute-start.37) | collective-permute-done | bytes 393248 | tf_op jit(solution)/shard_map/ppermute | solution.py:43
  295.0 8.1 %collective-permute-done.38.refs_2_ = bf16[256,768]{1,0:T(8,128)(2,1)} collective-permute-done((bf16[256,768]{1,0:T(8,128)(2,1)}, bf16[256,768]{1,0:T(8,128)(2,1)}, u32[]{:S(2)}, u32[]{:S(2)}) %collective-permute-start.38) | collective-permute-done | bytes 393248 | tf_op jit(solution)/shard_map/ppermute | solution.py:43
  308.5 8.2 %act_gradient.2.refs_2_ = bf16[1280,384]{1,0:T(8,128)(2,1)S(1)} custom-call(bf16[384,3072]{1,0:T(8,128)(2,1)S(1)} %placed.1.down_ref, f32[1280,384]{1,0:T(8,128)S(1)} %copy-done.9, bf16[2,1280,768]{2,1,0:T(8,128)(2,1)} %stacked_parts.2.own_ref.refs_0_, bf16[2,1280,768]{2,1,0:T(8,128)(2,1)} %collective-permute-done.45.other_ref.refs_0_), custom_call_target="tpu_custom_call" | custom-call | flops 3019898880 | bytes 7864320 | tf_op jit(solution)/shard_map/act_gradient/pallas_call | solution.py:243
  316.7 4.8 %weight_gradient.2 = (f32[4,384,384]{2,1,0:T(8,128)S(1)}, f32[4,384,384]{2,1,0:T(8,128)S(1)}) custom-call(s32[9]{0:T(128)S(1)} %concatenate.19.step_ref, bf16[2,1280,768]{2,1,0:T(8,128)(2,1)S(1)} %copy-done.39, bf16[2,1280,768]{2,1,0:T(8,128)(2,1)S(1)} %copy-done.41, bf16[1280,384]{1,0:T(8,128)(2,1)S(1)} %act_gradient.2.refs_2_), custom_call_target="tpu_custom_call" | custom-call | flops 3019898880 | bytes 7864320 | tf_op jit(solution)/shard_map/weight_gradient/pallas_call | solution.py:283
  323.0 5.4 %side_gradient.2.refs_4_ = bf16[8,192,384]{2,1,0:T(8,128)(2,1)S(1)} custom-call(s32[9]{0:T(128)S(1)} %concatenate.19.step_ref, bf16[2,1280,768]{2,1,0:T(8,128)(2,1)} %stacked_parts.2.own_ref.refs_0_, bf16[2,768,768]{2,1,0:T(8,128)(2,1)S(1)} %stacked_parts.3.refs_1_.own_ref, bf16[1280,384]{1,0:T(8,128)(2,1)S(1)} %slice.179.refs_2_, bf16[768,384]{1,0:T(8,128)(2,1)S(1)} %copy-done.2), custom_call_target="tpu_custom_call" | custom-call | flops 2415919104 | bytes 6291456 | tf_op jit(solution)/shard_map/side_gradient/pallas_call | solution.py:333
  336.5 6.5 %side_gradient.3 = bf16[8,192,384]{2,1,0:T(8,128)(2,1)} custom-call(s32[9]{0:T(128)S(1)} %concatenate.19.step_ref, bf16[2,1280,768]{2,1,0:T(8,128)(2,1)} %collective-permute-done.45.other_ref.refs_0_, bf16[2,768,768]{2,1,0:T(8,128)(2,1)S(1)} %collective-permute-done.50.other_ref.refs_1_, bf16[1280,384]{1,0:T(8,128)(2,1)S(1)} %slice.179.refs_2_, ...), custom_call_target="tpu_custom_call" | custom-call | flops 2415919104 | bytes 6291456 | tf_op jit(solution)/shard_map/side_gradient/pallas_call | solution.py:333
  343.0 4.5 %all-to-all-start.3 = ((bf16[8,192,384]{2,1,0:T(8,128)(2,1)}), bf16[8,192,384]{2,1,0:T(8,128)(2,1)S(1)}, u32[]{:S(2)}, u32[]{:S(2)}) async-start(bf16[8,192,384]{2,1,0:T(8,128)(2,1)} %side_gradient.3), calls=%async_computation.3 | async-start | bytes 2359296 | tf_op jit(solution)/shard_map/all_to_all | solution.py:574
  351.5 25.5 %collective-permute-done.51 = bf16[8,192,384]{2,1,0:T(8,128)(2,1)S(1)} collective-permute-done((bf16[8,192,384]{2,1,0:T(8,128)(2,1)}, bf16[8,192,384]{2,1,0:T(8,128)(2,1)S(1)}, u32[]{:S(2)}, u32[]{:S(2)}) %collective-permute-start.51) | collective-permute-done | bytes 1179680 | tf_op jit(solution)/shard_map/ppermute | solution.py:671
  378.2 6.0 %all-to-all-start.2 = ((bf16[8,192,384]{2,1,0:T(8,128)(2,1)}), bf16[8,192,384]{2,1,0:T(8,128)(2,1)S(1)}, u32[]{:S(2)}, u32[]{:S(2)}) async-start(bf16[8,192,384]{2,1,0:T(8,128)(2,1)} %broadcast_select_fusion.1), calls=%async_computation.2 | async-start | bytes 2359296 | tf_op jit(solution)/shard_map/all_to_all | solution.py:574
  386.7 22.5 %all-to-all-done.2.refs_0_ = bf16[8,192,384]{2,1,0:T(8,128)(2,1)S(1)} async-done(((bf16[8,192,384]{2,1,0:T(8,128)(2,1)}), bf16[8,192,384]{2,1,0:T(8,128)(2,1)S(1)}, u32[]{:S(2)}, u32[]{:S(2)}) %all-to-all-start.2) | async-done | bytes 1179680 | tf_op jit(solution)/shard_map/all_to_all | solution.py:574
  (275 shorter events, 182.5 us)
Async XLA Ops:
  16.4 19.2 %collective-permute-start.5 = (bf16[544,768]{1,0:T(8,128)(2,1)S(1)}, bf16[544,768]{1,0:T(8,128)(2,1)S(1)}, u32[]{:S(2)}, u32[]{:S(2)}) collective-permute-start(bf16[544,768]{1,0:T(8,128)(2,1)S(1)} %stacked.6), channel_id=1, source_target_pairs={{0,1},{1,0},{2,3},{3,2},{4,5},{5,4},{6,7},{7,6},{8,9},{9,8},{10,11... | collective-permute-start | bytes 2506760 | tf_op jit(solution)/shard_map/ppermute | solution.py:555
  46.6 54.5 %all-to-all-start = ((bf16[8,384,384]{2,1,0:T(8,128)(2,1)}), bf16[8,384,384]{2,1,0:T(8,128)(2,1)S(1)}, u32[]{:S(2)}, u32[]{:S(2)}) async-start(bf16[8,384,384]{2,1,0:T(8,128)(2,1)} %bitcast.61), calls=%async_computation | async-start | bytes 4718592 | tf_op jit(solution)/shard_map/all_to_all | solution.py:574
  56.2 44.9 %collective-permute-start.11 = (bf16[816,768]{1,0:T(8,128)(2,1)}, bf16[816,768]{1,0:T(8,128)(2,1)}, u32[]{:S(2)}, u32[]{:S(2)}) collective-permute-start(bf16[816,768]{1,0:T(8,128)(2,1)} %stacked.9), channel_id=1, source_target_pairs={{0,1},{1,0},{2,3},{3,2},{4,5},{5,4},{6,7},{7,6},{8,9},{9,8},{10,11... | collective-permute-start | bytes 3760136 | tf_op jit(solution)/shard_map/ppermute | solution.py:555
  56.8 43.4 %collective-permute-start.8 = (bf16[544,768]{1,0:T(8,128)(2,1)S(1)}, bf16[544,768]{1,0:T(8,128)(2,1)S(1)}, u32[]{:S(2)}, u32[]{:S(2)}) collective-permute-start(bf16[544,768]{1,0:T(8,128)(2,1)S(1)} %stacked.7), channel_id=1, source_target_pairs={{0,1},{1,0},{2,3},{3,2},{4,5},{5,4},{6,7},{7,6},{8,9},{9,8},{10,11... | collective-permute-start | bytes 2506760 | tf_op jit(solution)/shard_map/ppermute | solution.py:555
  101.1 56.9 %all-to-all-start.1 = ((bf16[8,384,384]{2,1,0:T(8,128)(2,1)}), bf16[8,384,384]{2,1,0:T(8,128)(2,1)}, u32[]{:S(2)}, u32[]{:S(2)}) async-start(bf16[8,384,384]{2,1,0:T(8,128)(2,1)} %bitcast.64), calls=%async_computation.1 | async-start | bytes 4718592 | tf_op jit(solution)/shard_map/all_to_all | solution.py:574
  113.1 26.4 %collective-permute-start.9 = (bf16[1360,768]{1,0:T(8,128)(2,1)}, bf16[1360,768]{1,0:T(8,128)(2,1)}, u32[]{:S(2)}, u32[]{:S(2)}) collective-permute-start(bf16[1360,768]{1,0:T(8,128)(2,1)} %stacked.5), channel_id=1, source_target_pairs={{2,0},{0,2},{3,1},{1,3},{6,4},{4,6},{7,5},{5,7},{10,8},{8,10},{11,... | collective-permute-start | bytes 6266888 | tf_op jit(solution)/shard_map/ppermute | solution.py:48
  115.2 24.4 %collective-permute-start.10 = (bf16[1360,768]{1,0:T(8,128)(2,1)}, bf16[1360,768]{1,0:T(8,128)(2,1)}, u32[]{:S(2)}, u32[]{:S(2)}) collective-permute-start(bf16[1360,768]{1,0:T(8,128)(2,1)} %stacked.8), channel_id=1, source_target_pairs={{2,0},{0,2},{3,1},{1,3},{6,4},{4,6},{7,5},{5,7},{10,8},{8,10},{11,... | collective-permute-start | bytes 6266888 | tf_op jit(solution)/shard_map/ppermute | solution.py:48
  165.4 33.2 %collective-permute-start.15 = (bf16[1280,1536]{1,0:T(8,128)(2,1)S(1)}, bf16[1280,1536]{1,0:T(8,128)(2,1)S(1)}, u32[]{:S(2)}, u32[]{:S(2)}) collective-permute-start(bf16[1280,1536]{1,0:T(8,128)(2,1)S(1)} %convolution_convert_fusion), channel_id=1, source_target_pairs={{2,0},{0,2},{3,1},{1,3},{6,4},{4,6},{7,5},{5,7},{10,8},{8,10},{11,... | collective-permute-start | bytes 11796488 | tf_op jit(solution)/shard_map/ppermute | solution.py:48
  174.9 16.3 %collective-permute-start.22 = (bf16[256,768]{1,0:T(8,128)(2,1)S(1)}, bf16[256,768]{1,0:T(8,128)(2,1)S(1)}, u32[]{:S(2)}, u32[]{:S(2)}) collective-permute-start(bf16[256,768]{1,0:T(8,128)(2,1)S(1)} %fusion.27), channel_id=1, source_target_pairs={{0,8},{8,16},{16,24},{24,28},{28,20},{20,12},{12,4},{4,0},{1,9},{9... | collective-permute-start | bytes 1179656 | tf_op jit(solution)/shard_map/ppermute | solution.py:43
  179.4 15.0 %collective-permute-start.20 = (bf16[256,768]{1,0:T(8,128)(2,1)S(1)}, bf16[256,768]{1,0:T(8,128)(2,1)S(1)}, u32[]{:S(2)}, u32[]{:S(2)}) collective-permute-start(bf16[256,768]{1,0:T(8,128)(2,1)S(1)} %fusion.20), channel_id=1, source_target_pairs={{0,4},{8,0},{16,8},{24,16},{28,24},{20,28},{12,20},{4,12},{1,5},{9... | collective-permute-start | bytes 1179656 | tf_op jit(solution)/shard_map/ppermute | solution.py:43
  183.2 15.4 %collective-permute-start.18 = (bf16[256,768]{1,0:T(8,128)(2,1)S(1)}, bf16[256,768]{1,0:T(8,128)(2,1)S(1)}, u32[]{:S(2)}, u32[]{:S(2)}) collective-permute-start(bf16[256,768]{1,0:T(8,128)(2,1)S(1)} %fusion.21), channel_id=1, source_target_pairs={{0,8},{8,16},{16,24},{24,28},{28,20},{20,12},{12,4},{4,0},{1,9},{9... | collective-permute-start | bytes 1179656 | tf_op jit(solution)/shard_map/ppermute | solution.py:43
  183.6 15.0 %collective-permute-start.21 = (bf16[256,768]{1,0:T(8,128)(2,1)S(1)}, bf16[256,768]{1,0:T(8,128)(2,1)S(1)}, u32[]{:S(2)}, u32[]{:S(2)}) collective-permute-start(bf16[256,768]{1,0:T(8,128)(2,1)S(1)} %fusion.26), channel_id=1, source_target_pairs={{0,4},{8,0},{16,8},{24,16},{28,24},{20,28},{12,20},{4,12},{1,5},{9... | collective-permute-start | bytes 1179656 | tf_op jit(solution)/shard_map/ppermute | solution.py:43
  191.2 39.2 %collective-permute-start.31 = (bf16[2048,384]{1,0:T(8,128)(2,1)}, bf16[2048,384]{1,0:T(8,128)(2,1)}, u32[]{:S(2)}, u32[]{:S(2)}) collective-permute-start(bf16[2048,384]{1,0:T(8,128)(2,1)} %constant_dynamic-update-slice_fusion), channel_id=1, source_target_pairs={{1,0},{3,2},{5,4},{7,6},{9,8},{11,10},{13,12},{15,14},{17,16},{19,... | collective-permute-start | bytes 4718600 | tf_op jit(solution)/shard_map/ppermute | solution.py:531
  204.5 14.3 %collective-permute-start.23 = (bf16[256,768]{1,0:T(8,128)(2,1)}, bf16[256,768]{1,0:T(8,128)(2,1)}, u32[]{:S(2)}, u32[]{:S(2)}) collective-permute-start(bf16[256,768]{1,0:T(8,128)(2,1)} %fusion.22), channel_id=1, source_target_pairs={{0,8},{8,16},{16,24},{24,28},{28,20},{20,12},{12,4},{4,0},{1,9},{9... | collective-permute-start | bytes 1179656 | tf_op jit(solution)/shard_map/ppermute | solution.py:43
  212.5 32.8 %collective-permute-start.32 = (f32[1536]{0:T(1024)S(1)}, f32[1536]{0:T(1024)S(1)}, u32[]{:S(2)}, u32[]{:S(2)}) collective-permute-start(f32[1536]{0:T(1024)S(1)} %dynamic-slice_reduce_fusion), channel_id=1, source_target_pairs={{1,0},{3,2},{5,4},{7,6},{9,8},{11,10},{13,12},{15,14},{17,16},{19,... | collective-permute-start | bytes 18440 | tf_op jit(solution)/shard_map/ppermute | solution.py:531
  262.6 14.5 %collective-permute-start.41 = (bf16[256,768]{1,0:T(8,128)(2,1)S(1)}, bf16[256,768]{1,0:T(8,128)(2,1)S(1)}, u32[]{:S(2)}, u32[]{:S(2)}) collective-permute-start(bf16[256,768]{1,0:T(8,128)(2,1)S(1)} %fusion.38.refs_0_), channel_id=1, source_target_pairs={{0,4},{8,0},{16,8},{24,16},{28,24},{20,28},{12,20},{4,12},{1,5},{9... | collective-permute-start | bytes 1179656 | tf_op jit(solution)/shard_map/ppermute | solution.py:43
  266.6 16.5 %collective-permute-start.44 = (bf16[256,768]{1,0:T(8,128)(2,1)S(1)}, bf16[256,768]{1,0:T(8,128)(2,1)S(1)}, u32[]{:S(2)}, u32[]{:S(2)}) collective-permute-start(bf16[256,768]{1,0:T(8,128)(2,1)S(1)} %collective-permute-done.43.refs_7_), channel_id=1, source_target_pairs={{0,8},{8,16},{16,24},{24,28},{28,20},{20,12},{12,4},{4,0},{1,9},{9... | collective-permute-start | bytes 1179656 | tf_op jit(solution)/shard_map/ppermute | solution.py:43
  293.0 28.5 %collective-permute-start.49 = (bf16[256,768]{1,0:T(8,128)(2,1)}, bf16[256,768]{1,0:T(8,128)(2,1)S(1)}, u32[]{:S(2)}, u32[]{:S(2)}) collective-permute-start(bf16[256,768]{1,0:T(8,128)(2,1)} %copy-done.36), channel_id=1, source_target_pairs={{0,8},{8,16},{16,24},{24,28},{28,20},{20,12},{12,4},{4,0},{1,9},{9... | collective-permute-start | bytes 1179656 | tf_op jit(solution)/shard_map/ppermute | solution.py:43
  294.7 26.8 %collective-permute-start.47 = (bf16[256,768]{1,0:T(8,128)(2,1)}, bf16[256,768]{1,0:T(8,128)(2,1)S(1)}, u32[]{:S(2)}, u32[]{:S(2)}) collective-permute-start(bf16[256,768]{1,0:T(8,128)(2,1)} %copy-done.37), channel_id=1, source_target_pairs={{0,4},{8,0},{16,8},{24,16},{28,24},{20,28},{12,20},{4,12},{1,5},{9... | collective-permute-start | bytes 1179656 | tf_op jit(solution)/shard_map/ppermute | solution.py:43
  304.9 16.7 %collective-permute-start.46 = (bf16[256,768]{1,0:T(8,128)(2,1)}, bf16[256,768]{1,0:T(8,128)(2,1)S(1)}, u32[]{:S(2)}, u32[]{:S(2)}) collective-permute-start(bf16[256,768]{1,0:T(8,128)(2,1)} %collective-permute-done.38.refs_2_), channel_id=1, source_target_pairs={{0,8},{8,16},{16,24},{24,28},{28,20},{20,12},{12,4},{4,0},{1,9},{9... | collective-permute-start | bytes 1179656 | tf_op jit(solution)/shard_map/ppermute | solution.py:43
  305.9 15.7 %collective-permute-start.48 = (bf16[256,768]{1,0:T(8,128)(2,1)}, bf16[256,768]{1,0:T(8,128)(2,1)S(1)}, u32[]{:S(2)}, u32[]{:S(2)}) collective-permute-start(bf16[256,768]{1,0:T(8,128)(2,1)} %collective-permute-done.40.refs_4_), channel_id=1, source_target_pairs={{0,4},{8,0},{16,8},{24,16},{28,24},{20,28},{12,20},{4,12},{1,5},{9... | collective-permute-start | bytes 1179656 | tf_op jit(solution)/shard_map/ppermute | solution.py:43
  343.0 35.1 %all-to-all-start.3 = ((bf16[8,192,384]{2,1,0:T(8,128)(2,1)}), bf16[8,192,384]{2,1,0:T(8,128)(2,1)S(1)}, u32[]{:S(2)}, u32[]{:S(2)}) async-start(bf16[8,192,384]{2,1,0:T(8,128)(2,1)} %side_gradient.3), calls=%async_computation.3 | async-start | bytes 2359296 | tf_op jit(solution)/shard_map/all_to_all | solution.py:574
  347.5 29.5 %collective-permute-start.51 = (bf16[8,192,384]{2,1,0:T(8,128)(2,1)}, bf16[8,192,384]{2,1,0:T(8,128)(2,1)S(1)}, u32[]{:S(2)}, u32[]{:S(2)}) collective-permute-start(bf16[8,192,384]{2,1,0:T(8,128)(2,1)} %copy-done.42), channel_id=1, source_target_pairs={{1,0},{3,2},{5,4},{7,6},{9,8},{11,10},{13,12},{15,14},{17,16},{19,... | collective-permute-start | bytes 3538952 | tf_op jit(solution)/shard_map/ppermute | solution.py:671
  378.2 31.1 %all-to-all-start.2 = ((bf16[8,192,384]{2,1,0:T(8,128)(2,1)}), bf16[8,192,384]{2,1,0:T(8,128)(2,1)S(1)}, u32[]{:S(2)}, u32[]{:S(2)}) async-start(bf16[8,192,384]{2,1,0:T(8,128)(2,1)} %broadcast_select_fusion.1), calls=%async_computation.2 | async-start | bytes 2359296 | tf_op jit(solution)/shard_map/all_to_all | solution.py:574
  (88 other events, 716.4 us)
